TPU v7x, 256 devices: a whole 4x4x8 slice. The times are simulated.
256 devices in a mesh: ctx: 32 (over z, y), head: 4 (over x), side: 2 (over core).
Axes of the slice: x: 4, y: 4, z: 8, core: 2. Of those that a mesh axis runs over, the one named last changes fastest.
Arguments:
- x_in: bfloat16 [2, 16384, 8192], P('side', 'ctx', 'head'), may hold values from -6 to 6
- bc_in: bfloat16 [2, 16384, 2, 1024], P('side', 'ctx', None, 'head'), may hold values from -6 to 6
- z_in: bfloat16 [2, 16384, 8192], P('side', 'ctx', 'head'), may hold values from -6 to 6
- dt_in: float32 [2, 16384, 128], P('side', 'ctx', 'head'), may hold values from -4 to 11
- conv_x_w: float32 [4, 8192], P(None, 'head'), may hold values from -3 to 3
- conv_x_b: float32 [8192], P('head'), may hold values from -1 to 0
- conv_bc_w: float32 [4, 2, 1024], P(None, None, 'head'), may hold values from -3 to 3
- conv_bc_b: float32 [2, 1024], P(None, 'head'), may hold values from -1 to 0
- a_log: float32 [128], P('head'), may hold values from -5 to 2.7
- dt_bias: float32 [128], P('head'), may hold values from -7 to -2
- skip_d: float32 [128], P('head'), may hold values from 0.5 to 1.5
- norm_gain: float32 [8192], P('head'), may hold values from 0.5 to 1.5
- lengths: int32 [2, 32], P('side'), may hold values from 1 to 1024, as said below
- owner_slot: int32 [2, 32], P('side'), may hold values from 0 to 31, each once within a row
Outputs:
- mixed: bfloat16 [2, 16384, 8192], P('side', 'ctx', 'head')
- handed_state: float32 [2, 32, 128, 64, 128], P('side', 'ctx', 'head')
- handed_tail_x: bfloat16 [2, 32, 3, 8192], P('side', 'ctx', None, 'head')
- handed_tail_bc: bfloat16 [2, 32, 3, 2, 1024], P('side', 'ctx', None, None, 'head')
Inputs may be any that keep to these rules, and one draw needn't show every extreme that they name: In each section the lengths add up to 16384. No block of 512 tokens that starts at a multiple of 512 holds the last token of more than 2 requests, and in each section some such block holds exactly 2. In each section some request holds exactly 1024 tokens.
All inputs are finite; a program needn't handle non-finite values.
Results may differ from a plain program's by a relative error of at most 0.0059.
Values may be sent and summed in bfloat16 or wider, within the bound.
No kernel may reach another device: no remote copies, remote signals or barrier semaphores. Data moves between devices by JAX's collectives and lax.ppermute only.
A program may use at most 128 MiB of HBM per device.

v0:
```python
import jax
import jax.numpy as jnp
from jax import lax
from jax.sharding import PartitionSpec as P

HEAD_DIM = 64
STATE = 128
STRETCH = 128
ENDS = 2


EPS = 1e-05


def from_behind(block, axis, distance):
    devices = range(lax.axis_size(axis))
    route = [(i - distance, i) for i in devices if i - distance in devices]
    return lax.ppermute(block, axis, route)


def entering_2(x, axis, combine, identity):
    count, here = (lax.axis_size(axis), lax.axis_index(axis))
    everything = jax.tree.map(lambda part: lax.all_gather(part, axis), x)
    start = jax.tree.map(
        lambda part, zero: jnp.broadcast_to(jnp.asarray(zero, part.dtype), part.shape), x, identity
    )

    def step(k, before):
        reached = k < here
        new = combine(before, jax.tree.map(lambda part: part[k], everything))
        return jax.tree.map(lambda a, b: jnp.where(reached, a, b), new, before)

    return lax.fori_loop(0, count, step, start)


def partner(x, axis, bit):
    return lax.ppermute(x, axis, [(i, i ^ 1 << bit) for i in range(lax.axis_size(axis))])


def conv_silu(extended, kernel, offset_bias, position, first_token):
    tap_count = kernel.shape[0]
    row_count = position.shape[0]
    summed = jnp.zeros((row_count, extended.shape[1]), jnp.float32) + offset_bias[None, :]
    for tap_index in range(tap_count):
        source = position - (tap_count - 1) + tap_index
        inside = (source >= first_token)[:, None]
        summed = summed + kernel[tap_index][None, :] * jnp.where(
            inside, extended[tap_index : tap_index + row_count].astype(jnp.float32), 0.0
        )
    return jax.nn.silu(summed).astype(jnp.bfloat16)


def carry_combine(earlier, latter):
    return (earlier[0] * latter[0], latter[0][:, None, None] * earlier[1] + latter[1])


def on_device(
    x_in,
    bc_in,
    z_in,
    dt_in,
    conv_x_w,
    conv_x_b,
    conv_bc_w,
    conv_bc_b,
    a_log,
    dt_bias,
    skip_d,
    norm_gain,
    lengths,
    owner_slot,
):
    ctx_count = lax.axis_size("ctx")
    shard_index = lax.axis_index("ctx")
    x_rows = x_in[0]
    tok_count, inner_width = x_rows.shape
    group_width = bc_in.shape[3]
    group_count = group_width // STATE
    head_count = dt_in.shape[2]
    per_group = head_count // group_count
    tap_count = conv_x_w.shape[0]
    stretch_count = tok_count // STRETCH
    bc_rows = bc_in[0].reshape(tok_count, 2 * group_width)
    req_lengths = lengths[0]
    req_count = req_lengths.shape[0]
    req_index = jnp.arange(req_count, dtype=jnp.int32)
    last_token = jnp.cumsum(req_lengths) - 1
    first_of_req = last_token - req_lengths + 1
    offset = shard_index * tok_count
    position = offset + jnp.arange(tok_count, dtype=jnp.int32)
    request_of = jnp.sum((last_token[None, :] < position[:, None]).astype(jnp.int32), axis=1)
    member = request_of[:, None] == req_index[None, :]
    first_token = jnp.sum(jnp.where(member, first_of_req[None, :], 0), axis=1)
    rim_rows = from_behind(
        jnp.concatenate(
            [x_rows[tok_count - tap_count + 1 :], bc_rows[tok_count - tap_count + 1 :]], axis=1
        ),
        "ctx",
        1,
    )
    ext_x = jnp.concatenate([rim_rows[:, :inner_width], x_rows], axis=0)
    ext_bc = jnp.concatenate([rim_rows[:, inner_width:], bc_rows], axis=0)
    x_conv = conv_silu(ext_x, conv_x_w, conv_x_b, position, first_token)
    bc_conv = conv_silu(
        ext_bc,
        conv_bc_w.reshape(tap_count, 2 * group_width),
        conv_bc_b.reshape(2 * group_width),
        position,
        first_token,
    )
    step_size = jax.nn.softplus(dt_in[0] + dt_bias[None, :])
    log_decay = -jnp.exp(a_log)[None, :] * step_size
    x_stretches = x_conv.reshape(stretch_count, STRETCH, group_count, per_group, HEAD_DIM)
    b_stretches = bc_conv[:, :group_width].reshape(stretch_count, STRETCH, group_count, STATE)
    c_stretches = bc_conv[:, group_width:].reshape(stretch_count, STRETCH, group_count, STATE)
    step_stretches = step_size.reshape(stretch_count, STRETCH, head_count)
    cum_decay = jnp.cumsum(log_decay.reshape(stretch_count, STRETCH, head_count), axis=1)
    req_stretches = request_of.reshape(stretch_count, STRETCH)
    first_stretches = first_token.reshape(stretch_count, STRETCH)
    stretch_starts = offset + STRETCH * jnp.arange(stretch_count, dtype=jnp.int32)
    inflow = jnp.where(
        (first_stretches < stretch_starts[:, None])[:, :, None], jnp.exp(cum_decay), 0.0
    )
    within = jnp.arange(STRETCH)
    causal = (req_stretches[:, :, None] == req_stretches[:, None, :]) & (
        within[None, None, :] <= within[None, :, None]
    )
    cum_heads = jnp.swapaxes(cum_decay, 1, 2)
    decay = (
        jnp.exp(
            jnp.where(
                causal[:, None], cum_heads[:, :, :, None] - cum_heads[:, :, None, :], -jnp.inf
            )
        )
        * jnp.swapaxes(step_stretches, 1, 2)[:, :, None, :]
    )
    scores = jnp.einsum(
        "ctgn,csgn->cgts", c_stretches, b_stretches, preferred_element_type=jnp.float32
    )
    weights = (
        scores[:, :, None] * decay.reshape(stretch_count, group_count, per_group, STRETCH, STRETCH)
    ).astype(jnp.bfloat16)
    inner = jnp.einsum(
        "cghts,csghp->ctghp", weights, x_stretches, preferred_element_type=jnp.float32
    )
    last_req = req_stretches[:, STRETCH - 1]
    tail_keep = req_stretches == last_req[:, None]
    end_weights = (
        jnp.exp(
            jnp.where(
                tail_keep[:, :, None], cum_decay[:, STRETCH - 1][:, None, :] - cum_decay, -jnp.inf
            )
        )
        * step_stretches
    )
    scaled = (
        x_stretches * end_weights.reshape(stretch_count, STRETCH, group_count, per_group)[..., None]
    ).astype(jnp.bfloat16)
    local = jnp.einsum(
        "csghp,csgn->cghpn", scaled, b_stretches, preferred_element_type=jnp.float32
    ).reshape(stretch_count, head_count, HEAD_DIM, STATE)
    through = inflow[:, STRETCH - 1]

    def advance(carried, pieces):
        state_now, gain_now = carried
        passing, added = pieces
        return (
            (passing[:, None, None] * state_now + added, gain_now * passing),
            (state_now, gain_now),
        )

    start_carry = (
        jnp.zeros((head_count, HEAD_DIM, STATE), jnp.float32),
        jnp.ones((head_count,), jnp.float32),
    )
    (dev_state, dev_gain), (entered, entered_gain) = lax.scan(
        advance, start_carry, (through, local)
    )
    incoming = entering_2(
        (dev_gain, dev_state),
        "ctx",
        carry_combine,
        (jnp.ones_like(dev_gain), jnp.zeros_like(dev_state)),
    )[1]
    entering = entered + entered_gain[:, :, None, None] * incoming[None]
    carried_in = jnp.einsum(
        "ctgn,cghpn->ctghp",
        c_stretches.astype(jnp.float32),
        entering.reshape(stretch_count, group_count, per_group, HEAD_DIM, STATE),
        precision=lax.Precision.HIGHEST,
    )
    inter = inflow.reshape(stretch_count, STRETCH, group_count, per_group)[..., None] * carried_in
    skip_wide = jnp.repeat(skip_d, HEAD_DIM)
    mixed_f = (inner + inter).reshape(tok_count, inner_width) + skip_wide[None, :] * x_conv.astype(
        jnp.float32
    )
    gated = mixed_f * jax.nn.silu(z_in[0].astype(jnp.float32))
    grouped = gated.reshape(tok_count, group_count, inner_width // group_count)
    norm_scale = lax.rsqrt(jnp.mean(grouped * grouped, axis=2, keepdims=True) + EPS)
    mixed = ((grouped * norm_scale).reshape(tok_count, inner_width) * norm_gain[None, :]).astype(
        jnp.bfloat16
    )
    slot_index = jnp.arange(ENDS, dtype=jnp.int32)
    lower_count = jnp.sum((last_token < offset).astype(jnp.int32))
    upper_count = jnp.sum((last_token < offset + tok_count).astype(jnp.int32))
    slot_req = lower_count + slot_index
    valid = slot_req < upper_count
    member_end = jnp.minimum(slot_req, req_count - 1)[:, None] == req_index[None, :]
    end_local = jnp.where(
        valid, jnp.sum(jnp.where(member_end, last_token[None, :], 0), axis=1) - offset, 0
    )
    end_first = jnp.sum(jnp.where(member_end, first_of_req[None, :], 0), axis=1)

    def one_end(point):
        stretch_index = point // STRETCH
        inside_point = point - stretch_index * STRETCH
        cum_here = cum_decay[stretch_index]
        req_here = req_stretches[stretch_index]
        chosen = (req_here == req_here[inside_point]) & (within <= inside_point)
        point_weights = (
            jnp.exp(
                jnp.where(chosen[:, None], cum_here[inside_point][None, :] - cum_here, -jnp.inf)
            )
            * step_stretches[stretch_index]
        )
        scaled_here = (
            x_stretches[stretch_index]
            * point_weights.reshape(STRETCH, group_count, per_group)[..., None]
        ).astype(jnp.bfloat16)
        summed = jnp.einsum(
            "sghp,sgn->ghpn",
            scaled_here,
            b_stretches[stretch_index],
            preferred_element_type=jnp.float32,
        )
        return inflow[stretch_index, inside_point][:, None, None] * entering[
            stretch_index
        ] + summed.reshape(head_count, HEAD_DIM, STATE)

    finals = jax.vmap(one_end)(end_local)
    finals = jnp.where(valid[:, None, None, None], finals, 0.0)
    tail_steps = jnp.arange(tap_count - 1, dtype=jnp.int32)
    tail_rows = end_local[:, None] + tail_steps[None, :] + 1
    tail_source = offset + end_local[:, None] - (tap_count - 2) + tail_steps[None, :]
    tail_inside = ((tail_source >= end_first[:, None]) & valid[:, None])[..., None]
    zero_value = jnp.zeros((), jnp.bfloat16)
    tail_x = jnp.where(tail_inside, ext_x[tail_rows], zero_value)
    tail_bc = jnp.where(tail_inside, ext_bc[tail_rows], zero_value)
    tail_flat = jnp.concatenate(
        [tail_x.reshape(ENDS, -1), tail_bc.reshape(ENDS, -1)], axis=1
    ).astype(jnp.float32)
    send_tail = tail_flat.reshape(ENDS, ctx_count, -1)
    got_state, got_tail = (
        lax.all_to_all(finals, "ctx", split_axis=1, concat_axis=0, tiled=True),
        lax.all_to_all(send_tail, "ctx", split_axis=1, concat_axis=0, tiled=True),
    )
    owner_of = owner_slot[0]
    home_shard = last_token // tok_count
    before_home = jnp.sum(
        (last_token[None, :] < (home_shard * tok_count)[:, None]).astype(jnp.int32), axis=1
    )
    source_row = home_shard * ENDS + req_index - before_home
    by_slot = owner_of[None, :] == req_index[:, None]
    take_row = jnp.sum(jnp.where(by_slot, source_row[None, :], 0), axis=1)
    per_owner = req_count // ctx_count
    held_state = got_state[take_row].reshape(ctx_count, per_owner, 1, -1, STATE)
    held_tail = got_tail[take_row].reshape(ctx_count, per_owner, 1, -1)
    own_state, own_tail = (
        lax.all_to_all(held_state, "ctx", split_axis=0, concat_axis=2, tiled=True),
        lax.all_to_all(held_tail, "ctx", split_axis=0, concat_axis=2, tiled=True),
    )
    swapped_state, swapped_tail = partner((own_state, own_tail), "side", 0)
    tail_rows_all = swapped_tail.reshape(per_owner, -1)
    split_point = (tap_count - 1) * inner_width
    handed_tail_x = (
        tail_rows_all[:, :split_point]
        .reshape(1, per_owner, tap_count - 1, inner_width)
        .astype(jnp.bfloat16)
    )
    handed_tail_bc = (
        tail_rows_all[:, split_point:]
        .reshape(1, per_owner, tap_count - 1, 2, group_width)
        .astype(jnp.bfloat16)
    )
    return (mixed[None], swapped_state, handed_tail_x, handed_tail_bc)


def solution(mesh):
    placed = (
        P("side", "ctx", "head"),
        P("side", "ctx", None, "head"),
        P("side", "ctx", "head"),
        P("side", "ctx", "head"),
        P(None, "head"),
        P("head"),
        P(None, None, "head"),
        P(None, "head"),
        P("head"),
        P("head"),
        P("head"),
        P("head"),
        P("side", None),
        P("side", None),
    )
    return jax.shard_map(
        on_device,
        mesh=mesh,
        in_specs=placed,
        out_specs=(
            P("side", "ctx", "head"),
            P("side", "ctx", "head", None, None),
            P("side", "ctx", None, "head"),
            P("side", "ctx", None, None, "head"),
        ),
        check_vma=False,
    )
```

profile of v0, /device:TPU:1, one launch (start us, length us, event | category | flops | bytes accessed | tf_op | source)
XLA Modules:
  0.0 500.7 jit_solution(1864702419001816718)
XLA Ops:
  8.7 4.0 collective-permute-start
  14.4 1.5 broadcast_multiply_fusion
  25.1 2.0 copy.214
  28.2 9.1 %multiply_convert_fusion.4 = bf16[512,2048]{1,0:T(8,128)(2,1)S(1)} fusion(bf16[512,2048]{1,0:T(8,128)(2,1)} %bitcast.152, bf16[3,2048]{1,0:T(4,128)(2,1)S(1)} %slice.160, f32[2048]{0:T(1024)S(1)} %bitcast.176, f32[2048]{0:T(1024)S(1)} %bitcast.177, f32[2048]{0:T(1024)S(1)} %bitcast.175, f32[2048]{0:T(1024)S(1)} %bitcast.174, f32[2048]{0:T(1024)S(1)} %copy-done.15, ...), kind=kLoop, calls=%fused_computation.45 | loop fusion | flops 31457280 | bytes 4249600 | tf_op jit(solution)/shard_map/convert_element_type | solution.py:50
  37.4 2.5 copy.174
  39.9 4.0 reshape.638
  44.7 3.1 multiply_convert_fusion.5
  48.6 1.7 reshape.640
  50.4 2.7 multiply_convert_fusion.3
  53.1 2.7 fusion.20
  55.7 15.2 %while.31 = (s32[]{:T(128)}, f32[32,64,128]{2,1,0:T(8,128)S(1)}, f32[32]{0:T(128)S(1)}, f32[4,32,64,128]{3,2,1,0:T(8,128)}, f32[4,32]{1,0:T(4,128)}, /*index=5*/...) while((s32[]{:T(128)}, f32[32,64,128]{2,1,0:T(8,128)S(1)}, ...), condition=%wide.region_5.6_spmd.clone, body=%wide.region_4.5_spmd.clone.sunk | while | flops 1048643 | bytes 5244533 | solution.py:176
  74.5 1.7 or_bitcast_fusion.1
  78.1 1.5 gather_fusion.12
  83.0 1.9 add_add_fusion
  87.0 2.2 gather_fusion
  96.2 3.5 copy.191
  100.4 3.3 gather_fusion.2
  103.7 1.5 gather_fusion.6
  105.3 3.5 pad_maximum_fusion
  108.8 3.3 gather_fusion.8
  114.9 2.0 pad_maximum_fusion.1
  116.9 2.4 gather_fusion.9
  122.8 1.5 reshape.651
  125.7 11.0 %all-to-all-start.2 = ((bf16[2,32,240]{2,0,1:T(2,128)(2,1)}), bf16[2,32,240]{2,0,1:T(2,128)(2,1)}, u32[]{:S(2)}, u32[]{:S(2)}) async-start(bf16[2,32,240]{2,0,1:T(2,128)(2,1)} %copy.200), calls=%async_computation.2 | async-start | bytes 65536 | tf_op jit(solution)/shard_map/all_to_all | solution.py:255
  136.6 3.0 fusion.24
  139.8 61.7 %all-reduce.4 = f32[1024]{0:T(1024)S(1)} all-reduce(f32[1024]{0:T(1024)S(1)} %dynamic-update-slice), channel_id=2, replica_groups=mesh['ctx'=32,'head'=4,'side'=2] {'ctx'}, use_global_device_ids=true, to_apply=%add.4 | all-reduce | flops 1024 | bytes 8192
  203.8 4.8 all-to-all-start.3
  208.6 101.4 %all-gather.4.cloned.1.call-done = f32[1024,64,128]{2,1,0:T(8,128)} async-done(((f32[32,64,128]{2,1,0:T(8,128)}), f32[1024,64,128]{2,1,0:T(8,128)}) %all-gather.4.cloned.1.call-update) | async-done | bytes 33554448 | tf_op jit(solution)/shard_map/all_gather | solution.py:23
  310.0 48.0 %while.32 = (s32[]{:T(128)}, f32[32,64,128]{2,1,0:T(8,128)S(1)}, s32[]{:T(128)}, f32[32,32]{1,0:T(8,128)S(1)}, f32[32,32,64,128]{3,2,1,0:T(8,128)}, /*index=5*/s32[]{:T(128)}, s32[]{:T(128)}) while((s32[]{:T(128)}, f32[32,64,128]{2,1,0:T(8,128)S(1)}, s32[]{:T(128)}, f32[32,32]{1,0:T(8,128)S(1)}, f32[32,32,64,128]{3,2,1,0:T(8,128)}, ...), condition=%wide.region_7.8_spmd.clone, body=%wide.region_6.7_spmd.clone.sunk | while | flops 1048580 | bytes 3146217 | solution.py:33
  311.5 1.5 fusion.61
  313.0 1.5 fusion.61
  358.1 4.5 multiply_add_fusion
  362.6 4.2 gather_fusion.1
  366.8 2.5 add_select_fusion
  370.8 5.6 %all-to-all-start = ((f32[2,32,64,128]{3,2,0,1:T(8,128)}), f32[2,32,64,128]{3,2,0,1:T(8,128)}, u32[]{:S(2)}, u32[]{:S(2)}) async-start(f32[2,32,64,128]{3,2,0,1:T(8,128)} %copy.198), calls=%async_computation | async-start | bytes 4194304 | tf_op jit(solution)/shard_map/all_to_all | solution.py:254
  378.6 46.3 %all-to-all-done = f32[2,32,64,128]{3,2,0,1:T(8,128)} async-done(((f32[2,32,64,128]{3,2,0,1:T(8,128)}), f32[2,32,64,128]{3,2,0,1:T(8,128)}, u32[]{:S(2)}, u32[]{:S(2)}) %all-to-all-start) | async-done | bytes 2097184 | tf_op jit(solution)/shard_map/all_to_all | solution.py:254
  424.8 3.3 gather_fusion.7
  428.1 6.6 %all-to-all-start.1 = ((f32[32,1,1,64,128]{4,3,2,1,0:T(8,128)}), f32[32,1,1,64,128]{4,3,2,1,0:T(8,128)}, u32[]{:S(2)}, u32[]{:S(2)}) async-start(f32[32,1,1,64,128]{4,3,2,1,0:T(8,128)} %bitcast.44), calls=%async_computation.1 | async-start | bytes 2097152 | tf_op jit(solution)/shard_map/all_to_all | solution.py:269
  434.7 6.3 %fusion.4 = f32[4,2,16,64,128]{4,3,2,1,0:T(8,128)} fusion(f32[4,2,16,128]{3,2,1,0:T(8,128)S(1)} %bitcast.172, f32[4,2,16,128]{3,2,1,0:T(8,128)S(1)} %bitcast.171, f32[4,2,128,128]{3,2,1,0:T(8,128)S(1)} %fusion.31, pred[4,128,128]{2,1,0:T(8,128)(4,1)S(1)} %compare_and_fusion, bf16[4,128,2,16,64]{1,0,4,3,2:T(4,128)(2,1)} %reshape.638), kind=kOutput, calls=%fused_computation.30 | convolution fusion | flops 278921216 | bytes 7012352 | tf_op jit(solution)/shard_map/cghts,csghp->ctghp/dot_general | solution.py:143
  442.5 7.7 %fusion.9 = f32[4,128,2,16,64]{1,4,3,2,0:T(8,128)} fusion(f32[4,2,16,64,128]{4,3,2,1,0:T(8,128)} %fusion.4, f32[4,2,16,64,128]{4,3,2,1,0:T(8,128)} %bitcast.148, f32[4,128,2,16]{1,3,2,0:T(8,128)S(1)} %copy-done.9, bf16[4,128,2,128,1]{3,2,1,0,4:T(2,128)(2,1)S(1)} %bitcast.160), kind=kOutput, calls=%fused_computation.36 | convolution fusion | flops 1612709888 | bytes 12910592 | tf_op jit(solution)/shard_map/ctgn,cghpn->ctghp/dot_general | solution.py:186
  450.2 9.1 %copy.209 = f32[4,128,2,16,64]{4,3,2,1,0:T(8,128)} copy(f32[4,128,2,16,64]{1,4,3,2,0:T(8,128)} %fusion.9) | data formatting | bytes 8388608 | tf_op jit(solution)/shard_map/reshape | solution.py:194
  459.3 7.8 %reshape.779 = f32[512,2048]{1,0:T(8,128)} reshape(f32[4,128,2,16,64]{4,3,2,1,0:T(8,128)} %copy.209) | data formatting | bytes 8388608 | tf_op jit(solution)/shard_map/reshape | solution.py:194
  467.2 6.3 %fusion.49 = f32[512,2048]{1,0:T(8,128)} fusion(bf16[1,512,2048]{2,1,0:T(8,128)(2,1)} %param.20, f32[512,2048]{1,0:T(8,128)} %reshape.779, bf16[512,2048]{1,0:T(8,128)(2,1)S(1)} %multiply_convert_fusion.4, f32[2048]{0:T(1024)S(1)} %mul.341), kind=kLoop, calls=%fused_computation.164 | loop fusion | flops 10485760 | bytes 12591104 | tf_op jit(solution)/shard_map/mul | solution.py:199
  473.5 6.6 %mul.347 = f32[512,2,1024]{2,1,0:T(2,128)} reshape(f32[512,2048]{1,0:T(8,128)} %fusion.49) | data formatting | bytes 8388608 | tf_op jit(solution)/shard_map/mul | solution.py:199
  480.1 3.4 reduce_sum.85
  483.5 2.5 collective-permute-start.1
  487.2 2.0 copy.218
  490.0 2.8 fusion.16
  (257 shorter events, 110.5 us)
Async XLA Ops:
  7.2 19.9 %copy-start.33 = (f32[2,256]{1,0:T(2,128)S(1)}, f32[2,256]{1,0:T(2,128)}, u32[]{:S(2)}) copy-start(f32[2,256]{1,0:T(2,128)} %param.25) | copy-start | bytes 6148
  7.2 21.1 %copy-start.15 = (f32[2048]{0:T(1024)S(1)}, f32[2048]{0:T(1024)}, u32[]{:S(2)}) copy-start(f32[2048]{0:T(1024)} %param.23) | copy-start | bytes 24580
  7.2 302.8 %all-gather.4.cloned.1.call-start = ((), (), s32[]{:S(2)}) async-start(), calls=%async_computation.4 | async-start | bytes 34603008 | tf_op jit(solution)/shard_map/all_gather | solution.py:23
  8.7 18.9 %collective-permute-start = (bf16[3,2560]{1,0:T(4,128)(2,1)S(1)}, bf16[3,2560]{1,0:T(4,128)(2,1)S(1)}, u32[]{:S(2)}, u32[]{:S(2)}) collective-permute-start(bf16[3,2560]{1,0:T(4,128)(2,1)S(1)} %pad_maximum_fusion.2), channel_id=1, source_target_pairs={{0,8},{8,16},{16,24},{24,32},{32,40},{40,48},{48,56},{56,64},{64,7... | collective-permute-start | bytes 46088 | tf_op jit(solution)/shard_map/ppermute | solution.py:18
  18.9 5.0 %copy-start.20 = (s32[32]{0:T(128)}, s32[32]{0:T(128)S(1)}, u32[]{:S(2)}) copy-start(s32[32]{0:T(128)S(1)} %add_reduce_fusion) | copy-start | bytes 388
  19.5 1.1 copy-start.31
  21.9 5.8 %copy-start.8 = (f32[4,128,32]{2,1,0:T(8,128)}, f32[4,128,32]{2,1,0:T(8,128)S(1)}, u32[]{:S(2)}) copy-start(f32[4,128,32]{2,1,0:T(8,128)S(1)} %exponential_select_fusion) | copy-start | bytes 196612
  23.2 16.7 %copy-start.25 = (pred[512]{0:T(512)(128)(4,1)}, pred[512]{0:T(512)(128)(4,1)S(1)}, u32[]{:S(2)}) copy-start(pred[512]{0:T(512)(128)(4,1)S(1)} %get-tuple-element.238) | copy-start | bytes 1540
  27.6 0.6 copy-start.12
  27.7 12.3 %copy-start.10 = (bf16[3,2048]{1,0:T(4,128)(2,1)}, bf16[3,2048]{1,0:T(4,128)(2,1)S(1)}, u32[]{:S(2)}) copy-start(bf16[3,2048]{1,0:T(4,128)(2,1)S(1)} %slice.160) | copy-start | bytes 36868
  37.4 7.3 %copy-start.17 = (f32[1,2,2,128]{3,1,2,0:T(2,128)S(1)}, f32[1,2,2,128]{3,1,2,0:T(2,128)}, u32[]{:S(2)}) copy-start(f32[1,2,2,128]{3,1,2,0:T(2,128)} %copy.216) | copy-start | bytes 6148
  37.4 7.3 %copy-start.18 = (f32[1,2,2,128]{3,1,2,0:T(2,128)S(1)}, f32[1,2,2,128]{3,1,2,0:T(2,128)}, u32[]{:S(2)}) copy-start(f32[1,2,2,128]{3,1,2,0:T(2,128)} %copy.217) | copy-start | bytes 6148
  37.4 7.3 %copy-start.19 = (f32[1,2,2,128]{3,1,2,0:T(2,128)S(1)}, f32[1,2,2,128]{3,1,2,0:T(2,128)}, u32[]{:S(2)}) copy-start(f32[1,2,2,128]{3,1,2,0:T(2,128)} %copy.212) | copy-start | bytes 6148
  37.4 7.3 %copy-start.26 = (pred[512]{0:T(512)(128)(4,1)S(1)}, pred[512]{0:T(512)(128)(4,1)}, u32[]{:S(2)}) copy-start(pred[512]{0:T(512)(128)(4,1)} %get-tuple-element.239) | copy-start | bytes 1540
  37.4 7.3 %copy-start.27 = (pred[512]{0:T(512)(128)(4,1)S(1)}, pred[512]{0:T(512)(128)(4,1)}, u32[]{:S(2)}) copy-start(pred[512]{0:T(512)(128)(4,1)} %get-tuple-element.240) | copy-start | bytes 1540
  37.4 7.3 %copy-start.28 = (pred[512]{0:T(512)(128)(4,1)S(1)}, pred[512]{0:T(512)(128)(4,1)}, u32[]{:S(2)}) copy-start(pred[512]{0:T(512)(128)(4,1)} %get-tuple-element.241) | copy-start | bytes 1540
  50.4 2.7 copy-start.3
  55.7 16.2 %copy-start.21 = (s32[32]{0:T(128)S(1)}, s32[32]{0:T(128)}, u32[]{:S(2)}) copy-start(s32[32]{0:T(128)} %copy-done.20) | copy-start | bytes 388
  55.7 18.1 %copy-start.32 = (s32[32]{0:T(128)S(1)}, s32[32]{0:T(128)}, u32[]{:S(2)}) copy-start(s32[32]{0:T(128)} %copy-done.31) | copy-start | bytes 388
  71.0 1.0 copy-start
  71.0 5.2 %copy-start.13 = (f32[32]{0:T(128)}, f32[32]{0:T(128)S(1)}, u32[]{:S(2)}) copy-start(f32[32]{0:T(128)S(1)} %get-tuple-element.140) | copy-start | bytes 388
  74.5 1.7 copy-start.24
  84.9 15.5 %copy-start.22 = (pred[2]{0:T(512)(128)(4,1)}, pred[2]{0:T(512)(128)(4,1)S(1)}, u32[]{:S(2)}) copy-start(pred[2]{0:T(512)(128)(4,1)S(1)} %get-tuple-element.217) | copy-start | bytes 10
  89.4 10.2 %copy-start.4 = (bf16[4,128,2,128]{3,2,1,0:T(2,128)(2,1)S(1)}, bf16[4,128,2,128]{3,2,1,0:T(2,128)(2,1)}, u32[]{:S(2)}) copy-start(bf16[4,128,2,128]{3,2,1,0:T(2,128)(2,1)} %reshape.640) | copy-start | bytes 786436
  105.2 34.4 %copy-start.14 = (f32[32]{0:T(128)S(1)}, f32[32]{0:T(128)}, u32[]{:S(2)}) copy-start(f32[32]{0:T(128)} %copy-done.13) | copy-start | bytes 388
  125.7 76.0 %all-to-all-start.2 = ((bf16[2,32,240]{2,0,1:T(2,128)(2,1)}), bf16[2,32,240]{2,0,1:T(2,128)(2,1)}, u32[]{:S(2)}, u32[]{:S(2)}) async-start(bf16[2,32,240]{2,0,1:T(2,128)(2,1)} %copy.200), calls=%async_computation.2 | async-start | bytes 65536 | tf_op jit(solution)/shard_map/all_to_all | solution.py:255
  203.8 167.0 %all-to-all-start.3 = ((bf16[32,1,1,240]{3,2,1,0:T(2,128)(2,1)}), bf16[32,1,1,240]{3,2,1,0:T(2,128)(2,1)S(1)}, u32[]{:S(2)}, u32[]{:S(2)}) async-start(bf16[32,1,1,240]{3,2,1,0:T(2,128)(2,1)} %copy.201), calls=%async_computation.3 | async-start | bytes 65536 | tf_op jit(solution)/shard_map/all_to_all | solution.py:270
  310.0 48.1 %copy-start.30 = (f32[4,32]{1,0:T(4,128)S(1)}, f32[4,32]{1,0:T(4,128)}, u32[]{:S(2)}) copy-start(f32[4,32]{1,0:T(4,128)} %get-tuple-element.139) | copy-start | bytes 1540
  362.6 4.2 copy-start.23
  362.6 4.2 copy-start.29
  369.3 7.2 %copy-start.6 = (f32[4,128,32]{2,1,0:T(8,128)S(1)}, f32[4,128,32]{2,1,0:T(8,128)}, u32[]{:S(2)}) copy-start(f32[4,128,32]{2,1,0:T(8,128)} %get-tuple-element.224) | copy-start | bytes 196612
  369.3 7.3 %copy-start.34 = (f32[32]{0:T(128)S(1)}, f32[32]{0:T(128)}, u32[]{:S(2)}) copy-start(f32[32]{0:T(128)} %param.28) | copy-start | bytes 388
  369.3 7.7 %copy-start.7 = (bf16[512,256]{1,0:T(8,128)(2,1)S(1)}, bf16[512,256]{1,0:T(8,128)(2,1)}, u32[]{:S(2)}) copy-start(bf16[512,256]{1,0:T(8,128)(2,1)} %get-tuple-element.227) | copy-start | bytes 786436
  369.4 7.7 %copy-start.5 = (bf16[4,128,2,128]{3,2,1,0:T(2,128)(2,1)S(1)}, bf16[4,128,2,128]{3,2,1,0:T(2,128)(2,1)}, u32[]{:S(2)}) copy-start(bf16[4,128,2,128]{3,2,1,0:T(2,128)(2,1)} %reshape.640) | copy-start | bytes 786436
  370.8 5.6 %copy-start.11 = (bf16[32,1,1,240]{3,2,1,0:T(2,128)(2,1)}, bf16[32,1,1,240]{3,2,1,0:T(2,128)(2,1)S(1)}, u32[]{:S(2)}) copy-start(bf16[32,1,1,240]{3,2,1,0:T(2,128)(2,1)S(1)} %all-to-all-done.3) | copy-start | bytes 46084
  370.8 54.0 %all-to-all-start = ((f32[2,32,64,128]{3,2,0,1:T(8,128)}), f32[2,32,64,128]{3,2,0,1:T(8,128)}, u32[]{:S(2)}, u32[]{:S(2)}) async-start(f32[2,32,64,128]{3,2,0,1:T(8,128)} %copy.198), calls=%async_computation | async-start | bytes 4194304 | tf_op jit(solution)/shard_map/all_to_all | solution.py:254
  377.4 63.6 %collective-permute-start.2 = (bf16[1,1,32,240]{3,0,2,1:T(2,128)(2,1)}, bf16[1,1,32,240]{3,0,2,1:T(2,128)(2,1)S(1)}, u32[]{:S(2)}, u32[]{:S(2)}) collective-permute-start(bf16[1,1,32,240]{3,0,2,1:T(2,128)(2,1)} %bitcast.178), channel_id=1, source_target_pairs={{0,1},{1,0},{2,3},{3,2},{4,5},{5,4},{6,7},{7,6},{8,9},{9,8},{10,11... | collective-permute-start | bytes 46088 | tf_op jit(solution)/shard_map/ppermute | solution.py:37
  428.1 55.3 %all-to-all-start.1 = ((f32[32,1,1,64,128]{4,3,2,1,0:T(8,128)}), f32[32,1,1,64,128]{4,3,2,1,0:T(8,128)}, u32[]{:S(2)}, u32[]{:S(2)}) async-start(f32[32,1,1,64,128]{4,3,2,1,0:T(8,128)} %bitcast.44), calls=%async_computation.1 | async-start | bytes 2097152 | tf_op jit(solution)/shard_map/all_to_all | solution.py:269
  434.7 7.8 %copy-start.9 = (f32[4,128,2,16]{1,3,2,0:T(8,128)S(1)}, f32[4,128,2,16]{1,3,2,0:T(8,128)}, u32[]{:S(2)}) copy-start(f32[4,128,2,16]{1,3,2,0:T(8,128)} %get-tuple-element.228) | copy-start | bytes 196612
  483.5 9.4 %collective-permute-start.1 = (f32[1,1,32,64,128]{4,3,2,1,0:T(8,128)}, f32[1,1,32,64,128]{4,3,2,1,0:T(8,128)S(1)}, u32[]{:S(2)}, u32[]{:S(2)}) collective-permute-start(f32[1,1,32,64,128]{4,3,2,1,0:T(8,128)} %bitcast.45), channel_id=1, source_target_pairs={{0,1},{1,0},{2,3},{3,2},{4,5},{5,4},{6,7},{7,6},{8,9},{9,8},{10,11... | collective-permute-start | bytes 3145736 | tf_op jit(solution)/shard_map/ppermute | solution.py:37
  487.2 2.2 copy-start.1
  487.2 2.9 copy-start.2
  487.2 2.9 copy-start.16
Sparse Core Ops, SparseCore 0:
  72.1 237.8 all-gather.3
where the time goes:
time: 505 us; the launch traced here: 501 us
  waiting for transfers between devices  148 us (29%)
  other arithmetic  117 us (23%)
  local copies, waits for them, and re-layouts  102 us (20%)
  blocking collectives  61.7 us (12%)
  starting transfers between devices  35.7 us (7%)
  matrix products  19.9 us (4%)
  between operations  15.3 us (3%)
    all_gather x1, waiting for transfers between devices, entering_2(): everything = jax.tree.map(lambda part: lax.all_gather(part, axis), x)  101 us
    unnamed x1, blocking collectives  61.7 us
    select_n x32, other arithmetic, step(): return jax.tree.map(lambda a, b: jnp.where(reached, a, b), new, before)  46.8 us
    all_to_all x1, waiting for transfers between devices, on_device(): lax.all_to_all(finals, 'ctx', split_axis=1, concat_axis=0, tiled=True)  46.3 us
    reshape x2, local copies, waits for them, and re-layouts, on_device(): (inner + inter).reshape(tok_count, inner_width)  16.9 us
    unnamed x87, local copies, waits for them, and re-layouts  13.7 us
    convert_element_type x2, other arithmetic, conv_silu(): return jax.nn.silu(summed).astype(jnp.bfloat16)  12.2 us
    all_to_all x1, starting transfers between devices, on_device(): lax.all_to_all(send_tail, 'ctx', split_axis=1, concat_axis=0, tiled=True)  11 us
  transfers between devices with their start and end apart: 8, of which 2 were waited for; matrix products, arithmetic and copies ran while one was open for 38% of the time, Pallas kernels for 0%

commit v1 on v0

v1 whole, which is shorter than its diff:
```python
import functools

import jax
import jax.numpy as jnp
from jax import lax
from jax.experimental import pallas as pl
from jax.experimental.pallas import tpu as pltpu
from jax.sharding import PartitionSpec as P

HEAD_DIM = 64
STATE = 128
STRETCH = 128
LANES = 128
HALO = 16
KW = 4
EPS = 1e-05
BF = jnp.bfloat16
F32 = jnp.float32
I32 = jnp.int32
VMEM_LIMIT = 48 * 1024 * 1024

TOK = 512
NC = TOK // STRETCH
WIDTH = 2048
HEADS = WIDTH // HEAD_DIM
GROUPS = 2
GWIDTH = WIDTH // GROUPS
BCW = 512
REQS = 32
STEPS = 4
SW = WIDTH // STEPS
SLT = SW // LANES
ROWS_A = NC * STRETCH + 2 * STRETCH + 16
PIECE = 3 * 64 + 16
BACK = 64 + 16


def shift_in(block, distance):
    count = lax.axis_size("ctx")
    return lax.ppermute(block, "ctx", [(i, i + distance) for i in range(count - distance)])


def swish(v):
    half = 0.5 * v
    return half + half * jnp.tanh(half)


def split3(v, lane):
    hi = v.astype(BF).astype(F32)
    rest = v - hi
    mid = rest.astype(BF).astype(F32)
    low = rest - mid
    return jnp.where(
        lane < HEADS, hi, jnp.where(lane < 2 * HEADS, mid, jnp.where(lane < 3 * HEADS, low, 0.0))
    ).astype(BF)


def spread_matrix(first_head, width):
    row = lax.broadcasted_iota(I32, (LANES, width), 0)
    col = lax.broadcasted_iota(I32, (LANES, width), 1)
    same = ((row & (HEADS - 1)) == (col >> 6) + first_head) & (row < 3 * HEADS)
    return jnp.where(same, 1.0, 0.0).astype(BF)


def conv_tile(ext, taps, bias, masks):
    acc = bias + taps[KW - 1] * ext[HALO:]
    for d in range(1, KW):
        acc = acc + taps[KW - 1 - d] * (pltpu.roll(ext, d, 0)[HALO:] * masks[d - 1])
    return swish(acc)


def stage_a(
    idx_ref, len_ref, x_ref, xh_ref, bc_ref, bch_ref, dt_ref, wx_ref, bx_ref, wbc_ref, bbc_ref,
    al_ref, db_ref,
    piece_ref, s_ref, d_ref, eg_ref, ent_ref, xc_ref, bcc_ref, cum_ref, step_ref, fl_ref,
    mask_scr, wst_scr, spread_scr, bt_scr, entf_scr, first_scr, sc_scr,
):
    s = pl.program_id(0)
    lane = lax.broadcasted_iota(I32, (STRETCH, LANES), 1)
    row = lax.broadcasted_iota(I32, (STRETCH, LANES), 0)

    @pl.when(s == 0)
    def _():
        start = -idx_ref[0] * TOK
        zero = jnp.int32(0)

        def scan(r, carry):
            first, count, e0, f0, e1, f1, fa = carry
            last = first + len_ref[0, r] - 1
            first_scr[r] = first
            ends = (last >= 0) & (last < TOK)
            take0, take1 = ends & (count == 0), ends & (count == 1)
            fa = tuple(
                jnp.where(
                    (first <= c * STRETCH + STRETCH - 1) & (last >= c * STRETCH + STRETCH - 1),
                    first,
                    fa[c],
                )
                for c in range(NC)
            )
            return (
                last + 1,
                count + jnp.where(ends, 1, 0),
                jnp.where(take0, last, e0),
                jnp.where(take0, first, f0),
                jnp.where(take1, last, e1),
                jnp.where(take1, first, f1),
                fa,
            )

        _, _, e0, f0, e1, f1, fa = lax.fori_loop(
            0, REQS, scan, (start, zero, zero, zero, zero, zero, (zero,) * NC)
        )
        sc_scr[0], sc_scr[1], sc_scr[2], sc_scr[3] = e0, f0, e1, f1

        for c in range(NC):
            rows = pl.ds(c * STRETCH, STRETCH)
            here = row + c * STRETCH

            def later(r, fl):
                return jnp.where(here >= first_scr[r], first_scr[r], fl)

            fl = lax.fori_loop(0, REQS, later, jnp.full((STRETCH, LANES), start, I32))
            fl_ref[rows, :] = fl
            for d in range(1, KW):
                mask_scr[d - 1, rows, :] = jnp.where(here - fl >= d, 1.0, 0.0)

        raw = dt_ref[...] + db_ref[...]
        step = jnp.maximum(raw, 0.0) + jnp.log1p(jnp.exp(-jnp.abs(raw)))
        step_ref[...] = step
        log_decay = -jnp.exp(al_ref[...]) * step
        lower = jnp.where(row >= lane, 1.0, 0.0)
        for c in range(NC):
            cum_ref[c * STRETCH : (c + 1) * STRETCH, :] = jnp.dot(
                lower,
                log_decay[c * STRETCH : (c + 1) * STRETCH, :],
                precision=lax.Precision.HIGHEST,
                preferred_element_type=F32,
            )
        through = []
        for c in range(NC):
            rows = slice(c * STRETCH, (c + 1) * STRETCH)
            cum = cum_ref[rows, :]
            end = cum[STRETCH - 1 :, :]
            w = jnp.where(row + c * STRETCH >= fa[c], jnp.exp(end - cum) * step_ref[rows, :], 0.0)
            wst_scr[rows, :] = split3(w, lane)
            through.append(jnp.where(fa[c] < c * STRETCH, jnp.exp(end), 0.0))
        inflow_end = []
        for k, (e, f) in enumerate(((e0, f0), (e1, f1))):
            base = pl.multiple_of((e >> 7) * STRETCH, STRETCH)
            here = row + base
            end = cum_ref[pl.ds(e, 1), :]
            w = jnp.exp(end - cum_ref[pl.ds(base, STRETCH), :]) * step_ref[pl.ds(base, STRETCH), :]
            w = jnp.where((here >= f) & (here <= e), w, 0.0)
            at = (NC + k) * STRETCH
            wst_scr[at : at + STRETCH, :] = split3(w, lane)
            inflow_end.append(jnp.where(f < base, jnp.exp(end), 0.0))
        gains = [jnp.ones((1, LANES), F32)]
        for c in range(NC):
            gains.append(gains[-1] * through[c])
        gain_end = gains[0]
        for c in range(1, NC):
            gain_end = jnp.where((e0 >> 7) == c, gains[c], gain_end)
        extra = jnp.zeros((16, LANES), F32)
        row16 = lax.broadcasted_iota(I32, (16, LANES), 0)
        lane16 = lax.broadcasted_iota(I32, (16, LANES), 1)
        for i, v in enumerate(through + gains[:NC] + inflow_end + [gain_end * inflow_end[0], gains[NC]]):
            extra = jnp.where(row16 == i, v, extra)
        wst_scr[(NC + 2) * STRETCH :, :] = split3(extra, lane16)

        for part in range(2):
            for g in range(GROUPS):
                at = slice((part * GROUPS + g) * LANES, (part * GROUPS + g + 1) * LANES)
                own = slice(g * LANES, (g + 1) * LANES)
                taps = [wbc_ref[k, part : part + 1, own] for k in range(KW)]
                bias = bbc_ref[part : part + 1, own]
                for c in range(NC):
                    if c == 0:
                        ext = jnp.concatenate([bch_ref[:, at], bc_ref[0:STRETCH, at]], axis=0)
                    else:
                        ext = bc_ref[c * STRETCH - HALO : (c + 1) * STRETCH, at]
                    rows = slice(c * STRETCH, (c + 1) * STRETCH)
                    masks = [mask_scr[d, rows, :] for d in range(KW - 1)]
                    out = conv_tile(ext.astype(F32), taps, bias, masks).astype(BF)
                    bcc_ref[rows, at] = out
                    if part == 0:
                        bt_scr[g * NC + c] = out.astype(F32).T.astype(BF)

    e0, f0, e1, f1 = sc_scr[0], sc_scr[1], sc_scr[2], sc_scr[3]
    spread_scr[...] = jnp.dot(
        wst_scr[...], spread_matrix(s * (SW // HEAD_DIM), SW), preferred_element_type=F32
    )
    ex = (NC + 2) * STRETCH
    group = s // (STEPS // GROUPS)
    d_ref[...] = jnp.broadcast_to(spread_scr[ex + 11 : ex + 12, :], (8, SW))
    eg_ref[...] = spread_scr[ex : ex + 8, :]
    for c in range(NC):
        rows = slice(c * STRETCH, (c + 1) * STRETCH)
        masks = [mask_scr[d, rows, :] for d in range(KW - 1)]
        scaled = []
        for t in range(SLT):
            at = slice(t * LANES, (t + 1) * LANES)
            if c == 0:
                ext = jnp.concatenate([xh_ref[:, at], x_ref[0:STRETCH, at]], axis=0)
            else:
                ext = x_ref[c * STRETCH - HALO : (c + 1) * STRETCH, at]
            taps = [wx_ref[k : k + 1, at] for k in range(KW)]
            out = conv_tile(ext.astype(F32), taps, bx_ref[:, at], masks).astype(BF)
            xc_ref[rows, at] = out
            scaled.append((out.astype(F32) * spread_scr[rows, at]).astype(BF))
        local = jnp.dot(
            bt_scr[group * NC + c], jnp.concatenate(scaled, axis=1), preferred_element_type=F32
        )
        if c == 0:
            entf_scr[0] = jnp.zeros((STATE, SW), F32)
            ent_ref[0] = jnp.zeros((STATE, SW), BF)
            entering = local
        else:
            entering = spread_scr[ex + c : ex + c + 1, :] * entf_scr[c] + local
        if c < NC - 1:
            entf_scr[c + 1] = entering
            ent_ref[c + 1] = entering.astype(BF)
        else:
            leaving = entering.astype(BF)
            s_ref[...] = leaving
            for j in range(2 * SLT):
                piece_ref[j, 128:192, :] = leaving[
                    (j % 2) * 64 : (j % 2) * 64 + 64, (j // 2) * LANES : (j // 2 + 1) * LANES
                ]
    for k, e in enumerate((e0, e1)):
        c = e >> 7
        base = pl.multiple_of(c * STRETCH, STRETCH)
        at = (NC + k) * STRETCH
        scaled = (
            xc_ref[pl.ds(base, STRETCH), :].astype(F32) * spread_scr[at : at + STRETCH, :]
        ).astype(BF)
        final = spread_scr[ex + 8 + k : ex + 9 + k, :] * entf_scr[c] + jnp.dot(
            bt_scr[group * NC + c], scaled, preferred_element_type=F32
        )
        final = final.astype(BF)
        for j in range(2 * SLT):
            piece_ref[j, k * 64 : k * 64 + 64, :] = final[
                (j % 2) * 64 : (j % 2) * 64 + 64, (j // 2) * LANES : (j // 2 + 1) * LANES
            ]

    tails_x, tails_bc = [], []
    pick_row = lax.broadcasted_iota(I32, (16, 2 * HALO), 0)
    pick_col = lax.broadcasted_iota(I32, (16, 2 * HALO), 1)
    for e, f in ((e0, f0), (e1, f1)):
        base = pl.multiple_of((e >> 4) * HALO, HALO)
        before = pl.multiple_of(jnp.maximum(base - HALO, 0), HALO)
        source = e - (KW - 2) + pick_row
        pick = (pick_col + base - HALO == source) & (source >= f) & (pick_row < KW - 1)
        pick = jnp.where(pick, 1.0, 0.0).astype(BF)

        def tail(ref, halo_ref):
            head = jnp.where(base > 0, ref[pl.ds(before, HALO), :], halo_ref[...])
            window = jnp.concatenate([head, ref[pl.ds(base, HALO), :]], axis=0)
            return jnp.dot(pick, window, preferred_element_type=F32)

        tails_x.append(tail(x_ref, xh_ref))
        tails_bc.append(tail(bc_ref, bch_ref))
    row16 = lax.broadcasted_iota(I32, (16, LANES), 0)
    for t in range(SLT):
        at = slice(t * LANES, (t + 1) * LANES)
        gain_hi = spread_scr[ex + 10 : ex + 11, at].astype(BF).astype(F32)
        gain_lo = spread_scr[ex + 10 : ex + 11, at] - gain_hi
        pass_hi = spread_scr[ex + 11 : ex + 12, at].astype(BF).astype(F32)
        pass_lo = spread_scr[ex + 11 : ex + 12, at] - pass_hi
        bc_rows = []
        for k in range(2):
            one = tails_bc[k][:, at]
            bc_rows.append(jnp.sum(jnp.where(row16 == s, one, 0.0), axis=0, keepdims=True))
        for half in range(2):
            block = jnp.zeros((16, LANES), F32)
            values = [gain_hi, gain_lo, pass_hi, pass_lo]
            for k in range(2):
                one = tails_x[k][:, at]
                values += [one[0:1], one[1:2]] if half == 0 else [one[2:3], bc_rows[k]]
            for i, v in enumerate(values):
                block = jnp.where(row16 == i, v, block)
            piece_ref[2 * t + half, 192:208, :] = block.astype(BF)


def stage_b(xc_ref, bcc_ref, cum_ref, step_ref, fl_ref, skip_ref, y_ref):
    c = pl.program_id(0)
    row = lax.broadcasted_iota(I32, (STRETCH, LANES), 0)
    lane = lax.broadcasted_iota(I32, (STRETCH, LANES), 1)
    keep = (lane <= row) & (lane + c * STRETCH >= fl_ref[...])
    cum = cum_ref[...]
    cum_t = cum.T
    step_t = step_ref[...].T
    low = lax.broadcasted_iota(I32, (STRETCH, LANES), 1) < HEAD_DIM
    for g in range(GROUPS):
        b = bcc_ref[:, g * LANES : (g + 1) * LANES]
        cc = bcc_ref[:, (GROUPS + g) * LANES : (GROUPS + g + 1) * LANES]
        scores = lax.dot_general(cc, b, (((1,), (1,)), ((), ())), preferred_element_type=F32)
        for i in range(HEADS // GROUPS // 2):
            pair = g * (HEADS // GROUPS // 2) + i
            weights = []
            for h in (2 * pair, 2 * pair + 1):
                decay = jnp.exp(jnp.where(keep, cum[:, h : h + 1] - cum_t[h : h + 1, :], -jnp.inf))
                weights.append((scores * (decay * step_t[h : h + 1, :])).astype(BF))
            at = slice(pair * LANES, (pair + 1) * LANES)
            x = xc_ref[:, at]
            xf = x.astype(F32)
            both = jnp.concatenate(
                [jnp.where(low, xf, 0.0).astype(BF), jnp.where(low, 0.0, xf).astype(BF)], axis=0
            )
            inner = jnp.dot(
                jnp.concatenate(weights, axis=1), both, preferred_element_type=F32
            )
            y_ref[:, at] = inner + skip_ref[:, at] * xf


def stage_c(
    y_ref, z_ref, c_ref, ent_ref, s1_ref, s2_ref, d1_ref, eg_ref, cum_ref, fl_ref, gain_ref, out_ref
):
    g, c = pl.program_id(0), pl.program_id(1)
    lane = lax.broadcasted_iota(I32, (STRETCH, LANES), 1)
    inflow = jnp.where(fl_ref[...] < c * STRETCH, jnp.exp(cum_ref[...]), 0.0)
    wide = jnp.dot(
        split3(inflow, lane),
        spread_matrix(g * (HEADS // GROUPS), GWIDTH),
        preferred_element_type=F32,
    )
    incoming = s1_ref[...].astype(F32) + d1_ref[0:1, :] * s2_ref[...].astype(F32)
    entering = ent_ref[0].astype(F32) + eg_ref[pl.ds(NC + c, 1), :] * incoming
    carried = jnp.dot(c_ref[...], entering.astype(BF), preferred_element_type=F32)
    gated = (y_ref[...] + wide * carried) * swish(z_ref[...].astype(F32))
    mean = jnp.sum(gated * gated, axis=1, keepdims=True) * (1.0 / GWIDTH)
    out_ref[...] = (gated * lax.rsqrt(mean + EPS) * gain_ref[...]).astype(BF)


def combine(len_ref, owner_ref, got_ref, out_ref):
    row16 = lax.broadcasted_iota(I32, (16, LANES), 0)

    def one(r, carry):
        first, before = carry
        last = first + len_ref[0, r] - 1
        home = last >> 9
        second = before == home
        h1, h2 = jnp.maximum(home - 1, 0), jnp.maximum(home - 2, 0)
        slot = owner_ref[0, r]
        extra = got_ref[home, 192:208, :].astype(F32)
        extra1 = got_ref[h1, 192:208, :].astype(F32)
        gain = jnp.where(second, 0.0, extra[0:1] + extra[1:2])
        passing = extra1[2:3] + extra1[3:4]
        k = pl.multiple_of(jnp.where(second, 64, 0), 64)
        own = got_ref[home, pl.ds(k, 64), :].astype(F32)
        s1 = got_ref[h1, 128:192, :].astype(F32)
        s2 = got_ref[h2, 128:192, :].astype(F32)
        out_ref[slot, 0:64, :] = (own + gain * (s1 + passing * s2)).astype(BF)
        tail = jnp.where(second, pltpu.roll(extra, 10, 0), pltpu.roll(extra, 12, 0))
        out_ref[slot, 64:80, :] = jnp.where(row16 < 2, tail, 0.0).astype(BF)
        return last + 1, home

    lax.fori_loop(0, REQS, one, (jnp.int32(0), jnp.int32(-1)), unroll=2)


def finish(got_ref, state_ref, tx_ref, tbc_ref):
    tails = [got_ref[j, 64:80, :].astype(F32) for j in range(REQS)]
    for t in range(WIDTH // LANES):
        at = slice(t * LANES, (t + 1) * LANES)
        block = jnp.concatenate(
            [got_ref[2 * t, 0:64, :], got_ref[2 * t + 1, 0:64, :]], axis=0
        ).astype(F32)
        turned = block.T
        state_ref[2 * t] = turned[0:64]
        state_ref[2 * t + 1] = turned[64:128]
        tx_ref[:, at] = jnp.concatenate([tails[2 * t][0:2], tails[2 * t + 1][0:1]], axis=0).astype(BF)
    for k in range(KW - 1):
        for q in range(4):
            value = tails[2 * (4 * k + q) + 1][1:2].astype(BF)
            tbc_ref[k, q // 2 : q // 2 + 1, (q % 2) * LANES : (q % 2 + 1) * LANES] = value


def call(kernel, grid, ins, outs, scratch=(), flops=0, nbytes=0):
    return pl.pallas_call(
        kernel,
        grid=grid,
        in_specs=ins,
        out_specs=[o[1] for o in outs],
        out_shape=[o[0] for o in outs],
        scratch_shapes=list(scratch),
        compiler_params=pltpu.CompilerParams(vmem_limit_bytes=VMEM_LIMIT),
        cost_estimate=pl.CostEstimate(flops=flops, bytes_accessed=nbytes, transcendentals=0),
    )


def whole(*shape):
    return pl.BlockSpec(shape, lambda *_: (0,) * len(shape))


def on_device(
    x_in, bc_in, z_in, dt_in, conv_x_w, conv_x_b, conv_bc_w, conv_bc_b, a_log, dt_bias, skip_d,
    norm_gain, lengths, owner_slot,
):
    x = x_in[0]
    bc = bc_in[0].reshape(TOK, BCW)
    z = z_in[0]
    halo = shift_in(jnp.concatenate([x[TOK - HALO :], bc[TOK - HALO :]], axis=1), 1)
    dt = jnp.tile(dt_in[0], (1, 4))
    a_row = jnp.tile(a_log, 4).reshape(1, LANES)
    bias_row = jnp.tile(dt_bias, 4).reshape(1, LANES)
    index = lax.axis_index("ctx").astype(I32).reshape(1)
    smem = pl.BlockSpec(memory_space=pltpu.SMEM)
    shape = jax.ShapeDtypeStruct

    pieces, left, passing, entry, ent, xc, bcc, cum, step, fl = call(
        stage_a,
        (STEPS,),
        [
            smem,
            smem,
            pl.BlockSpec((TOK, SW), lambda s: (0, s)),
            pl.BlockSpec((HALO, SW), lambda s: (0, s)),
            whole(TOK, BCW),
            pl.BlockSpec((HALO, BCW), lambda s: (0, WIDTH // BCW)),
            whole(TOK, LANES),
            pl.BlockSpec((KW, SW), lambda s: (0, s)),
            pl.BlockSpec((1, SW), lambda s: (0, s)),
            whole(KW, 2, 2 * LANES),
            whole(2, 2 * LANES),
            whole(1, LANES),
            whole(1, LANES),
        ],
        [
            (shape((32, PIECE, LANES), BF), pl.BlockSpec((2 * SLT, PIECE, LANES), lambda s: (s, 0, 0))),
            (shape((STATE, WIDTH), BF), pl.BlockSpec((STATE, SW), lambda s: (0, s))),
            (shape((8, WIDTH), F32), pl.BlockSpec((8, SW), lambda s: (0, s))),
            (shape((8, WIDTH), F32), pl.BlockSpec((8, SW), lambda s: (0, s))),
            (shape((NC, STATE, WIDTH), BF), pl.BlockSpec((NC, STATE, SW), lambda s: (0, 0, s))),
            (shape((TOK, WIDTH), BF), pl.BlockSpec((TOK, SW), lambda s: (0, s))),
            (shape((TOK, BCW), BF), whole(TOK, BCW)),
            (shape((TOK, LANES), F32), whole(TOK, LANES)),
            (shape((TOK, LANES), F32), whole(TOK, LANES)),
            (shape((TOK, LANES), I32), whole(TOK, LANES)),
        ],
        [
            pltpu.VMEM((KW - 1, TOK, LANES), F32),
            pltpu.VMEM((ROWS_A, LANES), BF),
            pltpu.VMEM((ROWS_A, SW), F32),
            pltpu.VMEM((GROUPS * NC, STATE, STRETCH), BF),
            pltpu.VMEM((NC, STATE, SW), F32),
            pltpu.SMEM((REQS,), I32),
            pltpu.SMEM((4,), I32),
        ],
        flops=2 * 10**9,
        nbytes=10 * 2**20,
    )(
        index, lengths, x, halo, bc, halo, dt, conv_x_w, conv_x_b.reshape(1, WIDTH), conv_bc_w,
        conv_bc_b, a_row, bias_row,
    )

    got = lax.all_to_all(pieces, "ctx", split_axis=0, concat_axis=0, tiled=True)
    s1 = shift_in(left, 1)
    s2 = shift_in(left, 2)
    d1 = shift_in(passing, 1)

    (y,) = call(
        stage_b,
        (NC,),
        [
            pl.BlockSpec((STRETCH, WIDTH), lambda c: (c, 0)),
            pl.BlockSpec((STRETCH, BCW), lambda c: (c, 0)),
            pl.BlockSpec((STRETCH, LANES), lambda c: (c, 0)),
            pl.BlockSpec((STRETCH, LANES), lambda c: (c, 0)),
            pl.BlockSpec((STRETCH, LANES), lambda c: (c, 0)),
            whole(1, WIDTH),
        ],
        [(shape((TOK, WIDTH), F32), pl.BlockSpec((STRETCH, WIDTH), lambda c: (c, 0)))],
        flops=10**9,
        nbytes=20 * 2**20,
    )(xc, bcc, cum, step, fl, jnp.repeat(skip_d, HEAD_DIM).reshape(1, WIDTH))

    (back,) = call(
        combine,
        (),
        [smem, smem, pl.BlockSpec(memory_space=pltpu.VMEM)],
        [(shape((REQS, BACK, LANES), BF), pl.BlockSpec(memory_space=pltpu.VMEM))],
        flops=10**7,
        nbytes=3 * 2**20,
    )(lengths, owner_slot, got)
    own = lax.all_to_all(back, "ctx", split_axis=0, concat_axis=0, tiled=True)

    by_c = lambda g, c: (c, 0)
    by_g = lambda g, c: (0, g)
    by_cg = lambda g, c: (c, g)
    (mixed,) = call(
        stage_c,
        (GROUPS, NC),
        [
            pl.BlockSpec((STRETCH, GWIDTH), by_cg),
            pl.BlockSpec((STRETCH, GWIDTH), by_cg),
            pl.BlockSpec((STRETCH, LANES), lambda g, c: (c, GROUPS + g)),
            pl.BlockSpec((1, STATE, GWIDTH), lambda g, c: (c, 0, g)),
            pl.BlockSpec((STATE, GWIDTH), by_g),
            pl.BlockSpec((STATE, GWIDTH), by_g),
            pl.BlockSpec((8, GWIDTH), by_g),
            pl.BlockSpec((8, GWIDTH), by_g),
            pl.BlockSpec((STRETCH, LANES), by_c),
            pl.BlockSpec((STRETCH, LANES), by_c),
            pl.BlockSpec((1, GWIDTH), by_g),
        ],
        [(shape((TOK, WIDTH), BF), pl.BlockSpec((STRETCH, GWIDTH), by_cg))],
        flops=10**9,
        nbytes=15 * 2**20,
    )(y, z, bcc, ent, s1, s2, d1, entry, cum, fl, norm_gain.reshape(1, WIDTH))

    swapped = lax.ppermute(own, "side", [(0, 1), (1, 0)])
    state, tail_x, tail_bc = call(
        finish,
        (),
        [pl.BlockSpec(memory_space=pltpu.VMEM)],
        [
            (shape((HEADS, HEAD_DIM, STATE), F32), pl.BlockSpec(memory_space=pltpu.VMEM)),
            (shape((KW - 1, WIDTH), BF), pl.BlockSpec(memory_space=pltpu.VMEM)),
            (shape((KW - 1, 2, 2 * LANES), BF), pl.BlockSpec(memory_space=pltpu.VMEM)),
        ],
        flops=10**7,
        nbytes=3 * 2**20,
    )(swapped)
    return mixed[None], state[None, None], tail_x[None, None], tail_bc[None, None]


def solution(mesh):
    placed = (
        P("side", "ctx", "head"),
        P("side", "ctx", None, "head"),
        P("side", "ctx", "head"),
        P("side", "ctx", "head"),
        P(None, "head"),
        P("head"),
        P(None, None, "head"),
        P(None, "head"),
        P("head"),
        P("head"),
        P("head"),
        P("head"),
        P("side", None),
        P("side", None),
    )
    return jax.shard_map(
        on_device,
        mesh=mesh,
        in_specs=placed,
        out_specs=(
            P("side", "ctx", "head"),
            P("side", "ctx", "head", None, None),
            P("side", "ctx", None, "head"),
            P("side", "ctx", None, None, "head"),
        ),
        check_vma=False,
    )
```

time: 505 us -> 142 us (0.28)
  waiting for transfers between devices: 148 us -> 12.7 us
  other arithmetic: 117 us -> 0.01 us
  local copies, waits for them, and re-layouts: 102 us -> 6.73 us
  Pallas kernels: 0 us -> 27.8 us
  matrix products: 19.9 us -> 0 us
  starting transfers between devices: 35.7 us -> 17 us
  between operations: 15.3 us -> 0.83 us
  blocking collectives: 61.7 us -> 75.1 us
    all_gather x1 -> x0, waiting for transfers between devices: 101 us -> none  [entering_2(): everything = jax.tree.map(lambda part: lax.all_gather(part, axis), x)]
    all_to_all x0 -> x2, blocking collectives: none -> 75.1 us  [the longest x1 51.9 us: on_device(): got = lax.all_to_all(pieces, 'ctx', split_axis=0, concat_axis=0, tiled=True)]
    unnamed x1 -> x0, blocking collectives: 61.7 us -> none
    select_n x37 -> x0, other arithmetic: 50.2 us -> none  [the longest x32 46.8 us: step(): return jax.tree.map(lambda a, b: jnp.where(reached, a, b), new, before)]
    all_to_all x4 -> x0, waiting for transfers between devices: 46.3 us -> none  [the longest x1 46.3 us: on_device(): lax.all_to_all(finals, 'ctx', split_axis=1, concat_axis=0, tiled=True)]
    gather x16 -> x0, local copies, waits for them, and re-layouts: 28.8 us -> none  [the longest x2 4.66 us: on_device(): tail_x = jnp.where(tail_inside, ext_x[tail_rows], zero_value)]
    reshape x9 -> x0, local copies, waits for them, and re-layouts: 28.4 us -> none  [the longest x2 16.9 us: on_device(): (inner + inter).reshape(tok_count, inner_width)]
    all_to_all x4 -> x0, starting transfers between devices: 27.9 us -> none  [the longest x1 11 us: on_device(): lax.all_to_all(send_tail, 'ctx', split_axis=1, concat_axis=0, tiled=True)]
  transfers between devices with their start and end apart: 8 -> 5, of which waited for: 2 -> 1; matrix products, arithmetic and copies ran while one was open for 38% -> 4% of each run, Pallas kernels for 0% -> 10%
where the time goes in v1:
time: 142 us; the launch traced here: 140 us
  blocking collectives  75.1 us (53%)
  Pallas kernels  27.8 us (20%)
  starting transfers between devices  17 us (12%)
  waiting for transfers between devices  12.7 us (9%)
  local copies, waits for them, and re-layouts  6.73 us (5%)
    all_to_all x1, blocking collectives, on_device(): got = lax.all_to_all(pieces, 'ctx', split_axis=0, concat_axis=0, tiled=True)  51.9 us
    all_to_all x1, blocking collectives, on_device(): own = lax.all_to_all(back, 'ctx', split_axis=0, concat_axis=0, tiled=True)  23.1 us
    ppermute x4, starting transfers between devices, shift_in(): lax.ppermute(block, 'ctx', [(i, i + distance) for i in range(count - dist...  13.3 us
    ppermute x4, waiting for transfers between devices, shift_in(): lax.ppermute(block, 'ctx', [(i, i + distance) for i in range(count - dist...  12.7 us
    pallas_call x1, Pallas kernels, on_device(): call(stage_a, (STEPS,), [smem, smem, pl.BlockSpec((TOK, SW), lambda s: (0...  11.1 us
    pallas_call x1, Pallas kernels, on_device(): call(stage_c, (GROUPS, NC), [pl.BlockSpec((STRETCH, GWIDTH), by_cg), pl.B...  8.5 us
    pallas_call x1, Pallas kernels, on_device(): call(stage_b, (NC,), [pl.BlockSpec((STRETCH, WIDTH), lambda c: (c, 0)), p...  4.88 us
    ppermute x1, starting transfers between devices, on_device(): swapped = lax.ppermute(own, 'side', [(0, 1), (1, 0)])  3.67 us
  transfers between devices with their start and end apart: 5, of which 1 were waited for; matrix products, arithmetic and copies ran while one was open for 4% of the time, Pallas kernels for 10%

profile of v1, /device:TPU:1, one launch (start us, length us, event | category | flops | bytes accessed | tf_op | source)
XLA Modules:
  0.0 140.1 jit_solution(18316978477663880222)
XLA Ops:
  0.6 0.0 copy-start.3
  0.6 0.0 copy-start.8
  0.7 0.0 copy-start.7
  0.7 0.0 copy-start.6
  0.7 0.0 copy-start.5
  0.7 0.8 slice.14
  1.5 0.8 slice_bitcast_fusion
  2.3 4.0 %collective-permute-start = (bf16[16,2560]{1,0:T(8,128)(2,1)S(1)}, bf16[16,2560]{1,0:T(8,128)(2,1)S(1)}, u32[]{:S(2)}, u32[]{:S(2)}) collective-permute-start(bf16[16,2560]{1,0:T(8,128)(2,1)S(1)} %pad_maximum_fusion), channel_id=1, source_target_pairs={{0,8},{8,16},{16,24},{24,32},{32,40},{40,48},{48,56},{56,64},{64,7... | collective-permute-start | bytes 245768 | tf_op jit(solution)/shard_map/ppermute | solution.py:40
  6.4 0.7 tile.25
  7.0 0.1 reshape_tile.6.al_ref
  7.1 0.7 tile.26
  7.8 0.1 reshape_tile.7.db_ref
  7.8 0.9 tile.11
  8.7 0.1 copy.19.dt_ref
  8.8 1.1 copy.21
  10.0 0.0 collective-permute-done.xh_ref.bch_ref
  10.0 0.0 copy-done.3
  10.0 0.0 copy-done.8
  10.0 0.0 copy-done.7
  10.0 0.0 copy-done.6
  10.0 0.0 copy-done.5
  10.0 11.1 %shard_map.165 = (bf16[32,208,128]{2,1,0:T(8,128)(2,1)S(1)}, bf16[128,2048]{1,0:T(8,128)(2,1)}, f32[8,2048]{1,0:T(8,128)S(1)}, f32[8,2048]{1,0:T(8,128)S(1)}, bf...) custom-call(s32[1]{0:T(128)} %bitcast.idx_ref, ...), custom_call_target="tpu_custom_call" | custom-call | flops 2000000000 | bytes 10485760 | tf_op jit(solution)/shard_map/pallas_call | solution.py:410
  21.1 0.0 copy-start.4
  21.1 51.9 %all_to_all.10.got_ref = bf16[32,208,128]{2,1,0:T(8,128)(2,1)S(1)} all-to-all(bf16[32,208,128]{2,1,0:T(8,128)(2,1)S(1)} %get-tuple-element.26), channel_id=1, replica_groups=mesh['ctx'=32,'head'=4,'side'=2] {'ctx'}, dimensions={0} | all-to-all | bytes 3407872 | tf_op jit(solution)/shard_map/all_to_all | solution.py:456
  73.1 0.0 copy-done.4
  73.1 0.0 copy-start.9
  73.1 0.0 copy-start
  73.1 1.1 shard_map.168
  74.1 23.1 %all_to_all.11 = bf16[32,80,128]{2,1,0:T(8,128)(2,1)} all-to-all(bf16[32,80,128]{2,1,0:T(8,128)(2,1)S(1)} %shard_map.168), channel_id=1, replica_groups=mesh['ctx'=32,'head'=4,'side'=2] {'ctx'}, dimensions={0} | all-to-all | bytes 1310720 | tf_op jit(solution)/shard_map/all_to_all | solution.py:485
  97.3 3.7 %collective-permute-start.4 = (bf16[32,80,128]{2,1,0:T(8,128)(2,1)}, bf16[32,80,128]{2,1,0:T(8,128)(2,1)}, u32[]{:S(2)}, u32[]{:S(2)}) collective-permute-start(bf16[32,80,128]{2,1,0:T(8,128)(2,1)} %all_to_all.11), channel_id=1, source_target_pairs={{0,1},{1,0},{2,3},{3,2},{4,5},{5,4},{6,7},{7,6},{8,9},{9,8},{10,11... | collective-permute-start | bytes 1966088 | tf_op jit(solution)/shard_map/ppermute | solution.py:511
  101.0 5.0 %collective-permute-start.2 = (bf16[128,2048]{1,0:T(8,128)(2,1)}, bf16[128,2048]{1,0:T(8,128)(2,1)}, u32[]{:S(2)}, u32[]{:S(2)}) collective-permute-start(bf16[128,2048]{1,0:T(8,128)(2,1)} %get-tuple-element.23), channel_id=1, source_target_pairs={{0,16},{8,24},{16,32},{24,40},{32,48},{40,56},{48,64},{56,72},{64,... | collective-permute-start | bytes 1572872 | tf_op jit(solution)/shard_map/ppermute | solution.py:40
  105.9 3.0 %collective-permute-start.1 = (bf16[128,2048]{1,0:T(8,128)(2,1)}, bf16[128,2048]{1,0:T(8,128)(2,1)}, u32[]{:S(2)}, u32[]{:S(2)}) collective-permute-start(bf16[128,2048]{1,0:T(8,128)(2,1)} %get-tuple-element.23), channel_id=1, source_target_pairs={{0,8},{8,16},{16,24},{24,32},{32,40},{40,48},{48,56},{56,64},{64,7... | collective-permute-start | bytes 1572872 | tf_op jit(solution)/shard_map/ppermute | solution.py:40
  109.0 0.0 copy-done.9
  109.0 0.7 broadcast_in_dim.15
  109.6 0.8 reshape_reshape.3.skip_ref
  110.4 1.3 collective-permute-start.3
  111.7 0.0 copy-done
  111.7 0.0 copy-start.1
  111.7 0.0 copy-start.2
  111.8 4.9 %shard_map.166.y_ref = f32[512,2048]{1,0:T(8,128)} custom-call(bf16[512,2048]{1,0:T(8,128)(2,1)S(1)} %copy-done, bf16[512,512]{1,0:T(8,128)(2,1)S(1)} %get-tuple-element.18.bcc_ref.c_ref, f32[512,128]{1,0:T(8,128)S(1)} %get-tuple-element.19.cum_ref, f32[512,128]{1,0:T(8,128)S(1)} %get-tuple-element.20.step_ref, s32[512,128]{1,0:T(8,128)S(1)} %get-tuple-element.21.fl_ref, ...), custom_call_target="tpu_custom_call" | custom-call | flops 1000000000 | bytes 20971520 | tf_op jit(solution)/shard_map/pallas_call | solution.py:461
  116.6 12.7 %collective-permute-done.3.d1_ref = f32[8,2048]{1,0:T(8,128)S(1)} collective-permute-done((f32[8,2048]{1,0:T(8,128)S(1)}, f32[8,2048]{1,0:T(8,128)S(1)}, u32[]{:S(2)}, u32[]{:S(2)}) %collective-permute-start.3) | collective-permute-done | bytes 65568 | tf_op jit(solution)/shard_map/ppermute | solution.py:40
  129.3 0.0 collective-permute-done.2.s2_ref
  129.3 0.0 collective-permute-done.1.s1_ref
  129.3 0.0 copy-done.1
  129.3 0.0 copy-done.2
  129.4 8.5 %shard_map.167 = bf16[512,2048]{1,0:T(8,128)(2,1)} custom-call(f32[512,2048]{1,0:T(8,128)} %shard_map.166.y_ref, bf16[512,2048]{1,0:T(8,128)(2,1)S(1)} %bitcast.19, bf16[512,512]{1,0:T(8,128)(2,1)S(1)} %get-tuple-element.18.bcc_ref.c_ref, bf16[4,128,2048]{2,1,0:T(8,128)(2,1)} %get-tuple-element.22.ent_ref, bf16[128,2048]{1,0:T(8,128)(2,1)} %collective-permute-done.1.s1_ref, ...), custom_call_target="tpu_custom_call" | custom-call | flops 1000000000 | bytes 15728640 | tf_op jit(solution)/shard_map/pallas_call | solution.py:490
  137.8 0.0 collective-permute-done.4.got_ref
  137.9 2.3 %shard_map.169 = (f32[32,64,128]{2,1,0:T(8,128)}, bf16[3,2048]{1,0:T(4,128)(2,1)}, bf16[3,2,256]{2,1,0:T(2,128)(2,1)}) custom-call(bf16[32,80,128]{2,1,0:T(8,128)(2,1)} %collective-permute-done.4.got_ref), custom_call_target="tpu_custom_call" | custom-call | flops 10000000 | bytes 3145728 | tf_op jit(solution)/shard_map/pallas_call | solution.py:512
  (2 shorter events, 0.0 us)
Async XLA Ops:
  0.6 9.4 %copy-start.3 = (s32[1,32]{1,0:T(1,128)S(1)}, s32[1,32]{1,0:T(1,128)}, u32[]{:S(2)}) copy-start(s32[1,32]{1,0:T(1,128)} %len_ref.3) | copy-start | bytes 388
  0.6 9.4 %copy-start.8 = (f32[2,256]{1,0:T(2,128)S(1)}, f32[2,256]{1,0:T(2,128)}, u32[]{:S(2)}) copy-start(f32[2,256]{1,0:T(2,128)} %bbc_ref.1) | copy-start | bytes 6148
  0.7 9.4 %copy-start.7 = (f32[4,2,256]{2,1,0:T(2,128)S(1)}, f32[4,2,256]{2,1,0:T(2,128)}, u32[]{:S(2)}) copy-start(f32[4,2,256]{2,1,0:T(2,128)} %wbc_ref.1) | copy-start | bytes 24580
  0.7 9.4 %copy-start.6 = (f32[2048]{0:T(1024)S(1)}, f32[2048]{0:T(1024)}, u32[]{:S(2)}) copy-start(f32[2048]{0:T(1024)} %param.19) | copy-start | bytes 24580
  0.7 9.4 %copy-start.5 = (f32[4,2048]{1,0:T(4,128)S(1)}, f32[4,2048]{1,0:T(4,128)}, u32[]{:S(2)}) copy-start(f32[4,2048]{1,0:T(4,128)} %wx_ref.1) | copy-start | bytes 98308
  2.3 7.7 %collective-permute-start = (bf16[16,2560]{1,0:T(8,128)(2,1)S(1)}, bf16[16,2560]{1,0:T(8,128)(2,1)S(1)}, u32[]{:S(2)}, u32[]{:S(2)}) collective-permute-start(bf16[16,2560]{1,0:T(8,128)(2,1)S(1)} %pad_maximum_fusion), channel_id=1, source_target_pairs={{0,8},{8,16},{16,24},{24,32},{32,40},{40,48},{48,56},{56,64},{64,7... | collective-permute-start | bytes 245768 | tf_op jit(solution)/shard_map/ppermute | solution.py:40
  21.1 51.9 %copy-start.4 = (s32[1,32]{1,0:T(1,128)S(1)}, s32[1,32]{1,0:T(1,128)}, u32[]{:S(2)}) copy-start(s32[1,32]{1,0:T(1,128)} %owner_ref.1) | copy-start | bytes 388
  73.1 35.9 %copy-start.9 = (f32[32]{0:T(128)S(1)}, f32[32]{0:T(128)}, u32[]{:S(2)}) copy-start(f32[32]{0:T(128)} %param.24) | copy-start | bytes 388
  73.1 38.7 %copy-start = (bf16[512,2048]{1,0:T(8,128)(2,1)S(1)}, bf16[512,2048]{1,0:T(8,128)(2,1)}, u32[]{:S(2)}) copy-start(bf16[512,2048]{1,0:T(8,128)(2,1)} %get-tuple-element.17.xc_ref) | copy-start | bytes 6291460
  97.3 40.6 %collective-permute-start.4 = (bf16[32,80,128]{2,1,0:T(8,128)(2,1)}, bf16[32,80,128]{2,1,0:T(8,128)(2,1)}, u32[]{:S(2)}, u32[]{:S(2)}) collective-permute-start(bf16[32,80,128]{2,1,0:T(8,128)(2,1)} %all_to_all.11), channel_id=1, source_target_pairs={{0,1},{1,0},{2,3},{3,2},{4,5},{5,4},{6,7},{7,6},{8,9},{9,8},{10,11... | collective-permute-start | bytes 1966088 | tf_op jit(solution)/shard_map/ppermute | solution.py:511
  101.0 28.4 %collective-permute-start.2 = (bf16[128,2048]{1,0:T(8,128)(2,1)}, bf16[128,2048]{1,0:T(8,128)(2,1)}, u32[]{:S(2)}, u32[]{:S(2)}) collective-permute-start(bf16[128,2048]{1,0:T(8,128)(2,1)} %get-tuple-element.23), channel_id=1, source_target_pairs={{0,16},{8,24},{16,32},{24,40},{32,48},{40,56},{48,64},{56,72},{64,... | collective-permute-start | bytes 1572872 | tf_op jit(solution)/shard_map/ppermute | solution.py:40
  105.9 23.4 %collective-permute-start.1 = (bf16[128,2048]{1,0:T(8,128)(2,1)}, bf16[128,2048]{1,0:T(8,128)(2,1)}, u32[]{:S(2)}, u32[]{:S(2)}) collective-permute-start(bf16[128,2048]{1,0:T(8,128)(2,1)} %get-tuple-element.23), channel_id=1, source_target_pairs={{0,8},{8,16},{16,24},{24,32},{32,40},{40,48},{48,56},{56,64},{64,7... | collective-permute-start | bytes 1572872 | tf_op jit(solution)/shard_map/ppermute | solution.py:40
  110.4 18.9 %collective-permute-start.3 = (f32[8,2048]{1,0:T(8,128)S(1)}, f32[8,2048]{1,0:T(8,128)S(1)}, u32[]{:S(2)}, u32[]{:S(2)}) collective-permute-start(f32[8,2048]{1,0:T(8,128)S(1)} %get-tuple-element.24), channel_id=1, source_target_pairs={{0,8},{8,16},{16,24},{24,32},{32,40},{40,48},{48,56},{56,64},{64,7... | collective-permute-start | bytes 196616 | tf_op jit(solution)/shard_map/ppermute | solution.py:40
  111.7 17.6 %copy-start.1 = (bf16[1,512,2048]{2,1,0:T(8,128)(2,1)S(1)}, bf16[1,512,2048]{2,1,0:T(8,128)(2,1)}, u32[]{:S(2)}) copy-start(bf16[1,512,2048]{2,1,0:T(8,128)(2,1)} %param.16) | copy-start | bytes 6291460
  111.7 17.6 %copy-start.2 = (f32[2048]{0:T(1024)S(1)}, f32[2048]{0:T(1024)}, u32[]{:S(2)}) copy-start(f32[2048]{0:T(1024)} %param.25) | copy-start | bytes 24580

commit v2 on v1

v2 whole, which is shorter than its diff:
```python
import jax
import jax.numpy as jnp
from jax import lax
from jax.experimental import pallas as pl
from jax.experimental.pallas import tpu as pltpu
from jax.sharding import PartitionSpec as P

HEAD_DIM = 64
STATE = 128
STRETCH = 128
LANES = 128
HALO = 16
KW = 4
EPS = 1e-05
BF = jnp.bfloat16
F32 = jnp.float32
I32 = jnp.int32
LARGE = 60 * 1024 * 1024
SMALL = 16 * 1024 * 1024

TOK = 512
NC = TOK // STRETCH
WIDTH = 2048
HEADS = WIDTH // HEAD_DIM
GROUPS = 2
GWIDTH = WIDTH // GROUPS
BCW = 512
REQS = 32
STEPS = 4
SW = WIDTH // STEPS
SLT = SW // LANES
PIECE = 2 * 64 + 16
BACK = 64 + 16


def shift_in(block, distance):
    count = lax.axis_size("ctx")
    return lax.ppermute(block, "ctx", [(i, i + distance) for i in range(count - distance)])


def swish(v):
    half = 0.5 * v
    return half + half * jnp.tanh(half)


def split3(v, lane):
    hi = v.astype(BF).astype(F32)
    rest = v - hi
    mid = rest.astype(BF).astype(F32)
    low = rest - mid
    return jnp.where(
        lane < HEADS, hi, jnp.where(lane < 2 * HEADS, mid, jnp.where(lane < 3 * HEADS, low, 0.0))
    ).astype(BF)


def spread_matrix(first_head, width):
    row = lax.broadcasted_iota(I32, (LANES, width), 0)
    col = lax.broadcasted_iota(I32, (LANES, width), 1)
    same = ((row & (HEADS - 1)) == (col >> 6) + first_head) & (row < 3 * HEADS)
    return jnp.where(same, 1.0, 0.0).astype(BF)


def conv_tile(ext, taps, bias, masks):
    acc = bias + taps[KW - 1] * ext[HALO:]
    for d in range(1, KW):
        acc = acc + taps[KW - 1 - d] * (pltpu.roll(ext, d, 0)[HALO:] * masks[d - 1])
    return swish(acc)


def scan_lengths(idx_ref, len_ref, first_scr=None):
    zero = jnp.int32(0)

    def scan(r, carry):
        first, count, behind, e0, f0, e1, f1, fa = carry
        last = first + len_ref[0, r] - 1
        if first_scr is not None:
            first_scr[r] = first
        ends = (last >= 0) & (last < TOK)
        take0, take1 = ends & (count == 0), ends & (count == 1)
        points = [c * STRETCH + STRETCH - 1 for c in range(NC)]
        fa = tuple(
            jnp.where((first <= p) & (last >= p), first, old) for p, old in zip(points, fa)
        )
        return (
            last + 1,
            count + jnp.where(ends, 1, 0),
            behind + jnp.where((last >= -TOK) & (last < 0), 1, 0),
            jnp.where(take0, last, e0),
            jnp.where(take0, first, f0),
            jnp.where(take1, last, e1),
            jnp.where(take1, first, f1),
            fa,
        )

    start = -idx_ref[0] * TOK
    out = lax.fori_loop(
        0, REQS, scan, (start, zero, zero, zero, zero, zero, zero, (zero,) * NC), unroll=4
    )
    return out[1:]


def stretch_gains(cum_ref, fa):
    through = []
    gains = [jnp.ones((1, LANES), F32)]
    for c in range(NC):
        end = cum_ref[(c + 1) * STRETCH - 1 : (c + 1) * STRETCH, :]
        through.append(jnp.where(fa[c] < c * STRETCH, jnp.exp(end), 0.0))
        gains.append(gains[-1] * through[-1])
    return through, gains


def as_rows(values):
    row16 = lax.broadcasted_iota(I32, (16, LANES), 0)
    block = jnp.zeros((16, LANES), F32)
    for i, v in enumerate(values):
        block = jnp.where(row16 == i, v, block)
    return block


def stage_p(
    idx_ref, len_ref, dt_ref, al_ref, db_ref, cum_ref, step_ref, fl_ref, wst_ref, first_scr
):
    lane = lax.broadcasted_iota(I32, (STRETCH, LANES), 1)
    row = lax.broadcasted_iota(I32, (STRETCH, LANES), 0)
    fa = scan_lengths(idx_ref, len_ref, first_scr)[-1]
    start = -idx_ref[0] * TOK
    coef = -jnp.exp(jnp.concatenate([al_ref[...]] * 4, axis=1))
    bias = jnp.concatenate([db_ref[...]] * 4, axis=1)
    lower = jnp.where(row >= lane, 1.0, 0.0)
    for c in range(NC):
        rows = slice(c * STRETCH, (c + 1) * STRETCH)
        here = row + c * STRETCH

        def later(r, fl):
            return jnp.where(here >= first_scr[r], first_scr[r], fl)

        fl_ref[rows, :] = lax.fori_loop(
            0, REQS, later, jnp.full((STRETCH, LANES), start, I32), unroll=4
        )
        raw = jnp.concatenate([dt_ref[:, rows]] * 4, axis=0).T + bias
        step = jnp.maximum(raw, 0.0) + jnp.log1p(jnp.exp(-jnp.abs(raw)))
        step_ref[rows, :] = step
        cum = jnp.dot(
            lower, coef * step, precision=lax.Precision.HIGHEST, preferred_element_type=F32
        )
        cum_ref[rows, :] = cum
        w = jnp.exp(cum[STRETCH - 1 :, :] - cum) * step
        wst_ref[rows, :] = split3(jnp.where(here >= fa[c], w, 0.0), lane)
    through, gains = stretch_gains(cum_ref, fa)
    lane16 = lax.broadcasted_iota(I32, (16, LANES), 1)
    wst_ref[NC * STRETCH :, :] = split3(as_rows(through + gains), lane16)


def stage_a(
    x_ref, xh_ref, bc_ref, bch_ref, wx_ref, bx_ref, wbc_ref, bbc_ref, fl_ref, wst_ref,
    xc_ref, bcc_ref, ent_ref, s_ref, entry_ref,
    mask_scr, spread_scr, bt_scr,
):
    s = pl.program_id(0)
    row = lax.broadcasted_iota(I32, (STRETCH, LANES), 0)

    @pl.when(s == 0)
    def _():
        for c in range(NC):
            rows = slice(c * STRETCH, (c + 1) * STRETCH)
            since = row + c * STRETCH - fl_ref[rows, :]
            for d in range(1, KW):
                mask_scr[d - 1, rows, :] = jnp.where(since >= d, 1.0, 0.0)
        for part in range(2):
            for g in range(GROUPS):
                at = slice((part * GROUPS + g) * LANES, (part * GROUPS + g + 1) * LANES)
                own = slice(g * LANES, (g + 1) * LANES)
                taps = [wbc_ref[k, part : part + 1, own] for k in range(KW)]
                off = bbc_ref[part : part + 1, own]
                for c in range(NC):
                    if c == 0:
                        ext = jnp.concatenate([bch_ref[:, at], bc_ref[0:STRETCH, at]], axis=0)
                    else:
                        ext = bc_ref[c * STRETCH - HALO : (c + 1) * STRETCH, at]
                    rows = slice(c * STRETCH, (c + 1) * STRETCH)
                    masks = [mask_scr[d, rows, :] for d in range(KW - 1)]
                    out = conv_tile(ext.astype(F32), taps, off, masks).astype(BF)
                    bcc_ref[rows, at] = out
                    if part == 0:
                        bt_scr[g * NC + c] = out.astype(F32).T.astype(BF)

    spread_scr[...] = jnp.dot(
        wst_ref[...], spread_matrix(s * (SW // HEAD_DIM), SW), preferred_element_type=F32
    )
    ex = NC * STRETCH
    group = s // (STEPS // GROUPS)
    entry_ref[...] = spread_scr[ex:, :]
    entering = None
    for c in range(NC):
        rows = slice(c * STRETCH, (c + 1) * STRETCH)
        masks = [mask_scr[d, rows, :] for d in range(KW - 1)]
        scaled = []
        for t in range(SLT):
            at = slice(t * LANES, (t + 1) * LANES)
            if c == 0:
                ext = jnp.concatenate([xh_ref[:, at], x_ref[0:STRETCH, at]], axis=0)
            else:
                ext = x_ref[c * STRETCH - HALO : (c + 1) * STRETCH, at]
            taps = [wx_ref[k : k + 1, at] for k in range(KW)]
            out = conv_tile(ext.astype(F32), taps, bx_ref[:, at], masks).astype(BF)
            xc_ref[rows, at] = out
            scaled.append((out.astype(F32) * spread_scr[rows, at]).astype(BF))
        local = jnp.dot(
            bt_scr[group * NC + c], jnp.concatenate(scaled, axis=1), preferred_element_type=F32
        )
        if c == 0:
            ent_ref[0] = jnp.zeros((STATE, SW), BF)
            entering = local
        else:
            ent_ref[c] = entering.astype(BF)
            entering = spread_scr[ex + c : ex + c + 1, :] * entering + local
    s_ref[...] = entering.astype(BF)


def stage_e(
    idx_ref, len_ref, x_ref, xh_ref, bc_ref, bch_ref, xc_ref, bcc_ref, cum_ref, step_ref, ent_ref,
    s_ref,
    piece_ref, gain_ref,
    wst_scr, spread_scr, sc_scr,
):
    s = pl.program_id(0)
    lane = lax.broadcasted_iota(I32, (STRETCH, LANES), 1)
    row = lax.broadcasted_iota(I32, (STRETCH, LANES), 0)
    ex = 2 * STRETCH

    @pl.when(s == 0)
    def _():
        count, behind, e0, f0, e1, f1, fa = scan_lengths(idx_ref, len_ref)
        sc_scr[0], sc_scr[1], sc_scr[2], sc_scr[3], sc_scr[4] = e0, f0, e1, f1, count
        inflow = []
        for k, (e, f) in enumerate(((e0, f0), (e1, f1))):
            base = pl.multiple_of((e >> 7) * STRETCH, STRETCH)
            here = row + base
            end = cum_ref[pl.ds(e, 1), :]
            w = jnp.exp(end - cum_ref[pl.ds(base, STRETCH), :]) * step_ref[pl.ds(base, STRETCH), :]
            w = jnp.where((here >= f) & (here <= e), w, 0.0)
            wst_scr[k * STRETCH : (k + 1) * STRETCH, :] = split3(w, lane)
            inflow.append(jnp.where(f < base, jnp.exp(end), 0.0))
        _, gains = stretch_gains(cum_ref, fa)
        gain = gains[0]
        for c in range(1, NC):
            gain = jnp.where((e0 >> 7) == c, gains[c], gain)
        gain = gain * inflow[0]
        by_owner = jnp.where((count > 0) & (behind == 0), gain, 0.0)
        by_sender = jnp.where(count == 0, gains[NC], jnp.where(behind == 0, 0.0, gain))
        lane16 = lax.broadcasted_iota(I32, (16, LANES), 1)
        wst_scr[ex:, :] = split3(as_rows(inflow + [by_owner, by_sender]), lane16)

    e0, f0, e1, f1 = sc_scr[0], sc_scr[1], sc_scr[2], sc_scr[3]
    spread_scr[...] = jnp.dot(
        wst_scr[...], spread_matrix(s * (SW // HEAD_DIM), SW), preferred_element_type=F32
    )
    gain_ref[...] = jnp.broadcast_to(spread_scr[ex + 3 : ex + 4, :], (8, SW))
    group = s // (STEPS // GROUPS)
    for k, e in enumerate((e0, e1)):
        c = e >> 7
        base = pl.multiple_of(c * STRETCH, STRETCH)
        at = k * STRETCH
        scaled = (
            xc_ref[pl.ds(base, STRETCH), :].astype(F32) * spread_scr[at : at + STRETCH, :]
        ).astype(BF)
        b = jnp.where(
            group == 0,
            bcc_ref[pl.ds(base, STRETCH), 0:LANES].astype(F32),
            bcc_ref[pl.ds(base, STRETCH), LANES : 2 * LANES].astype(F32),
        )
        final = spread_scr[ex + k : ex + k + 1, :] * ent_ref[c].astype(F32) + jnp.dot(
            b.T.astype(BF), scaled, preferred_element_type=F32
        )
        if k == 0:
            final = jnp.where(sc_scr[4] == 0, s_ref[...].astype(F32), final)
        final = final.astype(BF)
        for j in range(2 * SLT):
            piece_ref[j, k * 64 : k * 64 + 64, :] = final[
                (j % 2) * 64 : (j % 2) * 64 + 64, (j // 2) * LANES : (j // 2 + 1) * LANES
            ]

    tails_x, tails_bc = [], []
    pick_row = lax.broadcasted_iota(I32, (16, 2 * HALO), 0)
    pick_col = lax.broadcasted_iota(I32, (16, 2 * HALO), 1)
    for e, f in ((e0, f0), (e1, f1)):
        base = pl.multiple_of((e >> 4) * HALO, HALO)
        before = pl.multiple_of(jnp.maximum(base - HALO, 0), HALO)
        source = e - (KW - 2) + pick_row
        pick = (pick_col + base - HALO == source) & (source >= f) & (pick_row < KW - 1)
        pick = jnp.where(pick, 1.0, 0.0).astype(BF)

        def tail(ref, halo_ref):
            head = jnp.where(base > 0, ref[pl.ds(before, HALO), :], halo_ref[...])
            window = jnp.concatenate([head, ref[pl.ds(base, HALO), :]], axis=0)
            return jnp.dot(pick, window, preferred_element_type=F32)

        tails_x.append(tail(x_ref, xh_ref))
        tails_bc.append(tail(bc_ref, bch_ref))
    row16 = lax.broadcasted_iota(I32, (16, LANES), 0)
    for t in range(SLT):
        at = slice(t * LANES, (t + 1) * LANES)
        gain = spread_scr[ex + 2 : ex + 3, at]
        gain_hi = gain.astype(BF).astype(F32)
        bc_rows = []
        for k in range(2):
            one = tails_bc[k][:, at]
            bc_rows.append(jnp.sum(jnp.where(row16 == s, one, 0.0), axis=0, keepdims=True))
        for half in range(2):
            values = [gain_hi, gain - gain_hi]
            for k in range(2):
                one = tails_x[k][:, at]
                values += [one[0:1], one[1:2]] if half == 0 else [one[2:3], bc_rows[k]]
            piece_ref[2 * t + half, 128:144, :] = as_rows(values).astype(BF)


def stage_b(xc_ref, bcc_ref, cum_ref, step_ref, fl_ref, skip_ref, y_ref):
    c = pl.program_id(0)
    row = lax.broadcasted_iota(I32, (STRETCH, LANES), 0)
    lane = lax.broadcasted_iota(I32, (STRETCH, LANES), 1)
    keep = (lane <= row) & (lane + c * STRETCH >= fl_ref[...])
    cum = cum_ref[...]
    cum_t = cum.T
    step_t = step_ref[...].T
    low = lax.broadcasted_iota(I32, (STRETCH, LANES), 1) < HEAD_DIM
    for g in range(GROUPS):
        b = bcc_ref[:, g * LANES : (g + 1) * LANES]
        cc = bcc_ref[:, (GROUPS + g) * LANES : (GROUPS + g + 1) * LANES]
        scores = lax.dot_general(cc, b, (((1,), (1,)), ((), ())), preferred_element_type=F32)
        for i in range(HEADS // GROUPS // 2):
            pair = g * (HEADS // GROUPS // 2) + i
            weights = []
            for h in (2 * pair, 2 * pair + 1):
                decay = jnp.exp(jnp.where(keep, cum[:, h : h + 1] - cum_t[h : h + 1, :], -jnp.inf))
                weights.append((scores * (decay * step_t[h : h + 1, :])).astype(BF))
            at = slice(pair * LANES, (pair + 1) * LANES)
            x = xc_ref[:, at]
            xf = x.astype(F32)
            both = jnp.concatenate(
                [jnp.where(low, xf, 0.0).astype(BF), jnp.where(low, 0.0, xf).astype(BF)], axis=0
            )
            inner = jnp.dot(
                jnp.concatenate(weights, axis=1), both, preferred_element_type=F32
            )
            y_ref[:, at] = inner + skip_ref[:, at] * xf


def stage_c(
    y_ref, z_ref, c_ref, ent_ref, s1_ref, s2_ref, entry_ref, cum_ref, fl_ref, gain_ref, out_ref
):
    g, c = pl.program_id(0), pl.program_id(1)
    lane = lax.broadcasted_iota(I32, (STRETCH, LANES), 1)
    inflow = jnp.where(fl_ref[...] < c * STRETCH, jnp.exp(cum_ref[...]), 0.0)
    wide = jnp.dot(
        split3(inflow, lane),
        spread_matrix(g * (HEADS // GROUPS), GWIDTH),
        preferred_element_type=F32,
    )
    incoming = s1_ref[...].astype(F32) + s2_ref[...].astype(F32)
    entering = ent_ref[0].astype(F32) + entry_ref[pl.ds(NC + c, 1), :] * incoming
    carried = jnp.dot(c_ref[...], entering.astype(BF), preferred_element_type=F32)
    gated = (y_ref[...] + wide * carried) * swish(z_ref[...].astype(F32))
    mean = jnp.sum(gated * gated, axis=1, keepdims=True) * (1.0 / GWIDTH)
    out_ref[...] = (gated * lax.rsqrt(mean + EPS) * gain_ref[...]).astype(BF)


def add_incoming(piece_ref, s1_ref, gain_ref, out_ref):
    for j in range(out_ref.shape[0]):
        at = slice((j // 2) * LANES, (j // 2 + 1) * LANES)
        came = s1_ref[(j % 2) * 64 : (j % 2) * 64 + 64, at].astype(F32)
        out_ref[j] = (piece_ref[j].astype(F32) + gain_ref[0:1, at] * came).astype(BF)


def pass_on(s1_ref, entry_ref, out_ref):
    out_ref[...] = (entry_ref[8:9, :] * s1_ref[...].astype(F32)).astype(BF)


def combine(len_ref, owner_ref, got_ref, out_ref):
    row16 = lax.broadcasted_iota(I32, (16, LANES), 0)

    def one(r, carry):
        first, before = carry
        last = first + len_ref[0, r] - 1
        home = last >> 9
        second = before == home
        h1 = jnp.maximum(home - 1, 0)
        slot = owner_ref[0, r]
        extra = got_ref[home, 128:144, :].astype(F32)
        gain = jnp.where(second, 0.0, extra[0:1] + extra[1:2])
        k = pl.multiple_of(jnp.where(second, 64, 0), 64)
        own = got_ref[home, pl.ds(k, 64), :].astype(F32)
        out_ref[slot, 0:64, :] = (own + gain * got_ref[h1, 0:64, :].astype(F32)).astype(BF)
        tail = jnp.where(second, pltpu.roll(extra, 12, 0), pltpu.roll(extra, 14, 0))
        out_ref[slot, 64:80, :] = jnp.where(row16 < 2, tail, 0.0).astype(BF)
        return last + 1, home

    lax.fori_loop(0, REQS, one, (jnp.int32(0), jnp.int32(-1)), unroll=2)


def finish(got_ref, state_ref, tx_ref, tbc_ref):
    tails = [got_ref[j, 64:80, :].astype(F32) for j in range(REQS)]
    for t in range(WIDTH // LANES):
        at = slice(t * LANES, (t + 1) * LANES)
        block = jnp.concatenate(
            [got_ref[2 * t, 0:64, :], got_ref[2 * t + 1, 0:64, :]], axis=0
        ).astype(F32)
        turned = block.T
        state_ref[2 * t] = turned[0:64]
        state_ref[2 * t + 1] = turned[64:128]
        tx_ref[:, at] = jnp.concatenate([tails[2 * t][0:2], tails[2 * t + 1][0:1]], axis=0).astype(BF)
    for k in range(KW - 1):
        for q in range(4):
            value = tails[2 * (4 * k + q) + 1][1:2].astype(BF)
            tbc_ref[k, q // 2 : q // 2 + 1, (q % 2) * LANES : (q % 2 + 1) * LANES] = value


def call(kernel, grid, ins, outs, scratch=(), flops=0, nbytes=0, aliases=None, limit=None):
    return pl.pallas_call(
        kernel,
        grid=grid,
        in_specs=ins,
        out_specs=[o[1] for o in outs],
        out_shape=[o[0] for o in outs],
        scratch_shapes=list(scratch),
        input_output_aliases=aliases or {},
        compiler_params=pltpu.CompilerParams(vmem_limit_bytes=limit or LARGE),
        cost_estimate=pl.CostEstimate(flops=flops, bytes_accessed=nbytes, transcendentals=0),
    )


def whole(*shape):
    return pl.BlockSpec(shape, lambda *_: (0,) * len(shape))


def on_device(
    x_in, bc_in, z_in, dt_in, conv_x_w, conv_x_b, conv_bc_w, conv_bc_b, a_log, dt_bias, skip_d,
    norm_gain, lengths, owner_slot,
):
    x = x_in[0]
    bc = bc_in[0].reshape(TOK, BCW)
    z = z_in[0]
    index = lax.axis_index("ctx").astype(I32).reshape(1)
    smem = pl.BlockSpec(memory_space=pltpu.SMEM)
    shape = jax.ShapeDtypeStruct
    cols = lambda rows: pl.BlockSpec((rows, SW), lambda s: (0, s))
    ends = bc_in[0, TOK - HALO :].reshape(HALO, BCW)
    halo = shift_in(jnp.concatenate([x[TOK - HALO :], ends], axis=1), 1)
    halo_cols = pl.BlockSpec((HALO, BCW), lambda s: (0, WIDTH // BCW))

    vmem = pl.BlockSpec(memory_space=pltpu.VMEM)
    by_head = shape((TOK, LANES), F32)
    cum, step, fl, wst = call(
        stage_p,
        (),
        [smem, smem, vmem, vmem, vmem],
        [
            (by_head, vmem),
            (by_head, vmem),
            (shape((TOK, LANES), I32), vmem),
            (shape((TOK + 16, LANES), BF), vmem),
        ],
        [pltpu.SMEM((REQS,), I32)],
        flops=10**8,
        nbytes=2**20,
    )(index, lengths, dt_in[0].T, a_log.reshape(1, HEADS), dt_bias.reshape(1, HEADS))

    xc, bcc, ent, left, entry = call(
        stage_a,
        (STEPS,),
        [
            cols(TOK),
            cols(HALO),
            whole(TOK, BCW),
            halo_cols,
            cols(KW),
            cols(1),
            whole(KW, 2, 2 * LANES),
            whole(2, 2 * LANES),
            whole(TOK, LANES),
            whole(TOK + 16, LANES),
        ],
        [
            (shape((TOK, WIDTH), BF), cols(TOK)),
            (shape((TOK, BCW), BF), whole(TOK, BCW)),
            (
                shape((NC, STATE, WIDTH), BF),
                pl.BlockSpec((NC, STATE, SW), lambda s: (0, 0, s)),
            ),
            (shape((STATE, WIDTH), BF), cols(STATE)),
            (shape((16, WIDTH), F32), cols(16)),
        ],
        [
            pltpu.VMEM((KW - 1, TOK, LANES), F32),
            pltpu.VMEM((TOK + 16, SW), F32),
            pltpu.VMEM((GROUPS * NC, STATE, STRETCH), BF),
        ],
        flops=10**9,
        nbytes=10 * 2**20,
    )(
        x, halo, bc, halo, conv_x_w, conv_x_b.reshape(1, WIDTH), conv_bc_w, conv_bc_b, fl, wst
    )

    s1 = shift_in(left, 1)

    pieces, gain = call(
        stage_e,
        (STEPS,),
        [
            smem,
            smem,
            cols(TOK),
            cols(HALO),
            whole(TOK, BCW),
            halo_cols,
            cols(TOK),
            whole(TOK, BCW),
            whole(TOK, LANES),
            whole(TOK, LANES),
            pl.BlockSpec((NC, STATE, SW), lambda s: (0, 0, s)),
            cols(STATE),
        ],
        [
            (
                shape((32, PIECE, LANES), BF),
                pl.BlockSpec((2 * SLT, PIECE, LANES), lambda s: (s, 0, 0)),
            ),
            (shape((8, WIDTH), F32), cols(8)),
        ],
        [
            pltpu.VMEM((2 * STRETCH + 16, LANES), BF),
            pltpu.VMEM((2 * STRETCH + 16, SW), F32),
            pltpu.SMEM((5,), I32),
        ],
        flops=5 * 10**8,
        nbytes=8 * 2**20,
    )(index, lengths, x, halo, bc, halo, xc, bcc, cum, step, ent, left)

    by_row = lambda width: pl.BlockSpec((STRETCH, width), lambda c: (c, 0))
    (y,) = call(
        stage_b,
        (NC,),
        [by_row(WIDTH), by_row(BCW), by_row(LANES), by_row(LANES), by_row(LANES), whole(1, WIDTH)],
        [(shape((TOK, WIDTH), F32), by_row(WIDTH))],
        flops=10**9,
        nbytes=20 * 2**20,
    )(xc, bcc, cum, step, fl, jnp.repeat(skip_d, HEAD_DIM).reshape(1, WIDTH))

    part = pl.BlockSpec((16, 64, LANES), lambda s: (s, 0, 0))
    half = lambda rows: pl.BlockSpec((rows, GWIDTH), lambda s: (0, s))
    (pieces,) = call(
        add_incoming,
        (2,),
        [part, half(STATE), half(8)],
        [(shape((32, PIECE, LANES), BF), part)],
        flops=10**7,
        nbytes=2 * 2**20,
        aliases={0: 0},
    )(pieces, s1, gain)
    got = lax.all_to_all(pieces, "ctx", split_axis=0, concat_axis=0, tiled=True)

    (passed,) = call(
        pass_on,
        (2,),
        [half(STATE), half(16)],
        [(shape((STATE, WIDTH), BF), half(STATE))],
        flops=10**7,
        nbytes=2 * 2**20,
        limit=SMALL,
    )(s1, entry)
    s2 = shift_in(passed, 1)

    got, s2, y = lax.optimization_barrier((got, s2, y))
    (back,) = call(
        combine,
        (),
        [smem, smem, pl.BlockSpec(memory_space=pltpu.VMEM)],
        [(shape((REQS, BACK, LANES), BF), pl.BlockSpec(memory_space=pltpu.VMEM))],
        flops=10**7,
        nbytes=3 * 2**20,
        limit=SMALL,
    )(lengths, owner_slot, got)
    own = lax.all_to_all(back, "ctx", split_axis=0, concat_axis=0, tiled=True)

    back, y = lax.optimization_barrier((back, y))
    by_c = lambda g, c: (c, 0)
    by_g = lambda g, c: (0, g)
    by_cg = lambda g, c: (c, g)
    (mixed,) = call(
        stage_c,
        (GROUPS, NC),
        [
            pl.BlockSpec((STRETCH, GWIDTH), by_cg),
            pl.BlockSpec((STRETCH, GWIDTH), by_cg),
            pl.BlockSpec((STRETCH, LANES), lambda g, c: (c, GROUPS + g)),
            pl.BlockSpec((1, STATE, GWIDTH), lambda g, c: (c, 0, g)),
            pl.BlockSpec((STATE, GWIDTH), by_g),
            pl.BlockSpec((STATE, GWIDTH), by_g),
            pl.BlockSpec((16, GWIDTH), by_g),
            pl.BlockSpec((STRETCH, LANES), by_c),
            pl.BlockSpec((STRETCH, LANES), by_c),
            pl.BlockSpec((1, GWIDTH), by_g),
        ],
        [(shape((TOK, WIDTH), BF), pl.BlockSpec((STRETCH, GWIDTH), by_cg))],
        flops=10**9,
        nbytes=15 * 2**20,
    )(y, z, bcc, ent, s1, s2, entry, cum, fl, norm_gain.reshape(1, WIDTH))

    own, mixed = lax.optimization_barrier((own, mixed))
    swapped = lax.ppermute(own, "side", [(0, 1), (1, 0)])
    state, tail_x, tail_bc = call(
        finish,
        (),
        [pl.BlockSpec(memory_space=pltpu.VMEM)],
        [
            (shape((HEADS, HEAD_DIM, STATE), F32), pl.BlockSpec(memory_space=pltpu.VMEM)),
            (shape((KW - 1, WIDTH), BF), pl.BlockSpec(memory_space=pltpu.VMEM)),
            (shape((KW - 1, 2, 2 * LANES), BF), pl.BlockSpec(memory_space=pltpu.VMEM)),
        ],
        flops=10**7,
        nbytes=3 * 2**20,
        limit=SMALL,
    )(swapped)
    return mixed[None], state[None, None], tail_x[None, None], tail_bc[None, None]


def solution(mesh):
    placed = (
        P("side", "ctx", "head"),
        P("side", "ctx", None, "head"),
        P("side", "ctx", "head"),
        P("side", "ctx", "head"),
        P(None, "head"),
        P("head"),
        P(None, None, "head"),
        P(None, "head"),
        P("head"),
        P("head"),
        P("head"),
        P("head"),
        P("side", None),
        P("side", None),
    )
    return jax.shard_map(
        on_device,
        mesh=mesh,
        in_specs=placed,
        out_specs=(
            P("side", "ctx", "head"),
            P("side", "ctx", "head", None, None),
            P("side", "ctx", None, "head"),
            P("side", "ctx", None, None, "head"),
        ),
        check_vma=False,
    )
```

time: 142 us -> 124 us (0.87)
  blocking collectives: 75.1 us -> 0 us
  starting transfers between devices: 17 us -> 45 us
  waiting for transfers between devices: 12.7 us -> 31.2 us
  Pallas kernels: 27.8 us -> 40.2 us
    all_to_all x2 -> x0, blocking collectives: 75.1 us -> none  [the longest x1 51.9 us: on_device(): got = lax.all_to_all(pieces, 'ctx', split_axis=0, concat_axis=0, tiled=True)]
    all_to_all x0 -> x2, starting transfers between devices: none -> 30.9 us  [the longest x1 18.1 us: on_device(): own = lax.all_to_all(back, 'ctx', split_axis=0, concat_axis=0, tiled=True)]
    all_to_all x0 -> x2, waiting for transfers between devices: none -> 15.1 us  [the longest x1 8.59 us: on_device(): own = lax.all_to_all(back, 'ctx', split_axis=0, concat_axis=0, tiled=True)]
    pallas_call x2 -> x6, Pallas kernels: 16 us -> 28.2 us  [the longest x1 8.48 us: on_device(): call(stage_a, (STEPS,), [cols(TOK), cols(HALO), whole(TOK, BCW), halo_col...]
    ppermute x4 -> x3, starting transfers between devices: 13.3 us -> 10.4 us  [shift_in(): lax.ppermute(block, 'ctx', [(i, i + distance) for i in range(count - dist...]
    another operation x6 -> x0, local copies, waits for them, and re-layouts: 2.47 us -> none  [the longest x2 0.98 us: on_device(): dt = jnp.tile(dt_in[0], (1, 4))]
    unnamed x22 -> x18, local copies, waits for them, and re-layouts: 1.18 us -> 3.43 us
    ppermute x1, waiting for transfers between devices: 0.01 us -> 1.72 us  [on_device(): swapped = lax.ppermute(own, 'side', [(0, 1), (1, 0)])]
  transfers between devices with their start and end apart: 5 -> 6, of which waited for: 1 -> 5; matrix products, arithmetic and copies ran while one was open for 4% -> 2% of each run, Pallas kernels for 10% -> 22%
where the time goes in v2:
time: 124 us; the launch traced here: 123 us
  starting transfers between devices  45 us (36%)
  Pallas kernels  40.2 us (32%)
  waiting for transfers between devices  31.2 us (25%)
  local copies, waits for them, and re-layouts  5.76 us (5%)
    all_to_all x1, starting transfers between devices, on_device(): own = lax.all_to_all(back, 'ctx', split_axis=0, concat_axis=0, tiled=True)  18.1 us
    ppermute x3, waiting for transfers between devices, shift_in(): lax.ppermute(block, 'ctx', [(i, i + distance) for i in range(count - dist...  14.4 us
    all_to_all x1, starting transfers between devices, on_device(): got = lax.all_to_all(pieces, 'ctx', split_axis=0, concat_axis=0, tiled=True)  12.8 us
    ppermute x3, starting transfers between devices, shift_in(): lax.ppermute(block, 'ctx', [(i, i + distance) for i in range(count - dist...  10.4 us
    pallas_call x1, Pallas kernels, on_device(): call(stage_c, (GROUPS, NC), [pl.BlockSpec((STRETCH, GWIDTH), by_cg), pl.B...  8.98 us
    all_to_all x1, waiting for transfers between devices, on_device(): own = lax.all_to_all(back, 'ctx', split_axis=0, concat_axis=0, tiled=True)  8.59 us
    pallas_call x1, Pallas kernels, on_device(): call(stage_a, (STEPS,), [cols(TOK), cols(HALO), whole(TOK, BCW), halo_col...  8.48 us
    pallas_call x1, Pallas kernels, on_device(): call(stage_b, (NC,), [by_row(WIDTH), by_row(BCW), by_row(LANES), by_row(L...  6.66 us
  transfers between devices with their start and end apart: 6, of which 5 were waited for; matrix products, arithmetic and copies ran while one was open for 2% of the time, Pallas kernels for 22%

profile of v2, /device:TPU:1, one launch (start us, length us, event | category | flops | bytes accessed | tf_op | source)
XLA Modules:
  0.0 122.9 jit_solution(12431498938355828712)
XLA Ops:
  0.6 0.8 slice_bitcast_fusion
  1.5 0.7 slice.11
  2.2 4.0 %collective-permute-start = (bf16[16,2560]{1,0:T(8,128)(2,1)S(1)}, bf16[16,2560]{1,0:T(8,128)(2,1)S(1)}, u32[]{:S(2)}, u32[]{:S(2)}) collective-permute-start(bf16[16,2560]{1,0:T(8,128)(2,1)S(1)} %pad_maximum_fusion), channel_id=1, source_target_pairs={{0,8},{8,16},{16,24},{24,32},{32,40},{40,48},{48,56},{56,64},{64,7... | collective-permute-start | bytes 245768 | tf_op jit(solution)/shard_map/ppermute | solution.py:38
  6.3 1.9 %copy.20 = bf16[64,8,2,256]{3,1,2,0:T(8,128)(2,1)} copy(bf16[64,8,2,256]{3,2,1,0:T(2,128)(2,1)} %bitcast.28) | data formatting | bytes 1048576
  8.2 4.2 %shard_map.165 = (f32[512,128]{1,0:T(8,128)}, f32[512,128]{1,0:T(8,128)}, s32[512,128]{1,0:T(8,128)}, bf16[528,128]{1,0:T(8,128)(2,1)}) custom-call(s32[1]{0:T(128)} %bitcast.idx_ref, s32[1,32]{1,0:T(1,128)} %len_ref.5, f32[32,512]{1,0:T(8,128)} %bitcast.33, f32[1,32]{1,0:T(1,128)} %bitcast.37, f32[1,32]{1,0:T(1,128)} %bitcast.38), custom_call_target="tpu_custom_call" | custom-call | flops 100000000 | bytes 1048576 | tf_op jit(solution)/shard_map/pallas_call | solution.py:452
  12.4 0.0 collective-permute-done.xh_ref.bch_ref
  12.4 0.0 copy-start.6
  12.4 0.6 copy-done.6
  13.1 8.5 %shard_map.166 = (bf16[512,2048]{1,0:T(8,128)(2,1)}, bf16[512,512]{1,0:T(8,128)(2,1)}, bf16[4,128,2048]{2,1,0:T(8,128)(2,1)}, bf16[128,2048]{1,0:T(8,128)(2,1)}, f32[16,2048]{1,0:T(8,128)}) custom-call(bf16[512,2048]{1,0:T(8,128)(2,1)} %bitcast.22, bf16[16,2560]{1,0:T(8,128)(2,1)} %copy-done.6, bf16[512,512]{1,0:T(8,128)(2,1)} %bitcast.24, ...), custom_call_target="tpu_custom_call" | custom-call | flops 1000000000 | bytes 10485760 | tf_op jit(solution)/shard_map/pallas_call | solution.py:467
  21.6 3.2 %collective-permute-start.1 = (bf16[128,2048]{1,0:T(8,128)(2,1)}, bf16[128,2048]{1,0:T(8,128)(2,1)S(1)}, u32[]{:S(2)}, u32[]{:S(2)}) collective-permute-start(bf16[128,2048]{1,0:T(8,128)(2,1)} %get-tuple-element.31.s_ref), channel_id=1, source_target_pairs={{0,8},{8,16},{16,24},{24,32},{32,40},{40,48},{48,56},{56,64},{64,7... | collective-permute-start | bytes 1572872 | tf_op jit(solution)/shard_map/ppermute | solution.py:38
  24.8 6.6 %shard_map.167 = (bf16[32,144,128]{2,1,0:T(8,128)(2,1)}, f32[8,2048]{1,0:T(8,128)}) custom-call(s32[1]{0:T(128)} %bitcast.idx_ref, s32[1,32]{1,0:T(1,128)} %len_ref.5, bf16[512,2048]{1,0:T(8,128)(2,1)} %bitcast.23, bf16[16,2560]{1,0:T(8,128)(2,1)} %copy-done.6, bf16[512,512]{1,0:T(8,128)(2,1)} %bitcast.25, bf16[16,2560]{1,0:T(8,128)(2,1)} %copy-done.6, ...), custom_call_target="tpu_custom_call" | custom-call | flops 500000000 | bytes 8388608 | tf_op jit(solution)/shard_map/pallas_call | solution.py:505
  31.4 4.0 %collective-permute-done.1.s1_ref = bf16[128,2048]{1,0:T(8,128)(2,1)S(1)} collective-permute-done((bf16[128,2048]{1,0:T(8,128)(2,1)}, bf16[128,2048]{1,0:T(8,128)(2,1)S(1)}, u32[]{:S(2)}, u32[]{:S(2)}) %collective-permute-start.1) | collective-permute-done | bytes 524320 | tf_op jit(solution)/shard_map/ppermute | solution.py:38
  35.4 0.0 copy-start
  35.4 0.8 copy-done
  36.2 0.0 copy-start.2
  36.2 2.0 %shard_map.168 = bf16[32,144,128]{2,1,0:T(8,128)(2,1)} custom-call(bf16[32,144,128]{2,1,0:T(8,128)(2,1)} %get-tuple-element.32.piece_ref, bf16[128,2048]{1,0:T(8,128)(2,1)} %copy-done, f32[8,2048]{1,0:T(8,128)} %get-tuple-element.33.gain_ref), custom_call_target="tpu_custom_call", output_to_operand_aliasing={{}: (0, {})} | custom-call | flops 10000000 | bytes 2097152 | tf_op jit(solution)/shard_map/pallas_call | solution.py:550
  38.2 0.0 copy-start.1
  38.2 0.0 copy-start.7
  38.2 12.8 %all-to-all-start = ((bf16[32,144,128]{2,1,0:T(8,128)(2,1)}), bf16[32,144,128]{2,1,0:T(8,128)(2,1)S(1)}, u32[]{:S(2)}, u32[]{:S(2)}) async-start(bf16[32,144,128]{2,1,0:T(8,128)(2,1)} %shard_map.168), calls=%async_computation | async-start | bytes 2359296 | tf_op jit(solution)/shard_map/all_to_all | solution.py:559
  51.0 0.0 copy-done.2
  51.0 0.0 copy-done.1
  51.1 0.2 shard_map.169
  51.3 3.2 %collective-permute-start.2 = (bf16[128,2048]{1,0:T(8,128)(2,1)S(1)}, bf16[128,2048]{1,0:T(8,128)(2,1)S(1)}, u32[]{:S(2)}, u32[]{:S(2)}) collective-permute-start(bf16[128,2048]{1,0:T(8,128)(2,1)S(1)} %shard_map.169), channel_id=1, source_target_pairs={{0,8},{8,16},{16,24},{24,32},{32,40},{40,48},{48,56},{56,64},{64,7... | collective-permute-start | bytes 1572872 | tf_op jit(solution)/shard_map/ppermute | solution.py:38
  54.5 0.0 copy-done.7
  54.5 0.1 broadcast_in_dim.15
  54.6 0.7 reshape_reshape.3.skip_ref
  55.2 0.0 copy-start.3
  55.2 0.0 copy-start.4
  55.2 6.7 %shard_map.170.y_ref = f32[512,2048]{1,0:T(8,128)} custom-call(bf16[512,2048]{1,0:T(8,128)(2,1)} %get-tuple-element.26.xc_ref, bf16[512,512]{1,0:T(8,128)(2,1)} %get-tuple-element.27.bcc_ref.c_ref, f32[512,128]{1,0:T(8,128)} %get-tuple-element.28.cum_ref, f32[512,128]{1,0:T(8,128)} %get-tuple-element.29.step_ref, s32[512,128]{1,0:T(8,128)} %get-tuple-element.24.fl_ref, ...), custom_call_target="tpu_custom_call" | custom-call | flops 1000000000 | bytes 20971520 | tf_op jit(solution)/shard_map/pallas_call | solution.py:539
  61.9 10.4 %collective-permute-done.2.s2_ref = bf16[128,2048]{1,0:T(8,128)(2,1)S(1)} collective-permute-done((bf16[128,2048]{1,0:T(8,128)(2,1)S(1)}, bf16[128,2048]{1,0:T(8,128)(2,1)S(1)}, u32[]{:S(2)}, u32[]{:S(2)}) %collective-permute-start.2) | collective-permute-done | bytes 524320 | tf_op jit(solution)/shard_map/ppermute | solution.py:38
  72.3 0.0 copy-start.5
  72.3 6.5 %all-to-all-done.got_ref = bf16[32,144,128]{2,1,0:T(8,128)(2,1)S(1)} async-done(((bf16[32,144,128]{2,1,0:T(8,128)(2,1)}), bf16[32,144,128]{2,1,0:T(8,128)(2,1)S(1)}, u32[]{:S(2)}, u32[]{:S(2)}) %all-to-all-start) | async-done | bytes 1179680 | tf_op jit(solution)/shard_map/all_to_all | solution.py:559
  78.9 0.0 copy-done.3
  78.9 0.0 copy-done.4
  78.9 1.8 %shard_map.171 = bf16[32,80,128]{2,1,0:T(8,128)(2,1)} custom-call(s32[1,32]{1,0:T(1,128)S(1)} %copy-done.3, s32[1,32]{1,0:T(1,128)S(1)} %copy-done.4, bf16[32,144,128]{2,1,0:T(8,128)(2,1)S(1)} %all-to-all-done.got_ref), custom_call_target="tpu_custom_call" | custom-call | flops 10000000 | bytes 3145728 | tf_op jit(solution)/shard_map/pallas_call | solution.py:573
  80.7 18.1 %all-to-all-start.1 = ((bf16[32,80,128]{2,1,0:T(8,128)(2,1)}), bf16[32,80,128]{2,1,0:T(8,128)(2,1)S(1)}, u32[]{:S(2)}, u32[]{:S(2)}) async-start(bf16[32,80,128]{2,1,0:T(8,128)(2,1)} %shard_map.171), calls=%async_computation.1 | async-start | bytes 1310720 | tf_op jit(solution)/shard_map/all_to_all | solution.py:582
  98.7 0.0 copy-done.5
  98.7 9.0 %shard_map.172 = bf16[512,2048]{1,0:T(8,128)(2,1)} custom-call(f32[512,2048]{1,0:T(8,128)} %shard_map.170.y_ref, bf16[512,2048]{1,0:T(8,128)(2,1)} %bitcast.26, bf16[512,512]{1,0:T(8,128)(2,1)} %get-tuple-element.27.bcc_ref.c_ref, bf16[4,128,2048]{2,1,0:T(8,128)(2,1)} %get-tuple-element.30.ent_ref, bf16[128,2048]{1,0:T(8,128)(2,1)} %copy-done, ...), custom_call_target="tpu_custom_call" | custom-call | flops 1000000000 | bytes 15728640 | tf_op jit(solution)/shard_map/pallas_call | solution.py:588
  107.7 8.6 %all-to-all-done.1 = bf16[32,80,128]{2,1,0:T(8,128)(2,1)S(1)} async-done(((bf16[32,80,128]{2,1,0:T(8,128)(2,1)}), bf16[32,80,128]{2,1,0:T(8,128)(2,1)S(1)}, u32[]{:S(2)}, u32[]{:S(2)}) %all-to-all-start.1) | async-done | bytes 655392 | tf_op jit(solution)/shard_map/all_to_all | solution.py:582
  116.3 3.7 %collective-permute-start.3 = (bf16[32,80,128]{2,1,0:T(8,128)(2,1)S(1)}, bf16[32,80,128]{2,1,0:T(8,128)(2,1)S(1)}, u32[]{:S(2)}, u32[]{:S(2)}) collective-permute-start(bf16[32,80,128]{2,1,0:T(8,128)(2,1)S(1)} %all-to-all-done.1), channel_id=1, source_target_pairs={{0,1},{1,0},{2,3},{3,2},{4,5},{5,4},{6,7},{7,6},{8,9},{9,8},{10,11... | collective-permute-start | bytes 1966088 | tf_op jit(solution)/shard_map/ppermute | solution.py:609
  120.0 1.7 %collective-permute-done.3.got_ref = bf16[32,80,128]{2,1,0:T(8,128)(2,1)S(1)} collective-permute-done((bf16[32,80,128]{2,1,0:T(8,128)(2,1)S(1)}, bf16[32,80,128]{2,1,0:T(8,128)(2,1)S(1)}, u32[]{:S(2)}, u32[]{:S(2)}) %collective-permute-start.3) | collective-permute-done | bytes 655392 | tf_op jit(solution)/shard_map/ppermute | solution.py:609
  121.7 1.2 shard_map.173
  (2 shorter events, 0.0 us)
Async XLA Ops:
  2.2 10.2 %collective-permute-start = (bf16[16,2560]{1,0:T(8,128)(2,1)S(1)}, bf16[16,2560]{1,0:T(8,128)(2,1)S(1)}, u32[]{:S(2)}, u32[]{:S(2)}) collective-permute-start(bf16[16,2560]{1,0:T(8,128)(2,1)S(1)} %pad_maximum_fusion), channel_id=1, source_target_pairs={{0,8},{8,16},{16,24},{24,32},{32,40},{40,48},{48,56},{56,64},{64,7... | collective-permute-start | bytes 245768 | tf_op jit(solution)/shard_map/ppermute | solution.py:38
  12.4 0.6 copy-start.6
  21.6 13.8 %collective-permute-start.1 = (bf16[128,2048]{1,0:T(8,128)(2,1)}, bf16[128,2048]{1,0:T(8,128)(2,1)S(1)}, u32[]{:S(2)}, u32[]{:S(2)}) collective-permute-start(bf16[128,2048]{1,0:T(8,128)(2,1)} %get-tuple-element.31.s_ref), channel_id=1, source_target_pairs={{0,8},{8,16},{16,24},{24,32},{32,40},{40,48},{48,56},{56,64},{64,7... | collective-permute-start | bytes 1572872 | tf_op jit(solution)/shard_map/ppermute | solution.py:38
  35.4 0.8 copy-start
  36.2 14.8 %copy-start.2 = (f32[16,2048]{1,0:T(8,128)S(1)}, f32[16,2048]{1,0:T(8,128)}, u32[]{:S(2)}) copy-start(f32[16,2048]{1,0:T(8,128)} %get-tuple-element.34.entry_ref) | copy-start | bytes 393220
  38.2 12.8 %copy-start.1 = (bf16[128,2048]{1,0:T(8,128)(2,1)S(1)}, bf16[128,2048]{1,0:T(8,128)(2,1)}, u32[]{:S(2)}) copy-start(bf16[128,2048]{1,0:T(8,128)(2,1)} %copy-done) | copy-start | bytes 1572868
  38.2 16.2 %copy-start.7 = (f32[32]{0:T(128)S(1)}, f32[32]{0:T(128)}, u32[]{:S(2)}) copy-start(f32[32]{0:T(128)} %param.24) | copy-start | bytes 388
  38.2 40.6 %all-to-all-start = ((bf16[32,144,128]{2,1,0:T(8,128)(2,1)}), bf16[32,144,128]{2,1,0:T(8,128)(2,1)S(1)}, u32[]{:S(2)}, u32[]{:S(2)}) async-start(bf16[32,144,128]{2,1,0:T(8,128)(2,1)} %shard_map.168), calls=%async_computation | async-start | bytes 2359296 | tf_op jit(solution)/shard_map/all_to_all | solution.py:559
  51.3 21.0 %collective-permute-start.2 = (bf16[128,2048]{1,0:T(8,128)(2,1)S(1)}, bf16[128,2048]{1,0:T(8,128)(2,1)S(1)}, u32[]{:S(2)}, u32[]{:S(2)}) collective-permute-start(bf16[128,2048]{1,0:T(8,128)(2,1)S(1)} %shard_map.169), channel_id=1, source_target_pairs={{0,8},{8,16},{16,24},{24,32},{32,40},{40,48},{48,56},{56,64},{64,7... | collective-permute-start | bytes 1572872 | tf_op jit(solution)/shard_map/ppermute | solution.py:38
  55.2 23.6 %copy-start.3 = (s32[1,32]{1,0:T(1,128)S(1)}, s32[1,32]{1,0:T(1,128)}, u32[]{:S(2)}) copy-start(s32[1,32]{1,0:T(1,128)} %len_ref.5) | copy-start | bytes 388
  55.2 23.6 %copy-start.4 = (s32[1,32]{1,0:T(1,128)S(1)}, s32[1,32]{1,0:T(1,128)}, u32[]{:S(2)}) copy-start(s32[1,32]{1,0:T(1,128)} %owner_ref.1) | copy-start | bytes 388
  72.3 26.4 %copy-start.5 = (bf16[128,2048]{1,0:T(8,128)(2,1)}, bf16[128,2048]{1,0:T(8,128)(2,1)S(1)}, u32[]{:S(2)}) copy-start(bf16[128,2048]{1,0:T(8,128)(2,1)S(1)} %collective-permute-done.2.s2_ref) | copy-start | bytes 1572868
  80.7 35.7 %all-to-all-start.1 = ((bf16[32,80,128]{2,1,0:T(8,128)(2,1)}), bf16[32,80,128]{2,1,0:T(8,128)(2,1)S(1)}, u32[]{:S(2)}, u32[]{:S(2)}) async-start(bf16[32,80,128]{2,1,0:T(8,128)(2,1)} %shard_map.171), calls=%async_computation.1 | async-start | bytes 1310720 | tf_op jit(solution)/shard_map/all_to_all | solution.py:582
  116.3 5.4 %collective-permute-start.3 = (bf16[32,80,128]{2,1,0:T(8,128)(2,1)S(1)}, bf16[32,80,128]{2,1,0:T(8,128)(2,1)S(1)}, u32[]{:S(2)}, u32[]{:S(2)}) collective-permute-start(bf16[32,80,128]{2,1,0:T(8,128)(2,1)S(1)} %all-to-all-done.1), channel_id=1, source_target_pairs={{0,1},{1,0},{2,3},{3,2},{4,5},{5,4},{6,7},{7,6},{8,9},{9,8},{10,11... | collective-permute-start | bytes 1966088 | tf_op jit(solution)/shard_map/ppermute | solution.py:609

commit v3 on v2

--- a/solution.py
+++ b/solution.py
@@ -29,8 +29,8 @@
 STEPS = 4
 SW = WIDTH // STEPS
 SLT = SW // LANES
-PIECE = 2 * 64 + 16
-BACK = 64 + 16
+PIECE = 2 * 64 + 8
+BACK = 64 + 8
 
 
 def shift_in(block, distance):
@@ -67,14 +67,12 @@
     return swish(acc)
 
 
-def scan_lengths(idx_ref, len_ref, first_scr=None):
+def scan_lengths(idx_ref, len_ref):
     zero = jnp.int32(0)
 
     def scan(r, carry):
         first, count, behind, e0, f0, e1, f1, fa = carry
         last = first + len_ref[0, r] - 1
-        if first_scr is not None:
-            first_scr[r] = first
         ends = (last >= 0) & (last < TOK)
         take0, take1 = ends & (count == 0), ends & (count == 1)
         points = [c * STRETCH + STRETCH - 1 for c in range(NC)]
@@ -118,25 +116,33 @@
 
 
 def stage_p(
-    idx_ref, len_ref, dt_ref, al_ref, db_ref, cum_ref, step_ref, fl_ref, wst_ref, first_scr
+    idx_ref, len_ref, dt_ref, al_ref, db_ref, cum_ref, step_ref, fl_ref, wst_ref
 ):
     lane = lax.broadcasted_iota(I32, (STRETCH, LANES), 1)
     row = lax.broadcasted_iota(I32, (STRETCH, LANES), 0)
-    fa = scan_lengths(idx_ref, len_ref, first_scr)[-1]
-    start = -idx_ref[0] * TOK
+    lane_f = lane.astype(F32)
+    start = (-idx_ref[0] * TOK).astype(F32)
+    lengths = jnp.concatenate([len_ref[...].astype(F32)] * 4, axis=1)
+    earlier = jnp.where((row < lane) & (row < REQS), 1.0, 0.0)
+    first = start + jnp.dot(
+        jnp.broadcast_to(lengths, (8, LANES)),
+        earlier,
+        precision=lax.Precision.HIGHEST,
+        preferred_element_type=F32,
+    )[0:1, :]
+    first = jnp.where(lane_f[0:1, :] < REQS, first, start)
     coef = -jnp.exp(jnp.concatenate([al_ref[...]] * 4, axis=1))
     bias = jnp.concatenate([db_ref[...]] * 4, axis=1)
     lower = jnp.where(row >= lane, 1.0, 0.0)
+    through = []
+    gains = [jnp.ones((1, LANES), F32)]
     for c in range(NC):
         rows = slice(c * STRETCH, (c + 1) * STRETCH)
         here = row + c * STRETCH
-
-        def later(r, fl):
-            return jnp.where(here >= first_scr[r], first_scr[r], fl)
-
-        fl_ref[rows, :] = lax.fori_loop(
-            0, REQS, later, jnp.full((STRETCH, LANES), start, I32), unroll=4
-        )
+        started = jnp.where(first <= here.astype(F32), first, start)
+        fl = jnp.broadcast_to(jnp.max(started, axis=1, keepdims=True), (STRETCH, LANES))
+        fl = fl.astype(I32)
+        fl_ref[rows, :] = fl
         raw = jnp.concatenate([dt_ref[:, rows]] * 4, axis=0).T + bias
         step = jnp.maximum(raw, 0.0) + jnp.log1p(jnp.exp(-jnp.abs(raw)))
         step_ref[rows, :] = step
@@ -144,9 +150,11 @@
             lower, coef * step, precision=lax.Precision.HIGHEST, preferred_element_type=F32
         )
         cum_ref[rows, :] = cum
-        w = jnp.exp(cum[STRETCH - 1 :, :] - cum) * step
-        wst_ref[rows, :] = split3(jnp.where(here >= fa[c], w, 0.0), lane)
-    through, gains = stretch_gains(cum_ref, fa)
+        end, fa = cum[STRETCH - 1 :, :], fl[STRETCH - 1 :, :]
+        w = jnp.exp(end - cum) * step
+        wst_ref[rows, :] = split3(jnp.where(here >= fa, w, 0.0), lane)
+        through.append(jnp.where(fa < c * STRETCH, jnp.exp(end), 0.0))
+        gains.append(gains[-1] * through[-1])
     lane16 = lax.broadcasted_iota(I32, (16, LANES), 1)
     wst_ref[NC * STRETCH :, :] = split3(as_rows(through + gains), lane16)
 
@@ -311,7 +319,7 @@
             for k in range(2):
                 one = tails_x[k][:, at]
                 values += [one[0:1], one[1:2]] if half == 0 else [one[2:3], bc_rows[k]]
-            piece_ref[2 * t + half, 128:144, :] = as_rows(values).astype(BF)
+            piece_ref[2 * t + half, 128:136, :] = as_rows(values)[0:8].astype(BF)
 
 
 def stage_b(xc_ref, bcc_ref, cum_ref, step_ref, fl_ref, skip_ref, y_ref):
@@ -376,7 +384,7 @@
 
 
 def combine(len_ref, owner_ref, got_ref, out_ref):
-    row16 = lax.broadcasted_iota(I32, (16, LANES), 0)
+    row8 = lax.broadcasted_iota(I32, (8, LANES), 0)
 
     def one(r, carry):
         first, before = carry
@@ -385,20 +393,20 @@
         second = before == home
         h1 = jnp.maximum(home - 1, 0)
         slot = owner_ref[0, r]
-        extra = got_ref[home, 128:144, :].astype(F32)
+        extra = got_ref[home, 128:136, :].astype(F32)
         gain = jnp.where(second, 0.0, extra[0:1] + extra[1:2])
         k = pl.multiple_of(jnp.where(second, 64, 0), 64)
         own = got_ref[home, pl.ds(k, 64), :].astype(F32)
         out_ref[slot, 0:64, :] = (own + gain * got_ref[h1, 0:64, :].astype(F32)).astype(BF)
-        tail = jnp.where(second, pltpu.roll(extra, 12, 0), pltpu.roll(extra, 14, 0))
-        out_ref[slot, 64:80, :] = jnp.where(row16 < 2, tail, 0.0).astype(BF)
+        tail = jnp.where(second, pltpu.roll(extra, 4, 0), pltpu.roll(extra, 6, 0))
+        out_ref[slot, 64:72, :] = jnp.where(row8 < 2, tail, 0.0).astype(BF)
         return last + 1, home
 
     lax.fori_loop(0, REQS, one, (jnp.int32(0), jnp.int32(-1)), unroll=2)
 
 
 def finish(got_ref, state_ref, tx_ref, tbc_ref):
-    tails = [got_ref[j, 64:80, :].astype(F32) for j in range(REQS)]
+    tails = [got_ref[j, 64:72, :].astype(F32) for j in range(REQS)]
     for t in range(WIDTH // LANES):
         at = slice(t * LANES, (t + 1) * LANES)
         block = jnp.concatenate(
@@ -452,14 +460,13 @@
     cum, step, fl, wst = call(
         stage_p,
         (),
-        [smem, smem, vmem, vmem, vmem],
+        [smem, vmem, vmem, vmem, vmem],
         [
             (by_head, vmem),
             (by_head, vmem),
             (shape((TOK, LANES), I32), vmem),
             (shape((TOK + 16, LANES), BF), vmem),
         ],
-        [pltpu.SMEM((REQS,), I32)],
         flops=10**8,
         nbytes=2**20,
     )(index, lengths, dt_in[0].T, a_log.reshape(1, HEADS), dt_bias.reshape(1, HEADS))

time: 124 us -> 119 us (0.960)
  waiting for transfers between devices: 31.2 us -> 27.2 us
  Pallas kernels: 40.2 us -> 38.2 us
    all_to_all x1, waiting for transfers between devices: 6.52 us -> 3.76 us  [on_device(): got = lax.all_to_all(pieces, 'ctx', split_axis=0, concat_axis=0, tiled=True)]
    pallas_call x1, Pallas kernels: 4.23 us -> 2.32 us  [on_device(): call(stage_p, (), [smem, vmem, vmem, vmem, vmem], [(by_head, vmem), (by_h...]
    all_to_all x1, waiting for transfers between devices: 8.59 us -> 6.71 us  [on_device(): own = lax.all_to_all(back, 'ctx', split_axis=0, concat_axis=0, tiled=True)]
  transfers between devices with their start and end apart: 6 -> 6, of which waited for: 5 -> 5; matrix products, arithmetic and copies ran while one was open for 2% -> 2% of each run, Pallas kernels for 22% -> 21%
where the time goes in v3:
time: 119 us; the launch traced here: 118 us
  starting transfers between devices  46 us (39%)
  Pallas kernels  38.2 us (32%)
  waiting for transfers between devices  27.2 us (23%)
  local copies, waits for them, and re-layouts  5.76 us (5%)
    all_to_all x1, starting transfers between devices, on_device(): own = lax.all_to_all(back, 'ctx', split_axis=0, concat_axis=0, tiled=True)  18.1 us
    ppermute x3, waiting for transfers between devices, shift_in(): lax.ppermute(block, 'ctx', [(i, i + distance) for i in range(count - dist...  15.1 us
    all_to_all x1, starting transfers between devices, on_device(): got = lax.all_to_all(pieces, 'ctx', split_axis=0, concat_axis=0, tiled=True)  13 us
    ppermute x3, starting transfers between devices, shift_in(): lax.ppermute(block, 'ctx', [(i, i + distance) for i in range(count - dist...  10.4 us
    pallas_call x1, Pallas kernels, on_device(): call(stage_c, (GROUPS, NC), [pl.BlockSpec((STRETCH, GWIDTH), by_cg), pl.B...  8.98 us
    pallas_call x1, Pallas kernels, on_device(): call(stage_a, (STEPS,), [cols(TOK), cols(HALO), whole(TOK, BCW), halo_col...  8.49 us
    all_to_all x1, waiting for transfers between devices, on_device(): own = lax.all_to_all(back, 'ctx', split_axis=0, concat_axis=0, tiled=True)  6.71 us
    pallas_call x1, Pallas kernels, on_device(): call(stage_b, (NC,), [by_row(WIDTH), by_row(BCW), by_row(LANES), by_row(L...  6.65 us
  transfers between devices with their start and end apart: 6, of which 5 were waited for; matrix products, arithmetic and copies ran while one was open for 2% of the time, Pallas kernels for 21%

profile of v3, /device:TPU:1, one launch (start us, length us, event | category | flops | bytes accessed | tf_op | source)
XLA Modules:
  0.0 118.0 jit_solution(6796317067109249562)
XLA Ops:
  0.6 0.8 slice_bitcast_fusion
  1.5 0.7 slice.11
  2.2 4.0 %collective-permute-start = (bf16[16,2560]{1,0:T(8,128)(2,1)S(1)}, bf16[16,2560]{1,0:T(8,128)(2,1)S(1)}, u32[]{:S(2)}, u32[]{:S(2)}) collective-permute-start(bf16[16,2560]{1,0:T(8,128)(2,1)S(1)} %pad_maximum_fusion), channel_id=1, source_target_pairs={{0,8},{8,16},{16,24},{24,32},{32,40},{40,48},{48,56},{56,64},{64,7... | collective-permute-start | bytes 245768 | tf_op jit(solution)/shard_map/ppermute | solution.py:38
  6.3 1.9 %copy.20 = bf16[64,8,2,256]{3,1,2,0:T(8,128)(2,1)} copy(bf16[64,8,2,256]{3,2,1,0:T(2,128)(2,1)} %bitcast.28) | data formatting | bytes 1048576
  8.2 2.3 %shard_map.165 = (f32[512,128]{1,0:T(8,128)}, f32[512,128]{1,0:T(8,128)}, s32[512,128]{1,0:T(8,128)}, bf16[528,128]{1,0:T(8,128)(2,1)}) custom-call(s32[1]{0:T(128)} %bitcast.idx_ref, s32[1,32]{1,0:T(1,128)} %len_ref.5, f32[32,512]{1,0:T(8,128)} %bitcast.33, f32[1,32]{1,0:T(1,128)} %bitcast.37, f32[1,32]{1,0:T(1,128)} %bitcast.38), custom_call_target="tpu_custom_call" | custom-call | flops 100000000 | bytes 1048576 | tf_op jit(solution)/shard_map/pallas_call | solution.py:460
  10.5 0.0 collective-permute-done.xh_ref.bch_ref
  10.5 0.0 copy-start.6
  10.5 0.6 copy-done.6
  11.2 8.5 %shard_map.166 = (bf16[512,2048]{1,0:T(8,128)(2,1)}, bf16[512,512]{1,0:T(8,128)(2,1)}, bf16[4,128,2048]{2,1,0:T(8,128)(2,1)}, bf16[128,2048]{1,0:T(8,128)(2,1)}, f32[16,2048]{1,0:T(8,128)}) custom-call(bf16[512,2048]{1,0:T(8,128)(2,1)} %bitcast.22, bf16[16,2560]{1,0:T(8,128)(2,1)} %copy-done.6, bf16[512,512]{1,0:T(8,128)(2,1)} %bitcast.24, ...), custom_call_target="tpu_custom_call" | custom-call | flops 1000000000 | bytes 10485760 | tf_op jit(solution)/shard_map/pallas_call | solution.py:474
  19.7 3.2 %collective-permute-start.1 = (bf16[128,2048]{1,0:T(8,128)(2,1)}, bf16[128,2048]{1,0:T(8,128)(2,1)S(1)}, u32[]{:S(2)}, u32[]{:S(2)}) collective-permute-start(bf16[128,2048]{1,0:T(8,128)(2,1)} %get-tuple-element.31.s_ref), channel_id=1, source_target_pairs={{0,8},{8,16},{16,24},{24,32},{32,40},{40,48},{48,56},{56,64},{64,7... | collective-permute-start | bytes 1572872 | tf_op jit(solution)/shard_map/ppermute | solution.py:38
  22.9 6.6 %shard_map.167 = (bf16[32,136,128]{2,1,0:T(8,128)(2,1)}, f32[8,2048]{1,0:T(8,128)}) custom-call(s32[1]{0:T(128)} %bitcast.idx_ref, s32[1,32]{1,0:T(1,128)} %len_ref.5, bf16[512,2048]{1,0:T(8,128)(2,1)} %bitcast.23, bf16[16,2560]{1,0:T(8,128)(2,1)} %copy-done.6, bf16[512,512]{1,0:T(8,128)(2,1)} %bitcast.25, bf16[16,2560]{1,0:T(8,128)(2,1)} %copy-done.6, ...), custom_call_target="tpu_custom_call" | custom-call | flops 500000000 | bytes 8388608 | tf_op jit(solution)/shard_map/pallas_call | solution.py:512
  29.5 3.9 %collective-permute-done.1.s1_ref = bf16[128,2048]{1,0:T(8,128)(2,1)S(1)} collective-permute-done((bf16[128,2048]{1,0:T(8,128)(2,1)}, bf16[128,2048]{1,0:T(8,128)(2,1)S(1)}, u32[]{:S(2)}, u32[]{:S(2)}) %collective-permute-start.1) | collective-permute-done | bytes 524320 | tf_op jit(solution)/shard_map/ppermute | solution.py:38
  33.4 0.0 copy-start
  33.4 0.8 copy-done
  34.2 0.0 copy-start.2
  34.3 2.1 %shard_map.168 = bf16[32,136,128]{2,1,0:T(8,128)(2,1)} custom-call(bf16[32,136,128]{2,1,0:T(8,128)(2,1)} %get-tuple-element.32.piece_ref, bf16[128,2048]{1,0:T(8,128)(2,1)} %copy-done, f32[8,2048]{1,0:T(8,128)} %get-tuple-element.33.gain_ref), custom_call_target="tpu_custom_call", output_to_operand_aliasing={{}: (0, {})} | custom-call | flops 10000000 | bytes 2097152 | tf_op jit(solution)/shard_map/pallas_call | solution.py:557
  36.3 0.0 copy-start.1
  36.3 0.0 copy-start.7
  36.3 13.0 %all-to-all-start = ((bf16[32,136,128]{2,1,0:T(8,128)(2,1)}), bf16[32,136,128]{2,1,0:T(8,128)(2,1)S(1)}, u32[]{:S(2)}, u32[]{:S(2)}) async-start(bf16[32,136,128]{2,1,0:T(8,128)(2,1)} %shard_map.168), calls=%async_computation | async-start | bytes 2228224 | tf_op jit(solution)/shard_map/all_to_all | solution.py:566
  49.3 0.0 copy-done.2
  49.3 0.0 copy-done.1
  49.3 0.2 shard_map.169
  49.6 3.2 %collective-permute-start.2 = (bf16[128,2048]{1,0:T(8,128)(2,1)S(1)}, bf16[128,2048]{1,0:T(8,128)(2,1)S(1)}, u32[]{:S(2)}, u32[]{:S(2)}) collective-permute-start(bf16[128,2048]{1,0:T(8,128)(2,1)S(1)} %shard_map.169), channel_id=1, source_target_pairs={{0,8},{8,16},{16,24},{24,32},{32,40},{40,48},{48,56},{56,64},{64,7... | collective-permute-start | bytes 1572872 | tf_op jit(solution)/shard_map/ppermute | solution.py:38
  52.8 0.0 copy-done.7
  52.8 0.1 broadcast_in_dim.15
  52.8 0.7 reshape_reshape.3.skip_ref
  53.5 0.0 copy-start.3
  53.5 0.0 copy-start.4
  53.5 6.7 %shard_map.170.y_ref = f32[512,2048]{1,0:T(8,128)} custom-call(bf16[512,2048]{1,0:T(8,128)(2,1)} %get-tuple-element.26.xc_ref, bf16[512,512]{1,0:T(8,128)(2,1)} %get-tuple-element.27.bcc_ref.c_ref, f32[512,128]{1,0:T(8,128)} %get-tuple-element.28.cum_ref, f32[512,128]{1,0:T(8,128)} %get-tuple-element.29.step_ref, s32[512,128]{1,0:T(8,128)} %get-tuple-element.24.fl_ref, ...), custom_call_target="tpu_custom_call" | custom-call | flops 1000000000 | bytes 20971520 | tf_op jit(solution)/shard_map/pallas_call | solution.py:546
  60.2 11.2 %collective-permute-done.2.s2_ref = bf16[128,2048]{1,0:T(8,128)(2,1)S(1)} collective-permute-done((bf16[128,2048]{1,0:T(8,128)(2,1)S(1)}, bf16[128,2048]{1,0:T(8,128)(2,1)S(1)}, u32[]{:S(2)}, u32[]{:S(2)}) %collective-permute-start.2) | collective-permute-done | bytes 524320 | tf_op jit(solution)/shard_map/ppermute | solution.py:38
  71.4 0.0 copy-start.5
  71.4 3.8 %all-to-all-done.got_ref = bf16[32,136,128]{2,1,0:T(8,128)(2,1)S(1)} async-done(((bf16[32,136,128]{2,1,0:T(8,128)(2,1)}), bf16[32,136,128]{2,1,0:T(8,128)(2,1)S(1)}, u32[]{:S(2)}, u32[]{:S(2)}) %all-to-all-start) | async-done | bytes 1114144 | tf_op jit(solution)/shard_map/all_to_all | solution.py:566
  75.1 0.0 copy-done.3
  75.1 0.0 copy-done.4
  75.1 1.7 %shard_map.171 = bf16[32,72,128]{2,1,0:T(8,128)(2,1)} custom-call(s32[1,32]{1,0:T(1,128)S(1)} %copy-done.3, s32[1,32]{1,0:T(1,128)S(1)} %copy-done.4, bf16[32,136,128]{2,1,0:T(8,128)(2,1)S(1)} %all-to-all-done.got_ref), custom_call_target="tpu_custom_call" | custom-call | flops 10000000 | bytes 3145728 | tf_op jit(solution)/shard_map/pallas_call | solution.py:580
  76.9 18.1 %all-to-all-start.1 = ((bf16[32,72,128]{2,1,0:T(8,128)(2,1)}), bf16[32,72,128]{2,1,0:T(8,128)(2,1)S(1)}, u32[]{:S(2)}, u32[]{:S(2)}) async-start(bf16[32,72,128]{2,1,0:T(8,128)(2,1)} %shard_map.171), calls=%async_computation.1 | async-start | bytes 1179648 | tf_op jit(solution)/shard_map/all_to_all | solution.py:589
  95.0 0.0 copy-done.5
  95.0 9.0 %shard_map.172 = bf16[512,2048]{1,0:T(8,128)(2,1)} custom-call(f32[512,2048]{1,0:T(8,128)} %shard_map.170.y_ref, bf16[512,2048]{1,0:T(8,128)(2,1)} %bitcast.26, bf16[512,512]{1,0:T(8,128)(2,1)} %get-tuple-element.27.bcc_ref.c_ref, bf16[4,128,2048]{2,1,0:T(8,128)(2,1)} %get-tuple-element.30.ent_ref, bf16[128,2048]{1,0:T(8,128)(2,1)} %copy-done, ...), custom_call_target="tpu_custom_call" | custom-call | flops 1000000000 | bytes 15728640 | tf_op jit(solution)/shard_map/pallas_call | solution.py:595
  104.0 6.7 %all-to-all-done.1 = bf16[32,72,128]{2,1,0:T(8,128)(2,1)S(1)} async-done(((bf16[32,72,128]{2,1,0:T(8,128)(2,1)}), bf16[32,72,128]{2,1,0:T(8,128)(2,1)S(1)}, u32[]{:S(2)}, u32[]{:S(2)}) %all-to-all-start.1) | async-done | bytes 589856 | tf_op jit(solution)/shard_map/all_to_all | solution.py:589
  110.7 4.5 %collective-permute-start.3 = (bf16[32,72,128]{2,1,0:T(8,128)(2,1)S(1)}, bf16[32,72,128]{2,1,0:T(8,128)(2,1)S(1)}, u32[]{:S(2)}, u32[]{:S(2)}) collective-permute-start(bf16[32,72,128]{2,1,0:T(8,128)(2,1)S(1)} %all-to-all-done.1), channel_id=1, source_target_pairs={{0,1},{1,0},{2,3},{3,2},{4,5},{5,4},{6,7},{7,6},{8,9},{9,8},{10,11... | collective-permute-start | bytes 1769480 | tf_op jit(solution)/shard_map/ppermute | solution.py:616
  115.2 1.6 %collective-permute-done.3.got_ref = bf16[32,72,128]{2,1,0:T(8,128)(2,1)S(1)} collective-permute-done((bf16[32,72,128]{2,1,0:T(8,128)(2,1)S(1)}, bf16[32,72,128]{2,1,0:T(8,128)(2,1)S(1)}, u32[]{:S(2)}, u32[]{:S(2)}) %collective-permute-start.3) | collective-permute-done | bytes 589856 | tf_op jit(solution)/shard_map/ppermute | solution.py:616
  116.8 1.2 %shard_map.173 = (f32[32,64,128]{2,1,0:T(8,128)}, bf16[3,2048]{1,0:T(4,128)(2,1)}, bf16[3,2,256]{2,1,0:T(2,128)(2,1)}) custom-call(bf16[32,72,128]{2,1,0:T(8,128)(2,1)S(1)} %collective-permute-done.3.got_ref), custom_call_target="tpu_custom_call" | custom-call | flops 10000000 | bytes 3145728 | tf_op jit(solution)/shard_map/pallas_call | solution.py:617
  (2 shorter events, 0.0 us)
Async XLA Ops:
  2.2 8.3 %collective-permute-start = (bf16[16,2560]{1,0:T(8,128)(2,1)S(1)}, bf16[16,2560]{1,0:T(8,128)(2,1)S(1)}, u32[]{:S(2)}, u32[]{:S(2)}) collective-permute-start(bf16[16,2560]{1,0:T(8,128)(2,1)S(1)} %pad_maximum_fusion), channel_id=1, source_target_pairs={{0,8},{8,16},{16,24},{24,32},{32,40},{40,48},{48,56},{56,64},{64,7... | collective-permute-start | bytes 245768 | tf_op jit(solution)/shard_map/ppermute | solution.py:38
  10.5 0.6 copy-start.6
  19.7 13.7 %collective-permute-start.1 = (bf16[128,2048]{1,0:T(8,128)(2,1)}, bf16[128,2048]{1,0:T(8,128)(2,1)S(1)}, u32[]{:S(2)}, u32[]{:S(2)}) collective-permute-start(bf16[128,2048]{1,0:T(8,128)(2,1)} %get-tuple-element.31.s_ref), channel_id=1, source_target_pairs={{0,8},{8,16},{16,24},{24,32},{32,40},{40,48},{48,56},{56,64},{64,7... | collective-permute-start | bytes 1572872 | tf_op jit(solution)/shard_map/ppermute | solution.py:38
  33.4 0.8 copy-start
  34.2 15.1 %copy-start.2 = (f32[16,2048]{1,0:T(8,128)S(1)}, f32[16,2048]{1,0:T(8,128)}, u32[]{:S(2)}) copy-start(f32[16,2048]{1,0:T(8,128)} %get-tuple-element.34.entry_ref) | copy-start | bytes 393220
  36.3 13.0 %copy-start.1 = (bf16[128,2048]{1,0:T(8,128)(2,1)S(1)}, bf16[128,2048]{1,0:T(8,128)(2,1)}, u32[]{:S(2)}) copy-start(bf16[128,2048]{1,0:T(8,128)(2,1)} %copy-done) | copy-start | bytes 1572868
  36.3 16.4 %copy-start.7 = (f32[32]{0:T(128)S(1)}, f32[32]{0:T(128)}, u32[]{:S(2)}) copy-start(f32[32]{0:T(128)} %param.24) | copy-start | bytes 388
  36.3 38.8 %all-to-all-start = ((bf16[32,136,128]{2,1,0:T(8,128)(2,1)}), bf16[32,136,128]{2,1,0:T(8,128)(2,1)S(1)}, u32[]{:S(2)}, u32[]{:S(2)}) async-start(bf16[32,136,128]{2,1,0:T(8,128)(2,1)} %shard_map.168), calls=%async_computation | async-start | bytes 2228224 | tf_op jit(solution)/shard_map/all_to_all | solution.py:566
  49.6 21.8 %collective-permute-start.2 = (bf16[128,2048]{1,0:T(8,128)(2,1)S(1)}, bf16[128,2048]{1,0:T(8,128)(2,1)S(1)}, u32[]{:S(2)}, u32[]{:S(2)}) collective-permute-start(bf16[128,2048]{1,0:T(8,128)(2,1)S(1)} %shard_map.169), channel_id=1, source_target_pairs={{0,8},{8,16},{16,24},{24,32},{32,40},{40,48},{48,56},{56,64},{64,7... | collective-permute-start | bytes 1572872 | tf_op jit(solution)/shard_map/ppermute | solution.py:38
  53.5 21.6 %copy-start.3 = (s32[1,32]{1,0:T(1,128)S(1)}, s32[1,32]{1,0:T(1,128)}, u32[]{:S(2)}) copy-start(s32[1,32]{1,0:T(1,128)} %len_ref.5) | copy-start | bytes 388
  53.5 21.6 %copy-start.4 = (s32[1,32]{1,0:T(1,128)S(1)}, s32[1,32]{1,0:T(1,128)}, u32[]{:S(2)}) copy-start(s32[1,32]{1,0:T(1,128)} %owner_ref.1) | copy-start | bytes 388
  71.4 23.6 %copy-start.5 = (bf16[128,2048]{1,0:T(8,128)(2,1)}, bf16[128,2048]{1,0:T(8,128)(2,1)S(1)}, u32[]{:S(2)}) copy-start(bf16[128,2048]{1,0:T(8,128)(2,1)S(1)} %collective-permute-done.2.s2_ref) | copy-start | bytes 1572868
  76.9 33.8 %all-to-all-start.1 = ((bf16[32,72,128]{2,1,0:T(8,128)(2,1)}), bf16[32,72,128]{2,1,0:T(8,128)(2,1)S(1)}, u32[]{:S(2)}, u32[]{:S(2)}) async-start(bf16[32,72,128]{2,1,0:T(8,128)(2,1)} %shard_map.171), calls=%async_computation.1 | async-start | bytes 1179648 | tf_op jit(solution)/shard_map/all_to_all | solution.py:589
  110.7 6.2 %collective-permute-start.3 = (bf16[32,72,128]{2,1,0:T(8,128)(2,1)S(1)}, bf16[32,72,128]{2,1,0:T(8,128)(2,1)S(1)}, u32[]{:S(2)}, u32[]{:S(2)}) collective-permute-start(bf16[32,72,128]{2,1,0:T(8,128)(2,1)S(1)} %all-to-all-done.1), channel_id=1, source_target_pairs={{0,1},{1,0},{2,3},{3,2},{4,5},{5,4},{6,7},{7,6},{8,9},{9,8},{10,11... | collective-permute-start | bytes 1769480 | tf_op jit(solution)/shard_map/ppermute | solution.py:616

commit v4 on v3

--- a/solution.py
+++ b/solution.py
@@ -26,6 +26,7 @@
 GWIDTH = WIDTH // GROUPS
 BCW = 512
 REQS = 32
+ROW_Y = 4
 STEPS = 4
 SW = WIDTH // STEPS
 SLT = SW // LANES
@@ -36,6 +37,12 @@
 def shift_in(block, distance):
     count = lax.axis_size("ctx")
     return lax.ppermute(block, "ctx", [(i, i + distance) for i in range(count - distance)])
+
+
+def shift_pairs(block, distance, keep):
+    count = lax.axis_size("ctx")
+    pairs = [(i, i + distance) for i in range(count - distance) if i % ROW_Y in keep]
+    return lax.ppermute(block, "ctx", pairs)
 
 
 def swish(v):
@@ -116,7 +123,7 @@
 
 
 def stage_p(
-    idx_ref, len_ref, dt_ref, al_ref, db_ref, cum_ref, step_ref, fl_ref, wst_ref
+    idx_ref, len_ref, dt_ref, al_ref, db_ref, cum_ref, step_ref, fl_ref, wst_ref, pass_ref
 ):
     lane = lax.broadcasted_iota(I32, (STRETCH, LANES), 1)
     row = lax.broadcasted_iota(I32, (STRETCH, LANES), 0)
@@ -157,6 +164,7 @@
         gains.append(gains[-1] * through[-1])
     lane16 = lax.broadcasted_iota(I32, (16, LANES), 1)
     wst_ref[NC * STRETCH :, :] = split3(as_rows(through + gains), lane16)
+    pass_ref[...] = jnp.broadcast_to(gains[NC], (16, LANES))
 
 
 def stage_a(
@@ -354,17 +362,19 @@
 
 
 def stage_c(
-    y_ref, z_ref, c_ref, ent_ref, s1_ref, s2_ref, entry_ref, cum_ref, fl_ref, gain_ref, out_ref
+    y_ref, z_ref, c_ref, ent_ref, s1_ref, s2_ref, far_ref, far_gain_ref, entry_ref, cum_ref, fl_ref, gain_ref, out_ref
 ):
     g, c = pl.program_id(0), pl.program_id(1)
     lane = lax.broadcasted_iota(I32, (STRETCH, LANES), 1)
     inflow = jnp.where(fl_ref[...] < c * STRETCH, jnp.exp(cum_ref[...]), 0.0)
+    both = jnp.concatenate([split3(inflow, lane), split3(far_gain_ref[...], lane[0:16])], axis=0)
     wide = jnp.dot(
-        split3(inflow, lane),
-        spread_matrix(g * (HEADS // GROUPS), GWIDTH),
-        preferred_element_type=F32,
-    )
+        both, spread_matrix(g * (HEADS // GROUPS), GWIDTH), preferred_element_type=F32
+    )
+    far_gain = wide[STRETCH : STRETCH + 1, :]
+    wide = wide[0:STRETCH, :]
     incoming = s1_ref[...].astype(F32) + s2_ref[...].astype(F32)
+    incoming = incoming + far_gain * far_ref[...].astype(F32)
     entering = ent_ref[0].astype(F32) + entry_ref[pl.ds(NC + c, 1), :] * incoming
     carried = jnp.dot(c_ref[...], entering.astype(BF), preferred_element_type=F32)
     gated = (y_ref[...] + wide * carried) * swish(z_ref[...].astype(F32))
@@ -457,7 +467,7 @@
 
     vmem = pl.BlockSpec(memory_space=pltpu.VMEM)
     by_head = shape((TOK, LANES), F32)
-    cum, step, fl, wst = call(
+    cum, step, fl, wst, passing = call(
         stage_p,
         (),
         [smem, vmem, vmem, vmem, vmem],
@@ -466,6 +476,7 @@
             (by_head, vmem),
             (shape((TOK, LANES), I32), vmem),
             (shape((TOK + 16, LANES), BF), vmem),
+            (shape((16, LANES), F32), vmem),
         ],
         flops=10**8,
         nbytes=2**20,
@@ -508,6 +519,8 @@
     )
 
     s1 = shift_in(left, 1)
+    crossed = shift_pairs(left, ROW_Y - 1, (ROW_Y - 2,))
+    far_gain = shift_pairs(passing, 1, (ROW_Y - 1,))
 
     pieces, gain = call(
         stage_e,
@@ -552,6 +565,7 @@
         nbytes=20 * 2**20,
     )(xc, bcc, cum, step, fl, jnp.repeat(skip_d, HEAD_DIM).reshape(1, WIDTH))
 
+    s1, crossed = lax.optimization_barrier((s1, crossed))
     part = pl.BlockSpec((16, 64, LANES), lambda s: (s, 0, 0))
     half = lambda rows: pl.BlockSpec((rows, GWIDTH), lambda s: (0, s))
     (pieces,) = call(
@@ -574,9 +588,11 @@
         nbytes=2 * 2**20,
         limit=SMALL,
     )(s1, entry)
-    s2 = shift_in(passed, 1)
-
-    got, s2, y = lax.optimization_barrier((got, s2, y))
+    s2 = shift_pairs(passed, 1, range(ROW_Y - 1))
+    count = lax.axis_size("ctx")
+    far = lax.ppermute(crossed, "ctx", [(i + 1, i) for i in range(0, count, ROW_Y)])
+
+    got, s2, far, far_gain, y = lax.optimization_barrier((got, s2, far, far_gain, y))
     (back,) = call(
         combine,
         (),
@@ -602,6 +618,8 @@
             pl.BlockSpec((1, STATE, GWIDTH), lambda g, c: (c, 0, g)),
             pl.BlockSpec((STATE, GWIDTH), by_g),
             pl.BlockSpec((STATE, GWIDTH), by_g),
+            pl.BlockSpec((STATE, GWIDTH), by_g),
+            whole(16, LANES),
             pl.BlockSpec((16, GWIDTH), by_g),
             pl.BlockSpec((STRETCH, LANES), by_c),
             pl.BlockSpec((STRETCH, LANES), by_c),
@@ -610,7 +628,7 @@
         [(shape((TOK, WIDTH), BF), pl.BlockSpec((STRETCH, GWIDTH), by_cg))],
         flops=10**9,
         nbytes=15 * 2**20,
-    )(y, z, bcc, ent, s1, s2, entry, cum, fl, norm_gain.reshape(1, WIDTH))
+    )(y, z, bcc, ent, s1, s2, far, far_gain, entry, cum, fl, norm_gain.reshape(1, WIDTH))
 
     own, mixed = lax.optimization_barrier((own, mixed))
     swapped = lax.ppermute(own, "side", [(0, 1), (1, 0)])

time: 119 us -> 110 us (0.924)
  starting transfers between devices: 46 us -> 39.3 us
  waiting for transfers between devices: 27.2 us -> 24.2 us
    ppermute x0 -> x4, waiting for transfers between devices: none -> 11.7 us  [the longest x3 8.88 us: shift_pairs(): return lax.ppermute(block, 'ctx', pairs)]
    ppermute x3 -> x2, waiting for transfers between devices: 15.1 us -> 3.94 us  [shift_in(): lax.ppermute(block, 'ctx', [(i, i + distance) for i in range(count - dist...]
    all_to_all x1, starting transfers between devices: 18.1 us -> 8.35 us  [on_device(): own = lax.all_to_all(back, 'ctx', split_axis=0, concat_axis=0, tiled=True)]
    ppermute x0 -> x4, starting transfers between devices: none -> 5.81 us  [the longest x3 4.52 us: shift_pairs(): return lax.ppermute(block, 'ctx', pairs)]
    ppermute x3 -> x2, starting transfers between devices: 10.4 us -> 7.27 us  [shift_in(): lax.ppermute(block, 'ctx', [(i, i + distance) for i in range(count - dist...]
    all_to_all x1, waiting for transfers between devices: 3.76 us -> 1.12 us  [on_device(): got = lax.all_to_all(pieces, 'ctx', split_axis=0, concat_axis=0, tiled=True)]
    pallas_call x1, Pallas kernels: 8.98 us -> 10.2 us  [on_device(): call(stage_c, (GROUPS, NC), [pl.BlockSpec((STRETCH, GWIDTH), by_cg), pl.B...]
    unnamed x18 -> x24, local copies, waits for them, and re-layouts: 3.43 us -> 3.45 us
  transfers between devices with their start and end apart: 6 -> 9, of which waited for: 5 -> 6; matrix products, arithmetic and copies ran while one was open for 2% -> 2% of each run, Pallas kernels for 21% -> 24%
where the time goes in v4:
time: 110 us; the launch traced here: 109 us
  starting transfers between devices  39.3 us (36%)
  Pallas kernels  39.3 us (36%)
  waiting for transfers between devices  24.2 us (22%)
  local copies, waits for them, and re-layouts  5.78 us (5%)
    all_to_all x1, starting transfers between devices, on_device(): got = lax.all_to_all(pieces, 'ctx', split_axis=0, concat_axis=0, tiled=True)  13.7 us
    pallas_call x1, Pallas kernels, on_device(): call(stage_c, (GROUPS, NC), [pl.BlockSpec((STRETCH, GWIDTH), by_cg), pl.B...  10.2 us
    ppermute x3, waiting for transfers between devices, shift_pairs(): return lax.ppermute(block, 'ctx', pairs)  8.88 us
    pallas_call x1, Pallas kernels, on_device(): call(stage_a, (STEPS,), [cols(TOK), cols(HALO), whole(TOK, BCW), halo_col...  8.46 us
    all_to_all x1, starting transfers between devices, on_device(): own = lax.all_to_all(back, 'ctx', split_axis=0, concat_axis=0, tiled=True)  8.35 us
    ppermute x2, starting transfers between devices, shift_in(): lax.ppermute(block, 'ctx', [(i, i + distance) for i in range(count - dist...  7.27 us
    pallas_call x1, Pallas kernels, on_device(): call(stage_b, (NC,), [by_row(WIDTH), by_row(BCW), by_row(LANES), by_row(L...  6.63 us
    pallas_call x1, Pallas kernels, on_device(): call(stage_e, (STEPS,), [smem, smem, cols(TOK), cols(HALO), whole(TOK, BC...  6.58 us
  transfers between devices with their start and end apart: 9, of which 6 were waited for; matrix products, arithmetic and copies ran while one was open for 2% of the time, Pallas kernels for 24%

profile of v4, /device:TPU:1, one launch (start us, length us, event | category | flops | bytes accessed | tf_op | source)
XLA Modules:
  0.0 109.4 jit_solution(13123381195596021277)
XLA Ops:
  0.6 0.7 slice.11
  1.4 0.8 slice_bitcast_fusion
  2.2 4.0 %collective-permute-start = (bf16[16,2560]{1,0:T(8,128)(2,1)S(1)}, bf16[16,2560]{1,0:T(8,128)(2,1)S(1)}, u32[]{:S(2)}, u32[]{:S(2)}) collective-permute-start(bf16[16,2560]{1,0:T(8,128)(2,1)S(1)} %pad_maximum_fusion), channel_id=1, source_target_pairs={{0,8},{8,16},{16,24},{24,32},{32,40},{40,48},{48,56},{56,64},{64,7... | collective-permute-start | bytes 245768 | tf_op jit(solution)/shard_map/ppermute | solution.py:39
  6.3 1.9 %copy.20 = bf16[64,8,2,256]{3,1,2,0:T(8,128)(2,1)} copy(bf16[64,8,2,256]{3,2,1,0:T(2,128)(2,1)} %bitcast.28) | data formatting | bytes 1048576
  8.2 2.2 %shard_map.165 = (f32[512,128]{1,0:T(8,128)}, f32[512,128]{1,0:T(8,128)}, s32[512,128]{1,0:T(8,128)}, bf16[528,128]{1,0:T(8,128)(2,1)}, f32[16,128]{1,0:T(8,128)}) custom-call(s32[1]{0:T(128)} %bitcast.idx_ref, s32[1,32]{1,0:T(1,128)} %len_ref.5, f32[32,512]{1,0:T(8,128)} %bitcast.33, f32[1,32]{1,0:T(1,128)} %bitcast.37, f32[1,32]{1,0:T(1,128)} %bitcast.38), custom_call_target="tpu_custom_call" | custom-call | flops 100000000 | bytes 1048576 | tf_op jit(solution)/shard_map/pallas_call | solution.py:470
  10.4 0.0 collective-permute-done.xh_ref.bch_ref
  10.4 0.0 copy-start.7
  10.4 0.6 copy-done.7
  11.1 8.5 %shard_map.166 = (bf16[512,2048]{1,0:T(8,128)(2,1)}, bf16[512,512]{1,0:T(8,128)(2,1)}, bf16[4,128,2048]{2,1,0:T(8,128)(2,1)}, bf16[128,2048]{1,0:T(8,128)(2,1)}, f32[16,2048]{1,0:T(8,128)}) custom-call(bf16[512,2048]{1,0:T(8,128)(2,1)} %bitcast.22, bf16[16,2560]{1,0:T(8,128)(2,1)} %copy-done.7, bf16[512,512]{1,0:T(8,128)(2,1)} %bitcast.26, ...), custom_call_target="tpu_custom_call" | custom-call | flops 1000000000 | bytes 10485760 | tf_op jit(solution)/shard_map/pallas_call | solution.py:485
  19.5 0.7 collective-permute-start.2
  20.2 3.2 %collective-permute-start.1 = (bf16[128,2048]{1,0:T(8,128)(2,1)}, bf16[128,2048]{1,0:T(8,128)(2,1)S(1)}, u32[]{:S(2)}, u32[]{:S(2)}) collective-permute-start(bf16[128,2048]{1,0:T(8,128)(2,1)} %get-tuple-element.36.s_ref), channel_id=1, source_target_pairs={{0,8},{8,16},{16,24},{24,32},{32,40},{40,48},{48,56},{56,64},{64,7... | collective-permute-start | bytes 1572872 | tf_op jit(solution)/shard_map/ppermute | solution.py:39
  23.5 6.6 %shard_map.167 = (bf16[32,136,128]{2,1,0:T(8,128)(2,1)}, f32[8,2048]{1,0:T(8,128)}) custom-call(s32[1]{0:T(128)} %bitcast.idx_ref, s32[1,32]{1,0:T(1,128)} %len_ref.5, bf16[512,2048]{1,0:T(8,128)(2,1)} %bitcast.23, bf16[16,2560]{1,0:T(8,128)(2,1)} %copy-done.7, bf16[512,512]{1,0:T(8,128)(2,1)} %bitcast.27, bf16[16,2560]{1,0:T(8,128)(2,1)} %copy-done.7, ...), custom_call_target="tpu_custom_call" | custom-call | flops 500000000 | bytes 8388608 | tf_op jit(solution)/shard_map/pallas_call | solution.py:525
  30.1 0.0 collective-permute-done.2
  30.1 3.9 %collective-permute-done.1.s1_ref = bf16[128,2048]{1,0:T(8,128)(2,1)S(1)} collective-permute-done((bf16[128,2048]{1,0:T(8,128)(2,1)}, bf16[128,2048]{1,0:T(8,128)(2,1)S(1)}, u32[]{:S(2)}, u32[]{:S(2)}) %collective-permute-start.1) | collective-permute-done | bytes 524320 | tf_op jit(solution)/shard_map/ppermute | solution.py:39
  34.0 0.0 copy-start
  34.0 0.9 copy-done
  34.9 2.0 %shard_map.168 = bf16[32,136,128]{2,1,0:T(8,128)(2,1)} custom-call(bf16[32,136,128]{2,1,0:T(8,128)(2,1)} %get-tuple-element.37.piece_ref, bf16[128,2048]{1,0:T(8,128)(2,1)} %copy-done, f32[8,2048]{1,0:T(8,128)} %get-tuple-element.39.gain_ref), custom_call_target="tpu_custom_call", output_to_operand_aliasing={{}: (0, {})} | custom-call | flops 10000000 | bytes 2097152 | tf_op jit(solution)/shard_map/pallas_call | solution.py:571
  36.9 0.0 copy-start.1
  36.9 0.0 copy-start.10
  36.9 0.0 copy-start.9
  36.9 13.7 %all-to-all-start = ((bf16[32,136,128]{2,1,0:T(8,128)(2,1)}), bf16[32,136,128]{2,1,0:T(8,128)(2,1)S(1)}, u32[]{:S(2)}, u32[]{:S(2)}) async-start(bf16[32,136,128]{2,1,0:T(8,128)(2,1)} %shard_map.168), calls=%async_computation | async-start | bytes 2228224 | tf_op jit(solution)/shard_map/all_to_all | solution.py:580
  50.6 0.0 copy-done.2
  50.7 0.0 copy-done.1
  50.7 0.2 shard_map.169
  50.9 3.2 %collective-permute-start.3 = (bf16[128,2048]{1,0:T(8,128)(2,1)S(1)}, bf16[128,2048]{1,0:T(8,128)(2,1)S(1)}, u32[]{:S(2)}, u32[]{:S(2)}) collective-permute-start(bf16[128,2048]{1,0:T(8,128)(2,1)S(1)} %shard_map.169), channel_id=1, source_target_pairs={{0,8},{8,16},{16,24},{32,40},{40,48},{48,56},{64,72},{72,80},{80,8... | collective-permute-start | bytes 1572872 | tf_op jit(solution)/shard_map/ppermute | solution.py:45
  54.1 1.3 %collective-permute-start.4 = (bf16[128,2048]{1,0:T(8,128)(2,1)S(1)}, bf16[128,2048]{1,0:T(8,128)(2,1)S(1)}, u32[]{:S(2)}, u32[]{:S(2)}) collective-permute-start(bf16[128,2048]{1,0:T(8,128)(2,1)S(1)} %collective-permute-done.2), channel_id=1, source_target_pairs={{8,0},{40,32},{72,64},{104,96},{136,128},{168,160},{200,192},{232,... | collective-permute-start | bytes 1572872 | tf_op jit(solution)/shard_map/ppermute | solution.py:593
  55.4 0.0 copy-done.10
  55.4 0.7 collective-permute-start.5
  56.1 0.0 copy-done.9
  56.1 0.1 broadcast_in_dim.15
  56.1 0.7 reshape_reshape.3.skip_ref
  56.8 6.6 %shard_map.170.y_ref = f32[512,2048]{1,0:T(8,128)} custom-call(bf16[512,2048]{1,0:T(8,128)(2,1)} %get-tuple-element.31.xc_ref, bf16[512,512]{1,0:T(8,128)(2,1)} %get-tuple-element.32.bcc_ref.c_ref, f32[512,128]{1,0:T(8,128)} %get-tuple-element.33.cum_ref, f32[512,128]{1,0:T(8,128)} %get-tuple-element.34.step_ref, s32[512,128]{1,0:T(8,128)} %get-tuple-element.29.fl_ref, ...), custom_call_target="tpu_custom_call" | custom-call | flops 1000000000 | bytes 20971520 | tf_op jit(solution)/shard_map/pallas_call | solution.py:559
  63.5 0.0 collective-permute-done.5.far_gain_ref
  63.5 8.9 %collective-permute-done.3.s2_ref = bf16[128,2048]{1,0:T(8,128)(2,1)S(1)} collective-permute-done((bf16[128,2048]{1,0:T(8,128)(2,1)S(1)}, bf16[128,2048]{1,0:T(8,128)(2,1)S(1)}, u32[]{:S(2)}, u32[]{:S(2)}) %collective-permute-start.3) | collective-permute-done | bytes 524320 | tf_op jit(solution)/shard_map/ppermute | solution.py:45
  72.3 2.8 %collective-permute-done.4.far_ref = bf16[128,2048]{1,0:T(8,128)(2,1)S(1)} collective-permute-done((bf16[128,2048]{1,0:T(8,128)(2,1)S(1)}, bf16[128,2048]{1,0:T(8,128)(2,1)S(1)}, u32[]{:S(2)}, u32[]{:S(2)}) %collective-permute-start.4) | collective-permute-done | bytes 524320 | tf_op jit(solution)/shard_map/ppermute | solution.py:593
  75.2 1.1 %all-to-all-done.got_ref = bf16[32,136,128]{2,1,0:T(8,128)(2,1)S(1)} async-done(((bf16[32,136,128]{2,1,0:T(8,128)(2,1)}), bf16[32,136,128]{2,1,0:T(8,128)(2,1)S(1)}, u32[]{:S(2)}, u32[]{:S(2)}) %all-to-all-start) | async-done | bytes 1114144 | tf_op jit(solution)/shard_map/all_to_all | solution.py:580
  76.3 0.0 copy-done.3
  76.3 0.0 copy-done.4
  76.3 1.7 %shard_map.171 = bf16[32,72,128]{2,1,0:T(8,128)(2,1)} custom-call(s32[1,32]{1,0:T(1,128)S(1)} %copy-done.3, s32[1,32]{1,0:T(1,128)S(1)} %copy-done.4, bf16[32,136,128]{2,1,0:T(8,128)(2,1)S(1)} %all-to-all-done.got_ref), custom_call_target="tpu_custom_call" | custom-call | flops 10000000 | bytes 3145728 | tf_op jit(solution)/shard_map/pallas_call | solution.py:596
  78.0 8.4 %all-to-all-start.1 = ((bf16[32,72,128]{2,1,0:T(8,128)(2,1)}), bf16[32,72,128]{2,1,0:T(8,128)(2,1)S(1)}, u32[]{:S(2)}, u32[]{:S(2)}) async-start(bf16[32,72,128]{2,1,0:T(8,128)(2,1)} %shard_map.171), calls=%async_computation.1 | async-start | bytes 1179648 | tf_op jit(solution)/shard_map/all_to_all | solution.py:605
  86.4 0.0 copy-done.8
  86.4 0.0 copy-done.5
  86.4 0.0 copy-done.6
  86.4 10.2 %shard_map.172 = bf16[512,2048]{1,0:T(8,128)(2,1)} custom-call(f32[512,2048]{1,0:T(8,128)} %shard_map.170.y_ref, bf16[512,2048]{1,0:T(8,128)(2,1)} %bitcast.24, bf16[512,512]{1,0:T(8,128)(2,1)} %get-tuple-element.32.bcc_ref.c_ref, bf16[4,128,2048]{2,1,0:T(8,128)(2,1)} %get-tuple-element.35.ent_ref, bf16[128,2048]{1,0:T(8,128)(2,1)} %copy-done, ...), custom_call_target="tpu_custom_call" | custom-call | flops 1000000000 | bytes 15728640 | tf_op jit(solution)/shard_map/pallas_call | solution.py:611
  96.7 5.8 %all-to-all-done.1 = bf16[32,72,128]{2,1,0:T(8,128)(2,1)S(1)} async-done(((bf16[32,72,128]{2,1,0:T(8,128)(2,1)}), bf16[32,72,128]{2,1,0:T(8,128)(2,1)S(1)}, u32[]{:S(2)}, u32[]{:S(2)}) %all-to-all-start.1) | async-done | bytes 589856 | tf_op jit(solution)/shard_map/all_to_all | solution.py:605
  102.5 4.1 %collective-permute-start.6 = (bf16[32,72,128]{2,1,0:T(8,128)(2,1)S(1)}, bf16[32,72,128]{2,1,0:T(8,128)(2,1)S(1)}, u32[]{:S(2)}, u32[]{:S(2)}) collective-permute-start(bf16[32,72,128]{2,1,0:T(8,128)(2,1)S(1)} %all-to-all-done.1), channel_id=1, source_target_pairs={{0,1},{1,0},{2,3},{3,2},{4,5},{5,4},{6,7},{7,6},{8,9},{9,8},{10,11... | collective-permute-start | bytes 1769480 | tf_op jit(solution)/shard_map/ppermute | solution.py:634
  106.6 1.6 %collective-permute-done.6.got_ref = bf16[32,72,128]{2,1,0:T(8,128)(2,1)S(1)} collective-permute-done((bf16[32,72,128]{2,1,0:T(8,128)(2,1)S(1)}, bf16[32,72,128]{2,1,0:T(8,128)(2,1)S(1)}, u32[]{:S(2)}, u32[]{:S(2)}) %collective-permute-start.6) | collective-permute-done | bytes 589856 | tf_op jit(solution)/shard_map/ppermute | solution.py:634
  108.3 1.2 %shard_map.173 = (f32[32,64,128]{2,1,0:T(8,128)}, bf16[3,2048]{1,0:T(4,128)(2,1)}, bf16[3,2,256]{2,1,0:T(2,128)(2,1)}) custom-call(bf16[32,72,128]{2,1,0:T(8,128)(2,1)S(1)} %collective-permute-done.6.got_ref), custom_call_target="tpu_custom_call" | custom-call | flops 10000000 | bytes 3145728 | tf_op jit(solution)/shard_map/pallas_call | solution.py:635
  (8 shorter events, 0.0 us)
Async XLA Ops:
  2.2 8.2 %collective-permute-start = (bf16[16,2560]{1,0:T(8,128)(2,1)S(1)}, bf16[16,2560]{1,0:T(8,128)(2,1)S(1)}, u32[]{:S(2)}, u32[]{:S(2)}) collective-permute-start(bf16[16,2560]{1,0:T(8,128)(2,1)S(1)} %pad_maximum_fusion), channel_id=1, source_target_pairs={{0,8},{8,16},{16,24},{24,32},{32,40},{40,48},{48,56},{56,64},{64,7... | collective-permute-start | bytes 245768 | tf_op jit(solution)/shard_map/ppermute | solution.py:39
  10.4 0.6 copy-start.7
  19.5 10.5 %collective-permute-start.2 = (bf16[128,2048]{1,0:T(8,128)(2,1)}, bf16[128,2048]{1,0:T(8,128)(2,1)S(1)}, u32[]{:S(2)}, u32[]{:S(2)}) collective-permute-start(bf16[128,2048]{1,0:T(8,128)(2,1)} %get-tuple-element.36.s_ref), channel_id=1, source_target_pairs={{16,40},{48,72},{80,104},{112,136},{144,168},{176,200},{208,232},{... | collective-permute-start | bytes 1572872 | tf_op jit(solution)/shard_map/ppermute | solution.py:45
  20.2 13.8 %collective-permute-start.1 = (bf16[128,2048]{1,0:T(8,128)(2,1)}, bf16[128,2048]{1,0:T(8,128)(2,1)S(1)}, u32[]{:S(2)}, u32[]{:S(2)}) collective-permute-start(bf16[128,2048]{1,0:T(8,128)(2,1)} %get-tuple-element.36.s_ref), channel_id=1, source_target_pairs={{0,8},{8,16},{16,24},{24,32},{32,40},{40,48},{48,56},{56,64},{64,7... | collective-permute-start | bytes 1572872 | tf_op jit(solution)/shard_map/ppermute | solution.py:39
  34.0 0.9 copy-start
  34.9 15.8 %copy-start.2 = (f32[16,2048]{1,0:T(8,128)S(1)}, f32[16,2048]{1,0:T(8,128)}, u32[]{:S(2)}) copy-start(f32[16,2048]{1,0:T(8,128)} %get-tuple-element.40.entry_ref) | copy-start | bytes 393220
  36.9 13.8 %copy-start.1 = (bf16[128,2048]{1,0:T(8,128)(2,1)S(1)}, bf16[128,2048]{1,0:T(8,128)(2,1)}, u32[]{:S(2)}) copy-start(bf16[128,2048]{1,0:T(8,128)(2,1)} %copy-done) | copy-start | bytes 1572868
  36.9 18.5 %copy-start.10 = (f32[16,128]{1,0:T(8,128)S(1)}, f32[16,128]{1,0:T(8,128)}, u32[]{:S(2)}) copy-start(f32[16,128]{1,0:T(8,128)} %get-tuple-element.42) | copy-start | bytes 24580
  36.9 19.2 %copy-start.9 = (f32[32]{0:T(128)S(1)}, f32[32]{0:T(128)}, u32[]{:S(2)}) copy-start(f32[32]{0:T(128)} %param.24) | copy-start | bytes 388
  36.9 39.4 %all-to-all-start = ((bf16[32,136,128]{2,1,0:T(8,128)(2,1)}), bf16[32,136,128]{2,1,0:T(8,128)(2,1)S(1)}, u32[]{:S(2)}, u32[]{:S(2)}) async-start(bf16[32,136,128]{2,1,0:T(8,128)(2,1)} %shard_map.168), calls=%async_computation | async-start | bytes 2228224 | tf_op jit(solution)/shard_map/all_to_all | solution.py:580
  50.9 21.4 %collective-permute-start.3 = (bf16[128,2048]{1,0:T(8,128)(2,1)S(1)}, bf16[128,2048]{1,0:T(8,128)(2,1)S(1)}, u32[]{:S(2)}, u32[]{:S(2)}) collective-permute-start(bf16[128,2048]{1,0:T(8,128)(2,1)S(1)} %shard_map.169), channel_id=1, source_target_pairs={{0,8},{8,16},{16,24},{32,40},{40,48},{48,56},{64,72},{72,80},{80,8... | collective-permute-start | bytes 1572872 | tf_op jit(solution)/shard_map/ppermute | solution.py:45
  54.1 21.1 %collective-permute-start.4 = (bf16[128,2048]{1,0:T(8,128)(2,1)S(1)}, bf16[128,2048]{1,0:T(8,128)(2,1)S(1)}, u32[]{:S(2)}, u32[]{:S(2)}) collective-permute-start(bf16[128,2048]{1,0:T(8,128)(2,1)S(1)} %collective-permute-done.2), channel_id=1, source_target_pairs={{8,0},{40,32},{72,64},{104,96},{136,128},{168,160},{200,192},{232,... | collective-permute-start | bytes 1572872 | tf_op jit(solution)/shard_map/ppermute | solution.py:593
  55.4 8.1 %collective-permute-start.5 = (f32[16,128]{1,0:T(8,128)S(1)}, f32[16,128]{1,0:T(8,128)S(1)}, u32[]{:S(2)}, u32[]{:S(2)}) collective-permute-start(f32[16,128]{1,0:T(8,128)S(1)} %copy-done.10), channel_id=1, source_target_pairs={{24,32},{56,64},{88,96},{120,128},{152,160},{184,192},{216,224},{2... | collective-permute-start | bytes 24584 | tf_op jit(solution)/shard_map/ppermute | solution.py:45
  56.8 19.5 %copy-start.3 = (s32[1,32]{1,0:T(1,128)S(1)}, s32[1,32]{1,0:T(1,128)}, u32[]{:S(2)}) copy-start(s32[1,32]{1,0:T(1,128)} %len_ref.5) | copy-start | bytes 388
  56.8 19.5 %copy-start.4 = (s32[1,32]{1,0:T(1,128)S(1)}, s32[1,32]{1,0:T(1,128)}, u32[]{:S(2)}) copy-start(s32[1,32]{1,0:T(1,128)} %owner_ref.1) | copy-start | bytes 388
  63.5 22.9 %copy-start.8 = (f32[16,128]{1,0:T(8,128)}, f32[16,128]{1,0:T(8,128)S(1)}, u32[]{:S(2)}) copy-start(f32[16,128]{1,0:T(8,128)S(1)} %collective-permute-done.5.far_gain_ref) | copy-start | bytes 24580
  72.3 14.1 %copy-start.5 = (bf16[128,2048]{1,0:T(8,128)(2,1)}, bf16[128,2048]{1,0:T(8,128)(2,1)S(1)}, u32[]{:S(2)}) copy-start(bf16[128,2048]{1,0:T(8,128)(2,1)S(1)} %collective-permute-done.3.s2_ref) | copy-start | bytes 1572868
  75.2 11.2 %copy-start.6 = (bf16[128,2048]{1,0:T(8,128)(2,1)}, bf16[128,2048]{1,0:T(8,128)(2,1)S(1)}, u32[]{:S(2)}) copy-start(bf16[128,2048]{1,0:T(8,128)(2,1)S(1)} %collective-permute-done.4.far_ref) | copy-start | bytes 1572868
  78.0 24.5 %all-to-all-start.1 = ((bf16[32,72,128]{2,1,0:T(8,128)(2,1)}), bf16[32,72,128]{2,1,0:T(8,128)(2,1)S(1)}, u32[]{:S(2)}, u32[]{:S(2)}) async-start(bf16[32,72,128]{2,1,0:T(8,128)(2,1)} %shard_map.171), calls=%async_computation.1 | async-start | bytes 1179648 | tf_op jit(solution)/shard_map/all_to_all | solution.py:605
  102.5 5.8 %collective-permute-start.6 = (bf16[32,72,128]{2,1,0:T(8,128)(2,1)S(1)}, bf16[32,72,128]{2,1,0:T(8,128)(2,1)S(1)}, u32[]{:S(2)}, u32[]{:S(2)}) collective-permute-start(bf16[32,72,128]{2,1,0:T(8,128)(2,1)S(1)} %all-to-all-done.1), channel_id=1, source_target_pairs={{0,1},{1,0},{2,3},{3,2},{4,5},{5,4},{6,7},{7,6},{8,9},{9,8},{10,11... | collective-permute-start | bytes 1769480 | tf_op jit(solution)/shard_map/ppermute | solution.py:634

commit v5 on v4

--- a/solution.py
+++ b/solution.py
@@ -30,8 +30,8 @@
 STEPS = 4
 SW = WIDTH // STEPS
 SLT = SW // LANES
-PIECE = 2 * 64 + 8
-BACK = 64 + 8
+PIECE = 2 * 64 + 16
+BACK = 64 + 16
 
 
 def shift_in(block, distance):
@@ -68,10 +68,10 @@
 
 
 def conv_tile(ext, taps, bias, masks):
-    acc = bias + taps[KW - 1] * ext[HALO:]
+    half = 0.5 * bias + (0.5 * taps[KW - 1]) * ext[HALO:]
     for d in range(1, KW):
-        acc = acc + taps[KW - 1 - d] * (pltpu.roll(ext, d, 0)[HALO:] * masks[d - 1])
-    return swish(acc)
+        half = half + (0.5 * taps[KW - 1 - d]) * (pltpu.roll(ext, d, 0)[HALO:] * masks[d - 1])
+    return half + half * jnp.tanh(half)
 
 
 def scan_lengths(idx_ref, len_ref):
@@ -327,7 +327,7 @@
             for k in range(2):
                 one = tails_x[k][:, at]
                 values += [one[0:1], one[1:2]] if half == 0 else [one[2:3], bc_rows[k]]
-            piece_ref[2 * t + half, 128:136, :] = as_rows(values)[0:8].astype(BF)
+            piece_ref[2 * t + half, 128:144, :] = as_rows(values).astype(BF)
 
 
 def stage_b(xc_ref, bcc_ref, cum_ref, step_ref, fl_ref, skip_ref, y_ref):
@@ -394,7 +394,7 @@
 
 
 def combine(len_ref, owner_ref, got_ref, out_ref):
-    row8 = lax.broadcasted_iota(I32, (8, LANES), 0)
+    row16 = lax.broadcasted_iota(I32, (16, LANES), 0)
 
     def one(r, carry):
         first, before = carry
@@ -403,20 +403,20 @@
         second = before == home
         h1 = jnp.maximum(home - 1, 0)
         slot = owner_ref[0, r]
-        extra = got_ref[home, 128:136, :].astype(F32)
+        extra = got_ref[home, 128:144, :].astype(F32)
         gain = jnp.where(second, 0.0, extra[0:1] + extra[1:2])
         k = pl.multiple_of(jnp.where(second, 64, 0), 64)
         own = got_ref[home, pl.ds(k, 64), :].astype(F32)
         out_ref[slot, 0:64, :] = (own + gain * got_ref[h1, 0:64, :].astype(F32)).astype(BF)
-        tail = jnp.where(second, pltpu.roll(extra, 4, 0), pltpu.roll(extra, 6, 0))
-        out_ref[slot, 64:72, :] = jnp.where(row8 < 2, tail, 0.0).astype(BF)
+        tail = jnp.where(second, pltpu.roll(extra, 12, 0), pltpu.roll(extra, 14, 0))
+        out_ref[slot, 64:80, :] = jnp.where(row16 < 2, tail, 0.0).astype(BF)
         return last + 1, home
 
     lax.fori_loop(0, REQS, one, (jnp.int32(0), jnp.int32(-1)), unroll=2)
 
 
 def finish(got_ref, state_ref, tx_ref, tbc_ref):
-    tails = [got_ref[j, 64:72, :].astype(F32) for j in range(REQS)]
+    tails = [got_ref[j, 64:80, :].astype(F32) for j in range(REQS)]
     for t in range(WIDTH // LANES):
         at = slice(t * LANES, (t + 1) * LANES)
         block = jnp.concatenate(

time: 110 us -> 112 us (1.018)
  waiting for transfers between devices: 24.2 us -> 26.8 us
    all_to_all x1, waiting for transfers between devices: 1.12 us -> 4.27 us  [on_device(): got = lax.all_to_all(pieces, 'ctx', split_axis=0, concat_axis=0, tiled=True)]
    ppermute x1, waiting for transfers between devices: 2.82 us -> 1.36 us  [on_device(): lax.ppermute(crossed, 'ctx', [(i + 1, i) for i in range(0, count, ROW_Y)])]
    all_to_all x1, starting transfers between devices: 8.35 us -> 7.07 us  [on_device(): own = lax.all_to_all(back, 'ctx', split_axis=0, concat_axis=0, tiled=True)]
  transfers between devices with their start and end apart: 9 -> 9, of which waited for: 6 -> 6; matrix products, arithmetic and copies ran while one was open for 2% -> 2% of each run, Pallas kernels for 24% -> 23%
where the time goes in v5:
time: 112 us; the launch traced here: 111 us
  Pallas kernels  39.3 us (35%)
  starting transfers between devices  38.8 us (35%)
  waiting for transfers between devices  26.8 us (24%)
  local copies, waits for them, and re-layouts  5.77 us (5%)
    all_to_all x1, starting transfers between devices, on_device(): got = lax.all_to_all(pieces, 'ctx', split_axis=0, concat_axis=0, tiled=True)  13.7 us
    pallas_call x1, Pallas kernels, on_device(): call(stage_c, (GROUPS, NC), [pl.BlockSpec((STRETCH, GWIDTH), by_cg), pl.B...  10.2 us
    ppermute x3, waiting for transfers between devices, shift_pairs(): return lax.ppermute(block, 'ctx', pairs)  9.08 us
    pallas_call x1, Pallas kernels, on_device(): call(stage_a, (STEPS,), [cols(TOK), cols(HALO), whole(TOK, BCW), halo_col...  8.42 us
    ppermute x2, starting transfers between devices, shift_in(): lax.ppermute(block, 'ctx', [(i, i + distance) for i in range(count - dist...  7.27 us
    all_to_all x1, starting transfers between devices, on_device(): own = lax.all_to_all(back, 'ctx', split_axis=0, concat_axis=0, tiled=True)  7.07 us
    pallas_call x1, Pallas kernels, on_device(): call(stage_b, (NC,), [by_row(WIDTH), by_row(BCW), by_row(LANES), by_row(L...  6.63 us
    pallas_call x1, Pallas kernels, on_device(): call(stage_e, (STEPS,), [smem, smem, cols(TOK), cols(HALO), whole(TOK, BC...  6.6 us
  transfers between devices with their start and end apart: 9, of which 6 were waited for; matrix products, arithmetic and copies ran while one was open for 2% of the time, Pallas kernels for 23%

profile of v5, /device:TPU:1, one launch (start us, length us, event | category | flops | bytes accessed | tf_op | source)
XLA Modules:
  0.0 111.4 jit_solution(11415163688144524942)
XLA Ops:
  0.6 0.7 slice.11
  1.4 0.8 slice_bitcast_fusion
  2.2 4.0 %collective-permute-start = (bf16[16,2560]{1,0:T(8,128)(2,1)S(1)}, bf16[16,2560]{1,0:T(8,128)(2,1)S(1)}, u32[]{:S(2)}, u32[]{:S(2)}) collective-permute-start(bf16[16,2560]{1,0:T(8,128)(2,1)S(1)} %pad_maximum_fusion), channel_id=1, source_target_pairs={{0,8},{8,16},{16,24},{24,32},{32,40},{40,48},{48,56},{56,64},{64,7... | collective-permute-start | bytes 245768 | tf_op jit(solution)/shard_map/ppermute | solution.py:39
  6.3 1.9 %copy.20 = bf16[64,8,2,256]{3,1,2,0:T(8,128)(2,1)} copy(bf16[64,8,2,256]{3,2,1,0:T(2,128)(2,1)} %bitcast.28) | data formatting | bytes 1048576
  8.2 2.2 %shard_map.165 = (f32[512,128]{1,0:T(8,128)}, f32[512,128]{1,0:T(8,128)}, s32[512,128]{1,0:T(8,128)}, bf16[528,128]{1,0:T(8,128)(2,1)}, f32[16,128]{1,0:T(8,128)}) custom-call(s32[1]{0:T(128)} %bitcast.idx_ref, s32[1,32]{1,0:T(1,128)} %len_ref.5, f32[32,512]{1,0:T(8,128)} %bitcast.33, f32[1,32]{1,0:T(1,128)} %bitcast.37, f32[1,32]{1,0:T(1,128)} %bitcast.38), custom_call_target="tpu_custom_call" | custom-call | flops 100000000 | bytes 1048576 | tf_op jit(solution)/shard_map/pallas_call | solution.py:470
  10.5 0.0 collective-permute-done.xh_ref.bch_ref
  10.5 0.0 copy-start.7
  10.5 0.6 copy-done.7
  11.1 8.4 %shard_map.166 = (bf16[512,2048]{1,0:T(8,128)(2,1)}, bf16[512,512]{1,0:T(8,128)(2,1)}, bf16[4,128,2048]{2,1,0:T(8,128)(2,1)}, bf16[128,2048]{1,0:T(8,128)(2,1)}, f32[16,2048]{1,0:T(8,128)}) custom-call(bf16[512,2048]{1,0:T(8,128)(2,1)} %bitcast.22, bf16[16,2560]{1,0:T(8,128)(2,1)} %copy-done.7, bf16[512,512]{1,0:T(8,128)(2,1)} %bitcast.26, ...), custom_call_target="tpu_custom_call" | custom-call | flops 1000000000 | bytes 10485760 | tf_op jit(solution)/shard_map/pallas_call | solution.py:485
  19.5 0.7 collective-permute-start.2
  20.2 3.2 %collective-permute-start.1 = (bf16[128,2048]{1,0:T(8,128)(2,1)}, bf16[128,2048]{1,0:T(8,128)(2,1)S(1)}, u32[]{:S(2)}, u32[]{:S(2)}) collective-permute-start(bf16[128,2048]{1,0:T(8,128)(2,1)} %get-tuple-element.36.s_ref), channel_id=1, source_target_pairs={{0,8},{8,16},{16,24},{24,32},{32,40},{40,48},{48,56},{56,64},{64,7... | collective-permute-start | bytes 1572872 | tf_op jit(solution)/shard_map/ppermute | solution.py:39
  23.4 6.6 %shard_map.167 = (bf16[32,144,128]{2,1,0:T(8,128)(2,1)}, f32[8,2048]{1,0:T(8,128)}) custom-call(s32[1]{0:T(128)} %bitcast.idx_ref, s32[1,32]{1,0:T(1,128)} %len_ref.5, bf16[512,2048]{1,0:T(8,128)(2,1)} %bitcast.23, bf16[16,2560]{1,0:T(8,128)(2,1)} %copy-done.7, bf16[512,512]{1,0:T(8,128)(2,1)} %bitcast.27, bf16[16,2560]{1,0:T(8,128)(2,1)} %copy-done.7, ...), custom_call_target="tpu_custom_call" | custom-call | flops 500000000 | bytes 8388608 | tf_op jit(solution)/shard_map/pallas_call | solution.py:525
  30.0 0.0 collective-permute-done.2
  30.1 3.9 %collective-permute-done.1.s1_ref = bf16[128,2048]{1,0:T(8,128)(2,1)S(1)} collective-permute-done((bf16[128,2048]{1,0:T(8,128)(2,1)}, bf16[128,2048]{1,0:T(8,128)(2,1)S(1)}, u32[]{:S(2)}, u32[]{:S(2)}) %collective-permute-start.1) | collective-permute-done | bytes 524320 | tf_op jit(solution)/shard_map/ppermute | solution.py:39
  34.0 0.0 copy-start
  34.0 0.8 copy-done
  34.8 0.0 copy-start.2
  34.8 2.0 %shard_map.168 = bf16[32,144,128]{2,1,0:T(8,128)(2,1)} custom-call(bf16[32,144,128]{2,1,0:T(8,128)(2,1)} %get-tuple-element.37.piece_ref, bf16[128,2048]{1,0:T(8,128)(2,1)} %copy-done, f32[8,2048]{1,0:T(8,128)} %get-tuple-element.39.gain_ref), custom_call_target="tpu_custom_call", output_to_operand_aliasing={{}: (0, {})} | custom-call | flops 10000000 | bytes 2097152 | tf_op jit(solution)/shard_map/pallas_call | solution.py:571
  36.9 0.0 copy-start.1
  36.9 0.0 copy-start.10
  36.9 13.7 %all-to-all-start = ((bf16[32,144,128]{2,1,0:T(8,128)(2,1)}), bf16[32,144,128]{2,1,0:T(8,128)(2,1)S(1)}, u32[]{:S(2)}, u32[]{:S(2)}) async-start(bf16[32,144,128]{2,1,0:T(8,128)(2,1)} %shard_map.168), calls=%async_computation | async-start | bytes 2359296 | tf_op jit(solution)/shard_map/all_to_all | solution.py:580
  50.6 0.0 copy-done.2
  50.6 0.0 copy-done.1
  50.6 0.2 shard_map.169
  50.9 3.2 %collective-permute-start.3 = (bf16[128,2048]{1,0:T(8,128)(2,1)S(1)}, bf16[128,2048]{1,0:T(8,128)(2,1)S(1)}, u32[]{:S(2)}, u32[]{:S(2)}) collective-permute-start(bf16[128,2048]{1,0:T(8,128)(2,1)S(1)} %shard_map.169), channel_id=1, source_target_pairs={{0,8},{8,16},{16,24},{32,40},{40,48},{48,56},{64,72},{72,80},{80,8... | collective-permute-start | bytes 1572872 | tf_op jit(solution)/shard_map/ppermute | solution.py:45
  54.1 1.3 %collective-permute-start.4 = (bf16[128,2048]{1,0:T(8,128)(2,1)S(1)}, bf16[128,2048]{1,0:T(8,128)(2,1)S(1)}, u32[]{:S(2)}, u32[]{:S(2)}) collective-permute-start(bf16[128,2048]{1,0:T(8,128)(2,1)S(1)} %collective-permute-done.2), channel_id=1, source_target_pairs={{8,0},{40,32},{72,64},{104,96},{136,128},{168,160},{200,192},{232,... | collective-permute-start | bytes 1572872 | tf_op jit(solution)/shard_map/ppermute | solution.py:593
  55.4 0.0 copy-done.10
  55.4 0.7 collective-permute-start.5
  56.0 0.0 copy-done.9
  56.1 0.1 broadcast_in_dim.15
  56.1 0.7 reshape_reshape.3.skip_ref
  56.8 6.6 %shard_map.170.y_ref = f32[512,2048]{1,0:T(8,128)} custom-call(bf16[512,2048]{1,0:T(8,128)(2,1)} %get-tuple-element.31.xc_ref, bf16[512,512]{1,0:T(8,128)(2,1)} %get-tuple-element.32.bcc_ref.c_ref, f32[512,128]{1,0:T(8,128)} %get-tuple-element.33.cum_ref, f32[512,128]{1,0:T(8,128)} %get-tuple-element.34.step_ref, s32[512,128]{1,0:T(8,128)} %get-tuple-element.29.fl_ref, ...), custom_call_target="tpu_custom_call" | custom-call | flops 1000000000 | bytes 20971520 | tf_op jit(solution)/shard_map/pallas_call | solution.py:559
  63.4 0.0 collective-permute-done.5.far_gain_ref
  63.5 9.1 %collective-permute-done.3.s2_ref = bf16[128,2048]{1,0:T(8,128)(2,1)S(1)} collective-permute-done((bf16[128,2048]{1,0:T(8,128)(2,1)S(1)}, bf16[128,2048]{1,0:T(8,128)(2,1)S(1)}, u32[]{:S(2)}, u32[]{:S(2)}) %collective-permute-start.3) | collective-permute-done | bytes 524320 | tf_op jit(solution)/shard_map/ppermute | solution.py:45
  72.5 1.4 %collective-permute-done.4.far_ref = bf16[128,2048]{1,0:T(8,128)(2,1)S(1)} collective-permute-done((bf16[128,2048]{1,0:T(8,128)(2,1)S(1)}, bf16[128,2048]{1,0:T(8,128)(2,1)S(1)}, u32[]{:S(2)}, u32[]{:S(2)}) %collective-permute-start.4) | collective-permute-done | bytes 524320 | tf_op jit(solution)/shard_map/ppermute | solution.py:593
  73.9 4.3 %all-to-all-done.got_ref = bf16[32,144,128]{2,1,0:T(8,128)(2,1)S(1)} async-done(((bf16[32,144,128]{2,1,0:T(8,128)(2,1)}), bf16[32,144,128]{2,1,0:T(8,128)(2,1)S(1)}, u32[]{:S(2)}, u32[]{:S(2)}) %all-to-all-start) | async-done | bytes 1179680 | tf_op jit(solution)/shard_map/all_to_all | solution.py:580
  78.2 0.0 copy-done.3
  78.2 0.0 copy-done.4
  78.2 1.8 %shard_map.171 = bf16[32,80,128]{2,1,0:T(8,128)(2,1)} custom-call(s32[1,32]{1,0:T(1,128)S(1)} %copy-done.3, s32[1,32]{1,0:T(1,128)S(1)} %copy-done.4, bf16[32,144,128]{2,1,0:T(8,128)(2,1)S(1)} %all-to-all-done.got_ref), custom_call_target="tpu_custom_call" | custom-call | flops 10000000 | bytes 3145728 | tf_op jit(solution)/shard_map/pallas_call | solution.py:596
  80.0 7.1 %all-to-all-start.1 = ((bf16[32,80,128]{2,1,0:T(8,128)(2,1)}), bf16[32,80,128]{2,1,0:T(8,128)(2,1)S(1)}, u32[]{:S(2)}, u32[]{:S(2)}) async-start(bf16[32,80,128]{2,1,0:T(8,128)(2,1)} %shard_map.171), calls=%async_computation.1 | async-start | bytes 1310720 | tf_op jit(solution)/shard_map/all_to_all | solution.py:605
  87.0 0.0 copy-done.8
  87.1 0.0 copy-done.5
  87.1 0.0 copy-done.6
  87.1 10.2 %shard_map.172 = bf16[512,2048]{1,0:T(8,128)(2,1)} custom-call(f32[512,2048]{1,0:T(8,128)} %shard_map.170.y_ref, bf16[512,2048]{1,0:T(8,128)(2,1)} %bitcast.24, bf16[512,512]{1,0:T(8,128)(2,1)} %get-tuple-element.32.bcc_ref.c_ref, bf16[4,128,2048]{2,1,0:T(8,128)(2,1)} %get-tuple-element.35.ent_ref, bf16[128,2048]{1,0:T(8,128)(2,1)} %copy-done, ...), custom_call_target="tpu_custom_call" | custom-call | flops 1000000000 | bytes 15728640 | tf_op jit(solution)/shard_map/pallas_call | solution.py:611
  97.3 6.4 %all-to-all-done.1 = bf16[32,80,128]{2,1,0:T(8,128)(2,1)S(1)} async-done(((bf16[32,80,128]{2,1,0:T(8,128)(2,1)}), bf16[32,80,128]{2,1,0:T(8,128)(2,1)S(1)}, u32[]{:S(2)}, u32[]{:S(2)}) %all-to-all-start.1) | async-done | bytes 655392 | tf_op jit(solution)/shard_map/all_to_all | solution.py:605
  103.6 4.9 %collective-permute-start.6 = (bf16[32,80,128]{2,1,0:T(8,128)(2,1)S(1)}, bf16[32,80,128]{2,1,0:T(8,128)(2,1)S(1)}, u32[]{:S(2)}, u32[]{:S(2)}) collective-permute-start(bf16[32,80,128]{2,1,0:T(8,128)(2,1)S(1)} %all-to-all-done.1), channel_id=1, source_target_pairs={{0,1},{1,0},{2,3},{3,2},{4,5},{5,4},{6,7},{7,6},{8,9},{9,8},{10,11... | collective-permute-start | bytes 1966088 | tf_op jit(solution)/shard_map/ppermute | solution.py:634
  108.5 1.7 %collective-permute-done.6.got_ref = bf16[32,80,128]{2,1,0:T(8,128)(2,1)S(1)} collective-permute-done((bf16[32,80,128]{2,1,0:T(8,128)(2,1)S(1)}, bf16[32,80,128]{2,1,0:T(8,128)(2,1)S(1)}, u32[]{:S(2)}, u32[]{:S(2)}) %collective-permute-start.6) | collective-permute-done | bytes 655392 | tf_op jit(solution)/shard_map/ppermute | solution.py:634
  110.3 1.2 %shard_map.173 = (f32[32,64,128]{2,1,0:T(8,128)}, bf16[3,2048]{1,0:T(4,128)(2,1)}, bf16[3,2,256]{2,1,0:T(2,128)(2,1)}) custom-call(bf16[32,80,128]{2,1,0:T(8,128)(2,1)S(1)} %collective-permute-done.6.got_ref), custom_call_target="tpu_custom_call" | custom-call | flops 10000000 | bytes 3145728 | tf_op jit(solution)/shard_map/pallas_call | solution.py:635
  (8 shorter events, 0.0 us)
Async XLA Ops:
  2.2 8.2 %collective-permute-start = (bf16[16,2560]{1,0:T(8,128)(2,1)S(1)}, bf16[16,2560]{1,0:T(8,128)(2,1)S(1)}, u32[]{:S(2)}, u32[]{:S(2)}) collective-permute-start(bf16[16,2560]{1,0:T(8,128)(2,1)S(1)} %pad_maximum_fusion), channel_id=1, source_target_pairs={{0,8},{8,16},{16,24},{24,32},{32,40},{40,48},{48,56},{56,64},{64,7... | collective-permute-start | bytes 245768 | tf_op jit(solution)/shard_map/ppermute | solution.py:39
  10.5 0.6 copy-start.7
  19.5 10.5 %collective-permute-start.2 = (bf16[128,2048]{1,0:T(8,128)(2,1)}, bf16[128,2048]{1,0:T(8,128)(2,1)S(1)}, u32[]{:S(2)}, u32[]{:S(2)}) collective-permute-start(bf16[128,2048]{1,0:T(8,128)(2,1)} %get-tuple-element.36.s_ref), channel_id=1, source_target_pairs={{16,40},{48,72},{80,104},{112,136},{144,168},{176,200},{208,232},{... | collective-permute-start | bytes 1572872 | tf_op jit(solution)/shard_map/ppermute | solution.py:45
  20.2 13.8 %collective-permute-start.1 = (bf16[128,2048]{1,0:T(8,128)(2,1)}, bf16[128,2048]{1,0:T(8,128)(2,1)S(1)}, u32[]{:S(2)}, u32[]{:S(2)}) collective-permute-start(bf16[128,2048]{1,0:T(8,128)(2,1)} %get-tuple-element.36.s_ref), channel_id=1, source_target_pairs={{0,8},{8,16},{16,24},{24,32},{32,40},{40,48},{48,56},{56,64},{64,7... | collective-permute-start | bytes 1572872 | tf_op jit(solution)/shard_map/ppermute | solution.py:39
  34.0 0.9 copy-start
  34.8 15.8 %copy-start.2 = (f32[16,2048]{1,0:T(8,128)S(1)}, f32[16,2048]{1,0:T(8,128)}, u32[]{:S(2)}) copy-start(f32[16,2048]{1,0:T(8,128)} %get-tuple-element.40.entry_ref) | copy-start | bytes 393220
  36.9 13.8 %copy-start.1 = (bf16[128,2048]{1,0:T(8,128)(2,1)S(1)}, bf16[128,2048]{1,0:T(8,128)(2,1)}, u32[]{:S(2)}) copy-start(bf16[128,2048]{1,0:T(8,128)(2,1)} %copy-done) | copy-start | bytes 1572868
  36.9 18.5 %copy-start.10 = (f32[16,128]{1,0:T(8,128)S(1)}, f32[16,128]{1,0:T(8,128)}, u32[]{:S(2)}) copy-start(f32[16,128]{1,0:T(8,128)} %get-tuple-element.42) | copy-start | bytes 24580
  36.9 19.2 %copy-start.9 = (f32[32]{0:T(128)S(1)}, f32[32]{0:T(128)}, u32[]{:S(2)}) copy-start(f32[32]{0:T(128)} %param.24) | copy-start | bytes 388
  36.9 41.3 %all-to-all-start = ((bf16[32,144,128]{2,1,0:T(8,128)(2,1)}), bf16[32,144,128]{2,1,0:T(8,128)(2,1)S(1)}, u32[]{:S(2)}, u32[]{:S(2)}) async-start(bf16[32,144,128]{2,1,0:T(8,128)(2,1)} %shard_map.168), calls=%async_computation | async-start | bytes 2359296 | tf_op jit(solution)/shard_map/all_to_all | solution.py:580
  50.9 21.6 %collective-permute-start.3 = (bf16[128,2048]{1,0:T(8,128)(2,1)S(1)}, bf16[128,2048]{1,0:T(8,128)(2,1)S(1)}, u32[]{:S(2)}, u32[]{:S(2)}) collective-permute-start(bf16[128,2048]{1,0:T(8,128)(2,1)S(1)} %shard_map.169), channel_id=1, source_target_pairs={{0,8},{8,16},{16,24},{32,40},{40,48},{48,56},{64,72},{72,80},{80,8... | collective-permute-start | bytes 1572872 | tf_op jit(solution)/shard_map/ppermute | solution.py:45
  54.1 19.8 %collective-permute-start.4 = (bf16[128,2048]{1,0:T(8,128)(2,1)S(1)}, bf16[128,2048]{1,0:T(8,128)(2,1)S(1)}, u32[]{:S(2)}, u32[]{:S(2)}) collective-permute-start(bf16[128,2048]{1,0:T(8,128)(2,1)S(1)} %collective-permute-done.2), channel_id=1, source_target_pairs={{8,0},{40,32},{72,64},{104,96},{136,128},{168,160},{200,192},{232,... | collective-permute-start | bytes 1572872 | tf_op jit(solution)/shard_map/ppermute | solution.py:593
  55.4 8.1 %collective-permute-start.5 = (f32[16,128]{1,0:T(8,128)S(1)}, f32[16,128]{1,0:T(8,128)S(1)}, u32[]{:S(2)}, u32[]{:S(2)}) collective-permute-start(f32[16,128]{1,0:T(8,128)S(1)} %copy-done.10), channel_id=1, source_target_pairs={{24,32},{56,64},{88,96},{120,128},{152,160},{184,192},{216,224},{2... | collective-permute-start | bytes 24584 | tf_op jit(solution)/shard_map/ppermute | solution.py:45
  56.8 21.4 %copy-start.3 = (s32[1,32]{1,0:T(1,128)S(1)}, s32[1,32]{1,0:T(1,128)}, u32[]{:S(2)}) copy-start(s32[1,32]{1,0:T(1,128)} %len_ref.5) | copy-start | bytes 388
  56.8 21.4 %copy-start.4 = (s32[1,32]{1,0:T(1,128)S(1)}, s32[1,32]{1,0:T(1,128)}, u32[]{:S(2)}) copy-start(s32[1,32]{1,0:T(1,128)} %owner_ref.1) | copy-start | bytes 388
  63.4 23.6 %copy-start.8 = (f32[16,128]{1,0:T(8,128)}, f32[16,128]{1,0:T(8,128)S(1)}, u32[]{:S(2)}) copy-start(f32[16,128]{1,0:T(8,128)S(1)} %collective-permute-done.5.far_gain_ref) | copy-start | bytes 24580
  72.5 14.5 %copy-start.5 = (bf16[128,2048]{1,0:T(8,128)(2,1)}, bf16[128,2048]{1,0:T(8,128)(2,1)S(1)}, u32[]{:S(2)}) copy-start(bf16[128,2048]{1,0:T(8,128)(2,1)S(1)} %collective-permute-done.3.s2_ref) | copy-start | bytes 1572868
  73.9 13.2 %copy-start.6 = (bf16[128,2048]{1,0:T(8,128)(2,1)}, bf16[128,2048]{1,0:T(8,128)(2,1)S(1)}, u32[]{:S(2)}) copy-start(bf16[128,2048]{1,0:T(8,128)(2,1)S(1)} %collective-permute-done.4.far_ref) | copy-start | bytes 1572868
  80.0 23.7 %all-to-all-start.1 = ((bf16[32,80,128]{2,1,0:T(8,128)(2,1)}), bf16[32,80,128]{2,1,0:T(8,128)(2,1)S(1)}, u32[]{:S(2)}, u32[]{:S(2)}) async-start(bf16[32,80,128]{2,1,0:T(8,128)(2,1)} %shard_map.171), calls=%async_computation.1 | async-start | bytes 1310720 | tf_op jit(solution)/shard_map/all_to_all | solution.py:605
  103.6 6.6 %collective-permute-start.6 = (bf16[32,80,128]{2,1,0:T(8,128)(2,1)S(1)}, bf16[32,80,128]{2,1,0:T(8,128)(2,1)S(1)}, u32[]{:S(2)}, u32[]{:S(2)}) collective-permute-start(bf16[32,80,128]{2,1,0:T(8,128)(2,1)S(1)} %all-to-all-done.1), channel_id=1, source_target_pairs={{0,1},{1,0},{2,3},{3,2},{4,5},{5,4},{6,7},{7,6},{8,9},{9,8},{10,11... | collective-permute-start | bytes 1966088 | tf_op jit(solution)/shard_map/ppermute | solution.py:634

commit v6 on v4

--- a/solution.py
+++ b/solution.py
@@ -182,7 +182,7 @@
             since = row + c * STRETCH - fl_ref[rows, :]
             for d in range(1, KW):
                 mask_scr[d - 1, rows, :] = jnp.where(since >= d, 1.0, 0.0)
-        for part in range(2):
+        for part in range(1):
             for g in range(GROUPS):
                 at = slice((part * GROUPS + g) * LANES, (part * GROUPS + g + 1) * LANES)
                 own = slice(g * LANES, (g + 1) * LANES)
@@ -235,8 +235,8 @@
 
 def stage_e(
     idx_ref, len_ref, x_ref, xh_ref, bc_ref, bch_ref, xc_ref, bcc_ref, cum_ref, step_ref, ent_ref,
-    s_ref,
-    piece_ref, gain_ref,
+    s_ref, wbc_ref, bbc_ref, fl_ref,
+    piece_ref, gain_ref, cc_ref,
     wst_scr, spread_scr, sc_scr,
 ):
     s = pl.program_id(0)
@@ -246,6 +246,21 @@
 
     @pl.when(s == 0)
     def _():
+        for c in range(NC):
+            rows = slice(c * STRETCH, (c + 1) * STRETCH)
+            since = row + c * STRETCH - fl_ref[rows, :]
+            masks = [jnp.where(since >= d, 1.0, 0.0) for d in range(1, KW)]
+            for g in range(GROUPS):
+                own = slice(g * LANES, (g + 1) * LANES)
+                at = slice((GROUPS + g) * LANES, (GROUPS + g + 1) * LANES)
+                if c == 0:
+                    ext = jnp.concatenate([bch_ref[:, at], bc_ref[0:STRETCH, at]], axis=0)
+                else:
+                    ext = bc_ref[c * STRETCH - HALO : (c + 1) * STRETCH, at]
+                taps = [wbc_ref[k, 1:2, own] for k in range(KW)]
+                cc_ref[rows, own] = conv_tile(
+                    ext.astype(F32), taps, bbc_ref[1:2, own], masks
+                ).astype(BF)
         count, behind, e0, f0, e1, f1, fa = scan_lengths(idx_ref, len_ref)
         sc_scr[0], sc_scr[1], sc_scr[2], sc_scr[3], sc_scr[4] = e0, f0, e1, f1, count
         inflow = []
@@ -330,7 +345,7 @@
             piece_ref[2 * t + half, 128:136, :] = as_rows(values)[0:8].astype(BF)
 
 
-def stage_b(xc_ref, bcc_ref, cum_ref, step_ref, fl_ref, skip_ref, y_ref):
+def stage_b(xc_ref, bcc_ref, cc_ref, cum_ref, step_ref, fl_ref, skip_ref, y_ref):
     c = pl.program_id(0)
     row = lax.broadcasted_iota(I32, (STRETCH, LANES), 0)
     lane = lax.broadcasted_iota(I32, (STRETCH, LANES), 1)
@@ -341,7 +356,7 @@
     low = lax.broadcasted_iota(I32, (STRETCH, LANES), 1) < HEAD_DIM
     for g in range(GROUPS):
         b = bcc_ref[:, g * LANES : (g + 1) * LANES]
-        cc = bcc_ref[:, (GROUPS + g) * LANES : (GROUPS + g + 1) * LANES]
+        cc = cc_ref[:, g * LANES : (g + 1) * LANES]
         scores = lax.dot_general(cc, b, (((1,), (1,)), ((), ())), preferred_element_type=F32)
         for i in range(HEADS // GROUPS // 2):
             pair = g * (HEADS // GROUPS // 2) + i
@@ -499,7 +514,7 @@
         ],
         [
             (shape((TOK, WIDTH), BF), cols(TOK)),
-            (shape((TOK, BCW), BF), whole(TOK, BCW)),
+            (shape((TOK, GROUPS * LANES), BF), whole(TOK, GROUPS * LANES)),
             (
                 shape((NC, STATE, WIDTH), BF),
                 pl.BlockSpec((NC, STATE, SW), lambda s: (0, 0, s)),
@@ -522,7 +537,7 @@
     crossed = shift_pairs(left, ROW_Y - 1, (ROW_Y - 2,))
     far_gain = shift_pairs(passing, 1, (ROW_Y - 1,))
 
-    pieces, gain = call(
+    pieces, gain, cc = call(
         stage_e,
         (STEPS,),
         [
@@ -533,11 +548,14 @@
             whole(TOK, BCW),
             halo_cols,
             cols(TOK),
-            whole(TOK, BCW),
+            whole(TOK, GROUPS * LANES),
             whole(TOK, LANES),
             whole(TOK, LANES),
             pl.BlockSpec((NC, STATE, SW), lambda s: (0, 0, s)),
             cols(STATE),
+            whole(KW, 2, 2 * LANES),
+            whole(2, 2 * LANES),
+            whole(TOK, LANES),
         ],
         [
             (
@@ -545,6 +563,7 @@
                 pl.BlockSpec((2 * SLT, PIECE, LANES), lambda s: (s, 0, 0)),
             ),
             (shape((8, WIDTH), F32), cols(8)),
+            (shape((TOK, GROUPS * LANES), BF), whole(TOK, GROUPS * LANES)),
         ],
         [
             pltpu.VMEM((2 * STRETCH + 16, LANES), BF),
@@ -553,17 +572,17 @@
         ],
         flops=5 * 10**8,
         nbytes=8 * 2**20,
-    )(index, lengths, x, halo, bc, halo, xc, bcc, cum, step, ent, left)
+    )(index, lengths, x, halo, bc, halo, xc, bcc, cum, step, ent, left, conv_bc_w, conv_bc_b, fl)
 
     by_row = lambda width: pl.BlockSpec((STRETCH, width), lambda c: (c, 0))
     (y,) = call(
         stage_b,
         (NC,),
-        [by_row(WIDTH), by_row(BCW), by_row(LANES), by_row(LANES), by_row(LANES), whole(1, WIDTH)],
+        [by_row(WIDTH), by_row(GROUPS * LANES), by_row(GROUPS * LANES), by_row(LANES), by_row(LANES), by_row(LANES), whole(1, WIDTH)],
         [(shape((TOK, WIDTH), F32), by_row(WIDTH))],
         flops=10**9,
         nbytes=20 * 2**20,
-    )(xc, bcc, cum, step, fl, jnp.repeat(skip_d, HEAD_DIM).reshape(1, WIDTH))
+    )(xc, bcc, cc, cum, step, fl, jnp.repeat(skip_d, HEAD_DIM).reshape(1, WIDTH))
 
     s1, crossed = lax.optimization_barrier((s1, crossed))
     part = pl.BlockSpec((16, 64, LANES), lambda s: (s, 0, 0))
@@ -614,7 +633,7 @@
         [
             pl.BlockSpec((STRETCH, GWIDTH), by_cg),
             pl.BlockSpec((STRETCH, GWIDTH), by_cg),
-            pl.BlockSpec((STRETCH, LANES), lambda g, c: (c, GROUPS + g)),
+            pl.BlockSpec((STRETCH, LANES), lambda g, c: (c, g)),
             pl.BlockSpec((1, STATE, GWIDTH), lambda g, c: (c, 0, g)),
             pl.BlockSpec((STATE, GWIDTH), by_g),
             pl.BlockSpec((STATE, GWIDTH), by_g),
@@ -628,7 +647,7 @@
         [(shape((TOK, WIDTH), BF), pl.BlockSpec((STRETCH, GWIDTH), by_cg))],
         flops=10**9,
         nbytes=15 * 2**20,
-    )(y, z, bcc, ent, s1, s2, far, far_gain, entry, cum, fl, norm_gain.reshape(1, WIDTH))
+    )(y, z, cc, ent, s1, s2, far, far_gain, entry, cum, fl, norm_gain.reshape(1, WIDTH))
 
     own, mixed = lax.optimization_barrier((own, mixed))
     swapped = lax.ppermute(own, "side", [(0, 1), (1, 0)])

time: 110 us -> 110 us (level)
    ppermute x2, waiting for transfers between devices: 3.94 us -> 2.75 us  [shift_in(): lax.ppermute(block, 'ctx', [(i, i + distance) for i in range(count - dist...]
where the time goes in v6:
time: 110 us; the launch traced here: 109 us
  starting transfers between devices  40 us (36%)
  Pallas kernels  39.1 us (36%)
  waiting for transfers between devices  23.3 us (21%)
  local copies, waits for them, and re-layouts  5.72 us (5%)
    all_to_all x1, starting transfers between devices, on_device(): got = lax.all_to_all(pieces, 'ctx', split_axis=0, concat_axis=0, tiled=True)  14.5 us
    pallas_call x1, Pallas kernels, on_device(): call(stage_c, (GROUPS, NC), [pl.BlockSpec((STRETCH, GWIDTH), by_cg), pl.B...  10.1 us
    ppermute x3, waiting for transfers between devices, shift_pairs(): return lax.ppermute(block, 'ctx', pairs)  8.86 us
    all_to_all x1, starting transfers between devices, on_device(): own = lax.all_to_all(back, 'ctx', split_axis=0, concat_axis=0, tiled=True)  8.3 us
    pallas_call x1, Pallas kernels, on_device(): call(stage_a, (STEPS,), [cols(TOK), cols(HALO), whole(TOK, BCW), halo_col...  7.96 us
    ppermute x2, starting transfers between devices, shift_in(): lax.ppermute(block, 'ctx', [(i, i + distance) for i in range(count - dist...  7.27 us
    pallas_call x1, Pallas kernels, on_device(): call(stage_e, (STEPS,), [smem, smem, cols(TOK), cols(HALO), whole(TOK, BC...  7.09 us
    pallas_call x1, Pallas kernels, on_device(): call(stage_b, (NC,), [by_row(WIDTH), by_row(GROUPS * LANES), by_row(GROUP...  6.58 us
  transfers between devices with their start and end apart: 9, of which 6 were waited for; matrix products, arithmetic and copies ran while one was open for 2% of the time, Pallas kernels for 24%

profile of v6, /device:TPU:1, one launch (start us, length us, event | category | flops | bytes accessed | tf_op | source)
XLA Modules:
  0.0 109.0 jit_solution(14428061455934663047)
XLA Ops:
  0.6 0.8 slice_bitcast_fusion
  1.5 0.7 slice.11
  2.2 4.0 %collective-permute-start = (bf16[16,2560]{1,0:T(8,128)(2,1)S(1)}, bf16[16,2560]{1,0:T(8,128)(2,1)S(1)}, u32[]{:S(2)}, u32[]{:S(2)}) collective-permute-start(bf16[16,2560]{1,0:T(8,128)(2,1)S(1)} %pad_maximum_fusion), channel_id=1, source_target_pairs={{0,8},{8,16},{16,24},{24,32},{32,40},{40,48},{48,56},{56,64},{64,7... | collective-permute-start | bytes 245768 | tf_op jit(solution)/shard_map/ppermute | solution.py:39
  6.3 1.9 %copy.20 = bf16[64,8,2,256]{3,1,2,0:T(8,128)(2,1)} copy(bf16[64,8,2,256]{3,2,1,0:T(2,128)(2,1)} %bitcast.28) | data formatting | bytes 1048576
  8.2 2.2 %shard_map.165 = (f32[512,128]{1,0:T(8,128)}, f32[512,128]{1,0:T(8,128)}, s32[512,128]{1,0:T(8,128)}, bf16[528,128]{1,0:T(8,128)(2,1)}, f32[16,128]{1,0:T(8,128)}) custom-call(s32[1]{0:T(128)} %bitcast.idx_ref, s32[1,32]{1,0:T(1,128)} %len_ref.5, f32[32,512]{1,0:T(8,128)} %bitcast.33, f32[1,32]{1,0:T(1,128)} %bitcast.37, f32[1,32]{1,0:T(1,128)} %bitcast.38), custom_call_target="tpu_custom_call" | custom-call | flops 100000000 | bytes 1048576 | tf_op jit(solution)/shard_map/pallas_call | solution.py:485
  10.4 0.0 collective-permute-done.xh_ref.bch_ref
  10.4 0.0 copy-start.7
  10.4 0.6 copy-done.7
  11.1 8.0 %shard_map.166 = (bf16[512,2048]{1,0:T(8,128)(2,1)}, bf16[512,256]{1,0:T(8,128)(2,1)}, bf16[4,128,2048]{2,1,0:T(8,128)(2,1)}, bf16[128,2048]{1,0:T(8,128)(2,1)}, f32[16,2048]{1,0:T(8,128)}) custom-call(bf16[512,2048]{1,0:T(8,128)(2,1)} %bitcast.22, bf16[16,2560]{1,0:T(8,128)(2,1)} %copy-done.7, bf16[512,512]{1,0:T(8,128)(2,1)} %bitcast.26, ...), custom_call_target="tpu_custom_call" | custom-call | flops 1000000000 | bytes 10485760 | tf_op jit(solution)/shard_map/pallas_call | solution.py:500
  19.0 3.2 %collective-permute-start.1 = (bf16[128,2048]{1,0:T(8,128)(2,1)}, bf16[128,2048]{1,0:T(8,128)(2,1)S(1)}, u32[]{:S(2)}, u32[]{:S(2)}) collective-permute-start(bf16[128,2048]{1,0:T(8,128)(2,1)} %get-tuple-element.37.s_ref), channel_id=1, source_target_pairs={{0,8},{8,16},{16,24},{24,32},{32,40},{40,48},{48,56},{56,64},{64,7... | collective-permute-start | bytes 1572872 | tf_op jit(solution)/shard_map/ppermute | solution.py:39
  22.3 0.7 collective-permute-start.2
  23.0 7.1 %shard_map.167 = (bf16[32,136,128]{2,1,0:T(8,128)(2,1)}, f32[8,2048]{1,0:T(8,128)}, bf16[512,256]{1,0:T(8,128)(2,1)}) custom-call(s32[1]{0:T(128)} %bitcast.idx_ref, s32[1,32]{1,0:T(1,128)} %len_ref.5, bf16[512,2048]{1,0:T(8,128)(2,1)} %bitcast.23, bf16[16,2560]{1,0:T(8,128)(2,1)} %copy-done.7, bf16[512,512]{1,0:T(8,128)(2,1)} %bitcast.27, ...), custom_call_target="tpu_custom_call" | custom-call | flops 500000000 | bytes 8388608 | tf_op jit(solution)/shard_map/pallas_call | solution.py:540
  30.1 2.7 %collective-permute-done.1.s1_ref = bf16[128,2048]{1,0:T(8,128)(2,1)S(1)} collective-permute-done((bf16[128,2048]{1,0:T(8,128)(2,1)}, bf16[128,2048]{1,0:T(8,128)(2,1)S(1)}, u32[]{:S(2)}, u32[]{:S(2)}) %collective-permute-start.1) | collective-permute-done | bytes 524320 | tf_op jit(solution)/shard_map/ppermute | solution.py:39
  32.8 0.0 copy-start
  32.8 0.0 collective-permute-done.2
  32.8 0.8 copy-done
  33.6 2.0 %shard_map.168 = bf16[32,136,128]{2,1,0:T(8,128)(2,1)} custom-call(bf16[32,136,128]{2,1,0:T(8,128)(2,1)} %get-tuple-element.38.piece_ref, bf16[128,2048]{1,0:T(8,128)(2,1)} %copy-done, f32[8,2048]{1,0:T(8,128)} %get-tuple-element.40.gain_ref), custom_call_target="tpu_custom_call", output_to_operand_aliasing={{}: (0, {})} | custom-call | flops 10000000 | bytes 2097152 | tf_op jit(solution)/shard_map/pallas_call | solution.py:590
  35.7 0.0 copy-start.1
  35.7 0.0 copy-start.10
  35.7 14.5 %all-to-all-start = ((bf16[32,136,128]{2,1,0:T(8,128)(2,1)}), bf16[32,136,128]{2,1,0:T(8,128)(2,1)S(1)}, u32[]{:S(2)}, u32[]{:S(2)}) async-start(bf16[32,136,128]{2,1,0:T(8,128)(2,1)} %shard_map.168), calls=%async_computation | async-start | bytes 2228224 | tf_op jit(solution)/shard_map/all_to_all | solution.py:599
  50.2 0.0 copy-done.2
  50.2 0.0 copy-done.1
  50.2 0.2 shard_map.169
  50.4 3.2 %collective-permute-start.3 = (bf16[128,2048]{1,0:T(8,128)(2,1)S(1)}, bf16[128,2048]{1,0:T(8,128)(2,1)S(1)}, u32[]{:S(2)}, u32[]{:S(2)}) collective-permute-start(bf16[128,2048]{1,0:T(8,128)(2,1)S(1)} %shard_map.169), channel_id=1, source_target_pairs={{0,8},{8,16},{16,24},{32,40},{40,48},{48,56},{64,72},{72,80},{80,8... | collective-permute-start | bytes 1572872 | tf_op jit(solution)/shard_map/ppermute | solution.py:45
  53.6 1.3 %collective-permute-start.4 = (bf16[128,2048]{1,0:T(8,128)(2,1)S(1)}, bf16[128,2048]{1,0:T(8,128)(2,1)S(1)}, u32[]{:S(2)}, u32[]{:S(2)}) collective-permute-start(bf16[128,2048]{1,0:T(8,128)(2,1)S(1)} %collective-permute-done.2), channel_id=1, source_target_pairs={{8,0},{40,32},{72,64},{104,96},{136,128},{168,160},{200,192},{232,... | collective-permute-start | bytes 1572872 | tf_op jit(solution)/shard_map/ppermute | solution.py:612
  54.9 0.0 copy-done.10
  54.9 0.7 collective-permute-start.5
  55.6 0.0 copy-done.9
  55.6 0.1 broadcast_in_dim.15
  55.7 0.7 reshape_reshape.3.skip_ref
  56.4 6.6 %shard_map.170.y_ref = f32[512,2048]{1,0:T(8,128)} custom-call(bf16[512,2048]{1,0:T(8,128)(2,1)} %get-tuple-element.32.xc_ref, bf16[512,256]{1,0:T(8,128)(2,1)} %get-tuple-element.33.bcc_ref, bf16[512,256]{1,0:T(8,128)(2,1)} %get-tuple-element.44.cc_ref.c_ref, f32[512,128]{1,0:T(8,128)} %get-tuple-element.34.cum_ref, f32[512,128]{1,0:T(8,128)} %get-tuple-element.35.step_ref, ...), custom_call_target="tpu_custom_call" | custom-call | flops 1000000000 | bytes 20971520 | tf_op jit(solution)/shard_map/pallas_call | solution.py:578
  62.9 0.0 collective-permute-done.5.far_gain_ref
  62.9 0.0 copy-start.8
  63.0 8.9 %collective-permute-done.3.s2_ref = bf16[128,2048]{1,0:T(8,128)(2,1)S(1)} collective-permute-done((bf16[128,2048]{1,0:T(8,128)(2,1)S(1)}, bf16[128,2048]{1,0:T(8,128)(2,1)S(1)}, u32[]{:S(2)}, u32[]{:S(2)}) %collective-permute-start.3) | collective-permute-done | bytes 524320 | tf_op jit(solution)/shard_map/ppermute | solution.py:45
  71.8 2.9 %collective-permute-done.4.far_ref = bf16[128,2048]{1,0:T(8,128)(2,1)S(1)} collective-permute-done((bf16[128,2048]{1,0:T(8,128)(2,1)S(1)}, bf16[128,2048]{1,0:T(8,128)(2,1)S(1)}, u32[]{:S(2)}, u32[]{:S(2)}) %collective-permute-start.4) | collective-permute-done | bytes 524320 | tf_op jit(solution)/shard_map/ppermute | solution.py:612
  74.7 1.2 %all-to-all-done.got_ref = bf16[32,136,128]{2,1,0:T(8,128)(2,1)S(1)} async-done(((bf16[32,136,128]{2,1,0:T(8,128)(2,1)}), bf16[32,136,128]{2,1,0:T(8,128)(2,1)S(1)}, u32[]{:S(2)}, u32[]{:S(2)}) %all-to-all-start) | async-done | bytes 1114144 | tf_op jit(solution)/shard_map/all_to_all | solution.py:599
  75.9 0.0 copy-done.3
  75.9 0.0 copy-done.4
  75.9 1.7 %shard_map.171 = bf16[32,72,128]{2,1,0:T(8,128)(2,1)} custom-call(s32[1,32]{1,0:T(1,128)S(1)} %copy-done.3, s32[1,32]{1,0:T(1,128)S(1)} %copy-done.4, bf16[32,136,128]{2,1,0:T(8,128)(2,1)S(1)} %all-to-all-done.got_ref), custom_call_target="tpu_custom_call" | custom-call | flops 10000000 | bytes 3145728 | tf_op jit(solution)/shard_map/pallas_call | solution.py:615
  77.6 8.3 %all-to-all-start.1 = ((bf16[32,72,128]{2,1,0:T(8,128)(2,1)}), bf16[32,72,128]{2,1,0:T(8,128)(2,1)S(1)}, u32[]{:S(2)}, u32[]{:S(2)}) async-start(bf16[32,72,128]{2,1,0:T(8,128)(2,1)} %shard_map.171), calls=%async_computation.1 | async-start | bytes 1179648 | tf_op jit(solution)/shard_map/all_to_all | solution.py:624
  85.9 0.0 copy-done.8
  85.9 0.0 copy-done.5
  85.9 0.0 copy-done.6
  86.0 10.1 %shard_map.172 = bf16[512,2048]{1,0:T(8,128)(2,1)} custom-call(f32[512,2048]{1,0:T(8,128)} %shard_map.170.y_ref, bf16[512,2048]{1,0:T(8,128)(2,1)} %bitcast.24, bf16[512,256]{1,0:T(8,128)(2,1)} %get-tuple-element.44.cc_ref.c_ref, bf16[4,128,2048]{2,1,0:T(8,128)(2,1)} %get-tuple-element.36.ent_ref, bf16[128,2048]{1,0:T(8,128)(2,1)} %copy-done, ...), custom_call_target="tpu_custom_call" | custom-call | flops 1000000000 | bytes 15728640 | tf_op jit(solution)/shard_map/pallas_call | solution.py:630
  96.1 6.0 %all-to-all-done.1 = bf16[32,72,128]{2,1,0:T(8,128)(2,1)S(1)} async-done(((bf16[32,72,128]{2,1,0:T(8,128)(2,1)}), bf16[32,72,128]{2,1,0:T(8,128)(2,1)S(1)}, u32[]{:S(2)}, u32[]{:S(2)}) %all-to-all-start.1) | async-done | bytes 589856 | tf_op jit(solution)/shard_map/all_to_all | solution.py:624
  102.0 4.1 %collective-permute-start.6 = (bf16[32,72,128]{2,1,0:T(8,128)(2,1)S(1)}, bf16[32,72,128]{2,1,0:T(8,128)(2,1)S(1)}, u32[]{:S(2)}, u32[]{:S(2)}) collective-permute-start(bf16[32,72,128]{2,1,0:T(8,128)(2,1)S(1)} %all-to-all-done.1), channel_id=1, source_target_pairs={{0,1},{1,0},{2,3},{3,2},{4,5},{5,4},{6,7},{7,6},{8,9},{9,8},{10,11... | collective-permute-start | bytes 1769480 | tf_op jit(solution)/shard_map/ppermute | solution.py:653
  106.2 1.6 %collective-permute-done.6.got_ref = bf16[32,72,128]{2,1,0:T(8,128)(2,1)S(1)} collective-permute-done((bf16[32,72,128]{2,1,0:T(8,128)(2,1)S(1)}, bf16[32,72,128]{2,1,0:T(8,128)(2,1)S(1)}, u32[]{:S(2)}, u32[]{:S(2)}) %collective-permute-start.6) | collective-permute-done | bytes 589856 | tf_op jit(solution)/shard_map/ppermute | solution.py:653
  107.8 1.2 %shard_map.173 = (f32[32,64,128]{2,1,0:T(8,128)}, bf16[3,2048]{1,0:T(4,128)(2,1)}, bf16[3,2,256]{2,1,0:T(2,128)(2,1)}) custom-call(bf16[32,72,128]{2,1,0:T(8,128)(2,1)S(1)} %collective-permute-done.6.got_ref), custom_call_target="tpu_custom_call" | custom-call | flops 10000000 | bytes 3145728 | tf_op jit(solution)/shard_map/pallas_call | solution.py:654
  (8 shorter events, 0.0 us)
Async XLA Ops:
  2.2 8.2 %collective-permute-start = (bf16[16,2560]{1,0:T(8,128)(2,1)S(1)}, bf16[16,2560]{1,0:T(8,128)(2,1)S(1)}, u32[]{:S(2)}, u32[]{:S(2)}) collective-permute-start(bf16[16,2560]{1,0:T(8,128)(2,1)S(1)} %pad_maximum_fusion), channel_id=1, source_target_pairs={{0,8},{8,16},{16,24},{24,32},{32,40},{40,48},{48,56},{56,64},{64,7... | collective-permute-start | bytes 245768 | tf_op jit(solution)/shard_map/ppermute | solution.py:39
  10.4 0.6 copy-start.7
  19.0 13.8 %collective-permute-start.1 = (bf16[128,2048]{1,0:T(8,128)(2,1)}, bf16[128,2048]{1,0:T(8,128)(2,1)S(1)}, u32[]{:S(2)}, u32[]{:S(2)}) collective-permute-start(bf16[128,2048]{1,0:T(8,128)(2,1)} %get-tuple-element.37.s_ref), channel_id=1, source_target_pairs={{0,8},{8,16},{16,24},{24,32},{32,40},{40,48},{48,56},{56,64},{64,7... | collective-permute-start | bytes 1572872 | tf_op jit(solution)/shard_map/ppermute | solution.py:39
  22.3 10.5 %collective-permute-start.2 = (bf16[128,2048]{1,0:T(8,128)(2,1)}, bf16[128,2048]{1,0:T(8,128)(2,1)S(1)}, u32[]{:S(2)}, u32[]{:S(2)}) collective-permute-start(bf16[128,2048]{1,0:T(8,128)(2,1)} %get-tuple-element.37.s_ref), channel_id=1, source_target_pairs={{16,40},{48,72},{80,104},{112,136},{144,168},{176,200},{208,232},{... | collective-permute-start | bytes 1572872 | tf_op jit(solution)/shard_map/ppermute | solution.py:45
  32.8 0.8 copy-start
  33.6 16.6 %copy-start.2 = (f32[16,2048]{1,0:T(8,128)S(1)}, f32[16,2048]{1,0:T(8,128)}, u32[]{:S(2)}) copy-start(f32[16,2048]{1,0:T(8,128)} %get-tuple-element.41.entry_ref) | copy-start | bytes 393220
  35.7 14.5 %copy-start.1 = (bf16[128,2048]{1,0:T(8,128)(2,1)S(1)}, bf16[128,2048]{1,0:T(8,128)(2,1)}, u32[]{:S(2)}) copy-start(bf16[128,2048]{1,0:T(8,128)(2,1)} %copy-done) | copy-start | bytes 1572868
  35.7 19.3 %copy-start.10 = (f32[16,128]{1,0:T(8,128)S(1)}, f32[16,128]{1,0:T(8,128)}, u32[]{:S(2)}) copy-start(f32[16,128]{1,0:T(8,128)} %get-tuple-element.43) | copy-start | bytes 24580
  35.7 19.9 %copy-start.9 = (f32[32]{0:T(128)S(1)}, f32[32]{0:T(128)}, u32[]{:S(2)}) copy-start(f32[32]{0:T(128)} %param.24) | copy-start | bytes 388
  35.7 40.2 %all-to-all-start = ((bf16[32,136,128]{2,1,0:T(8,128)(2,1)}), bf16[32,136,128]{2,1,0:T(8,128)(2,1)S(1)}, u32[]{:S(2)}, u32[]{:S(2)}) async-start(bf16[32,136,128]{2,1,0:T(8,128)(2,1)} %shard_map.168), calls=%async_computation | async-start | bytes 2228224 | tf_op jit(solution)/shard_map/all_to_all | solution.py:599
  50.4 21.4 %collective-permute-start.3 = (bf16[128,2048]{1,0:T(8,128)(2,1)S(1)}, bf16[128,2048]{1,0:T(8,128)(2,1)S(1)}, u32[]{:S(2)}, u32[]{:S(2)}) collective-permute-start(bf16[128,2048]{1,0:T(8,128)(2,1)S(1)} %shard_map.169), channel_id=1, source_target_pairs={{0,8},{8,16},{16,24},{32,40},{40,48},{48,56},{64,72},{72,80},{80,8... | collective-permute-start | bytes 1572872 | tf_op jit(solution)/shard_map/ppermute | solution.py:45
  53.6 21.1 %collective-permute-start.4 = (bf16[128,2048]{1,0:T(8,128)(2,1)S(1)}, bf16[128,2048]{1,0:T(8,128)(2,1)S(1)}, u32[]{:S(2)}, u32[]{:S(2)}) collective-permute-start(bf16[128,2048]{1,0:T(8,128)(2,1)S(1)} %collective-permute-done.2), channel_id=1, source_target_pairs={{8,0},{40,32},{72,64},{104,96},{136,128},{168,160},{200,192},{232,... | collective-permute-start | bytes 1572872 | tf_op jit(solution)/shard_map/ppermute | solution.py:612
  54.9 8.0 %collective-permute-start.5 = (f32[16,128]{1,0:T(8,128)S(1)}, f32[16,128]{1,0:T(8,128)S(1)}, u32[]{:S(2)}, u32[]{:S(2)}) collective-permute-start(f32[16,128]{1,0:T(8,128)S(1)} %copy-done.10), channel_id=1, source_target_pairs={{24,32},{56,64},{88,96},{120,128},{152,160},{184,192},{216,224},{2... | collective-permute-start | bytes 24584 | tf_op jit(solution)/shard_map/ppermute | solution.py:45
  56.4 19.5 %copy-start.3 = (s32[1,32]{1,0:T(1,128)S(1)}, s32[1,32]{1,0:T(1,128)}, u32[]{:S(2)}) copy-start(s32[1,32]{1,0:T(1,128)} %len_ref.5) | copy-start | bytes 388
  56.4 19.5 %copy-start.4 = (s32[1,32]{1,0:T(1,128)S(1)}, s32[1,32]{1,0:T(1,128)}, u32[]{:S(2)}) copy-start(s32[1,32]{1,0:T(1,128)} %owner_ref.1) | copy-start | bytes 388
  62.9 23.0 %copy-start.8 = (f32[16,128]{1,0:T(8,128)}, f32[16,128]{1,0:T(8,128)S(1)}, u32[]{:S(2)}) copy-start(f32[16,128]{1,0:T(8,128)S(1)} %collective-permute-done.5.far_gain_ref) | copy-start | bytes 24580
  71.8 14.1 %copy-start.5 = (bf16[128,2048]{1,0:T(8,128)(2,1)}, bf16[128,2048]{1,0:T(8,128)(2,1)S(1)}, u32[]{:S(2)}) copy-start(bf16[128,2048]{1,0:T(8,128)(2,1)S(1)} %collective-permute-done.3.s2_ref) | copy-start | bytes 1572868
  74.7 11.3 %copy-start.6 = (bf16[128,2048]{1,0:T(8,128)(2,1)}, bf16[128,2048]{1,0:T(8,128)(2,1)S(1)}, u32[]{:S(2)}) copy-start(bf16[128,2048]{1,0:T(8,128)(2,1)S(1)} %collective-permute-done.4.far_ref) | copy-start | bytes 1572868
  77.6 24.4 %all-to-all-start.1 = ((bf16[32,72,128]{2,1,0:T(8,128)(2,1)}), bf16[32,72,128]{2,1,0:T(8,128)(2,1)S(1)}, u32[]{:S(2)}, u32[]{:S(2)}) async-start(bf16[32,72,128]{2,1,0:T(8,128)(2,1)} %shard_map.171), calls=%async_computation.1 | async-start | bytes 1179648 | tf_op jit(solution)/shard_map/all_to_all | solution.py:624
  102.0 5.8 %collective-permute-start.6 = (bf16[32,72,128]{2,1,0:T(8,128)(2,1)S(1)}, bf16[32,72,128]{2,1,0:T(8,128)(2,1)S(1)}, u32[]{:S(2)}, u32[]{:S(2)}) collective-permute-start(bf16[32,72,128]{2,1,0:T(8,128)(2,1)S(1)} %all-to-all-done.1), channel_id=1, source_target_pairs={{0,1},{1,0},{2,3},{3,2},{4,5},{5,4},{6,7},{7,6},{8,9},{9,8},{10,11... | collective-permute-start | bytes 1769480 | tf_op jit(solution)/shard_map/ppermute | solution.py:653
